TPU v7x, 128 devices: a whole 4x4x4 slice. The times are simulated.
128 devices in a mesh: section: 2 (over core), tensor: 8 (over x_lo, y), dp: 8 (over z, x_hi).
Axes of the slice: x: 4 (x_hi: 2, x_lo: 2; x = x_hi * 2 + x_lo), y: 4, z: 4, core: 2. Of those that a mesh axis runs over, the one named last changes fastest.
Arguments:
- inputs: bfloat16 [2, 2048, 1536], P(None, 'dp'), may hold values from -6 to 6
- cotangent: bfloat16 [2, 2048, 1536], P(None, 'dp'), may hold values from -6 to 6
- doc_lengths: int32 [2, 32], replicated, may hold values from 0 to 1792, as said below
- norm_one: bfloat16 [2, 1536], P('section'), may hold values from 0.25 to 1.75
- query_w: bfloat16 [2, 1536, 1536], P('section', None, 'tensor'), may hold values from -0.15625 to 0.15625
- key_w: bfloat16 [2, 1536, 768], P('section', None, 'tensor'), may hold values from -0.15625 to 0.15625
- value_w: bfloat16 [2, 1536, 768], P('section', None, 'tensor'), may hold values from -0.15625 to 0.15625
- out_w: bfloat16 [2, 1536, 1536], P('section', 'tensor'), may hold values from -3.5 to 3.5
- norm_two: bfloat16 [2, 1536], P('section'), may hold values from 0.25 to 1.75
- gate_w: bfloat16 [2, 1536, 4096], P('section', None, 'tensor'), may hold values from -0.15625 to 0.15625
- up_w: bfloat16 [2, 1536, 4096], P('section', None, 'tensor'), may hold values from -0.15625 to 0.15625
- down_w: bfloat16 [2, 4096, 1536], P('section', 'tensor'), may hold values from -0.09375 to 0.09375
Outputs:
- layer_outputs: bfloat16 [2, 2, 2048, 1536], P('section', None, ('dp', 'tensor'))
- input_grads: float32 [2, 2, 2048, 1536], P('section', None, ('dp', 'tensor'))
- grad_norm_one: float32 [2, 1536], P('section')
- grad_query: float32 [2, 1536, 1536], P('section', None, 'tensor')
- grad_key: float32 [2, 1536, 768], P('section', None, 'tensor')
- grad_value: float32 [2, 1536, 768], P('section', None, 'tensor')
- grad_out: float32 [2, 1536, 1536], P('section', 'tensor')
- grad_norm_two: float32 [2, 1536], P('section')
- grad_gate: float32 [2, 1536, 4096], P('section', None, 'tensor')
- grad_up: float32 [2, 1536, 4096], P('section', None, 'tensor')
- grad_down: float32 [2, 4096, 1536], P('section', 'tensor')
Inputs may be any that keep to these rules, and one draw needn't show every extreme that they name: `doc_lengths`: each row lists the lengths of its documents in order, followed by zeros; they add up to 2048.
All inputs are finite; a program needn't handle non-finite values.
Results may differ from a plain program's by a relative error of at most 0.035.
Values may be sent and summed in bfloat16 or wider, within the bound.
A program may use at most 192 MiB of HBM per device.

v0:
```python
from functools import partial
import math

import jax
import jax.numpy as jnp
from jax import lax
from jax.sharding import PartitionSpec as P

HD = 96


eps_norm = 1e-05
rope_base = 100000.0
masked_score = -1e30


def in_blocks(x, dim, peers):
    lengths = x.shape
    blocks = x.reshape(*lengths[:dim], peers, lengths[dim] // peers, *lengths[dim + 1 :])
    return jnp.moveaxis(blocks, dim, 0)


def summed_on_arrival(x, axis, dim):
    peers = lax.axis_size(axis)
    blocks = lax.all_to_all(in_blocks(x, dim, peers), axis, 0, 0, tiled=True)
    return jnp.sum(blocks.astype(jnp.float32), axis=0)


def copy_for_each(x, axis):
    peers = lax.axis_size(axis)
    return lax.all_to_all(jnp.broadcast_to(x[None], (peers, *x.shape)), axis, 0, 0, tiled=True)


def in_order(blocks, dim):
    blocks = jnp.moveaxis(blocks, 0, dim)
    lengths = blocks.shape
    return blocks.reshape(*lengths[:dim], lengths[dim] * lengths[dim + 1], *lengths[dim + 2 :])


def gather_directly(x, axis, dim):
    blocks = copy_for_each(x, axis)
    return in_order(blocks, dim)


def one_gather(arrays, axis, dims):
    line = jnp.concatenate([a.reshape(-1) for a in arrays])
    lines, at, finished = (lax.all_gather(line, axis), 0, [])
    for a, dim in zip(arrays, dims):
        blocks = lines[:, at : at + a.size].reshape(-1, *a.shape)
        finished.append(in_order(blocks, dim))
        at += a.size
    return tuple(finished)


def from_behind(block, axis, distance):
    devices = range(lax.axis_size(axis))
    route = [(i - distance, i) for i in devices if i - distance in devices]
    return lax.ppermute(block, axis, route)


def of_everyone(x, axis):
    return copy_for_each(x, axis).sum(axis=0)


def together(arrays, axis):
    line, at, finished = (jnp.concatenate([a.reshape(-1) for a in arrays]), 0, [])
    subtotal = of_everyone(line, axis)
    for a in arrays:
        finished.append(subtotal[at : at + a.size].reshape(a.shape))
        at += a.size
    return tuple(finished)


def rotate(values, angles):
    half_size = values.shape[-1] // 2
    first_half = values[..., :half_size]
    second_half = values[..., half_size:]
    cosine = jnp.cos(angles)
    sine_values = jnp.sin(angles)
    return jnp.concatenate(
        [
            first_half * cosine - second_half * sine_values,
            second_half * cosine + first_half * sine_values,
        ],
        axis=-1,
    )


def unrotate(grad_rows, angles):
    half_size = grad_rows.shape[-1] // 2
    first_half = grad_rows[..., :half_size]
    second_half = grad_rows[..., half_size:]
    cosine = jnp.cos(angles)
    sine_values = jnp.sin(angles)
    return jnp.concatenate(
        [
            first_half * cosine + second_half * sine_values,
            second_half * cosine - first_half * sine_values,
        ],
        axis=-1,
    )


def doc_layout(lengths, row_start, row_count):
    doc_ends = jnp.cumsum(lengths)
    starts = doc_ends - lengths
    places = row_start + jnp.arange(row_count, dtype=jnp.int32)
    begins = jnp.max(jnp.where(starts[None, :] <= places[:, None], starts[None, :], 0), axis=1)
    inverse_freq = jnp.exp(
        jnp.arange(HD // 2, dtype=jnp.float32) * (-2.0 * math.log(rope_base) / HD)
    )
    angles = (places - begins).astype(jnp.float32)[:, None] * inverse_freq[None, :]
    return (places, begins, angles)


def forward_dot(left_side, right_side):
    return jnp.dot(left_side, right_side, preferred_element_type=jnp.float32)


def outer_sum(left_side, right_side):
    return lax.dot_general(
        left_side, right_side, (((0,), (0,)), ((), ())), preferred_element_type=jnp.float32
    )


def back_dot(grad_rows, weight):
    return lax.dot_general(
        grad_rows, weight, (((1,), (1,)), ((), ())), preferred_element_type=jnp.float32
    )


def norm_factor(values):
    return lax.rsqrt(jnp.mean(values * values, axis=-1, keepdims=True) + eps_norm)


def norm_back(grad_normed, values, factor, gain_row):
    scaled = grad_normed * gain_row
    grad_values = factor * scaled - values * factor * factor * factor * jnp.mean(
        values * scaled, axis=-1, keepdims=True
    )
    grad_gain = jnp.sum(grad_normed * values * factor, axis=0)
    return (grad_values, grad_gain)


def row_share(partial_rows):
    return summed_on_arrival(partial_rows.astype(jnp.bfloat16), "tensor", 0)


def all_rows(share_rows):
    return gather_directly(share_rows, "tensor", 0)


def own_rows(rows):
    count = rows.shape[0] // lax.axis_size("tensor")
    return lax.dynamic_slice_in_dim(rows, lax.axis_index("tensor") * count, count, 0)


def masked_scores(queries, all_keys, places, begins):
    score_scale = 1.0 / math.sqrt(HD)
    scores = (
        jnp.einsum("qkgd,skd->kgqs", queries, all_keys, preferred_element_type=jnp.float32)
        * score_scale
    )
    key_places = jnp.arange(all_keys.shape[0], dtype=jnp.int32)
    allowed = (key_places[None, :] <= places[:, None]) & (key_places[None, :] >= begins[:, None])
    return jnp.where(allowed[None, None], scores, masked_score)


def layer_forward(weights, layer_in, places, begins, angles):
    gain_one, query_w, key_w, value_w, out_w, gain_two, gate_w, up_w, down_w = weights
    span_rows = layer_in.shape[0]
    kv_local = key_w.shape[1] // HD
    group_size = query_w.shape[1] // key_w.shape[1]
    factor_one = norm_factor(layer_in)
    normed = (layer_in * factor_one * gain_one.astype(jnp.float32)).astype(jnp.bfloat16)
    query_raw = forward_dot(normed, query_w).reshape(span_rows, kv_local * group_size, HD)
    key_raw = forward_dot(normed, key_w).reshape(span_rows, kv_local, HD)
    values = forward_dot(normed, value_w).reshape(span_rows, kv_local, HD).astype(jnp.bfloat16)
    queries = (
        rotate(query_raw, angles[:, None, :])
        .astype(jnp.bfloat16)
        .reshape(span_rows, kv_local, group_size, HD)
    )
    key_rot = rotate(key_raw, angles[:, None, :]).astype(jnp.bfloat16)
    all_keys, all_values = one_gather((key_rot, values), "dp", (0, 0))
    scores = masked_scores(queries, all_keys, places, begins)
    row_peak = jnp.max(scores, axis=-1, keepdims=True)
    exp_total = jnp.sum(jnp.exp(scores - row_peak), axis=-1, keepdims=True)
    log_total = row_peak + jnp.log(exp_total)
    soft_weights = jnp.exp(scores - log_total).astype(jnp.bfloat16)
    mixed_heads = jnp.einsum(
        "kgqs,skd->qkgd", soft_weights, all_values, preferred_element_type=jnp.float32
    )
    mixed_heads = mixed_heads.reshape(span_rows, kv_local * group_size * HD).astype(jnp.bfloat16)
    attn_partial = forward_dot(mixed_heads, out_w)
    hidden_state = own_rows(layer_in) + row_share(attn_partial)
    factor_two = norm_factor(hidden_state)
    normed_two = (hidden_state * factor_two * gain_two.astype(jnp.float32)).astype(jnp.bfloat16)
    normed_two = all_rows(normed_two)
    gate_act = forward_dot(normed_two, gate_w)
    upward = forward_dot(normed_two, up_w)
    inner_act = (jax.nn.silu(gate_act) * upward).astype(jnp.bfloat16)
    down_partial = forward_dot(inner_act, down_w)
    result = hidden_state + row_share(down_partial)
    kept_values = (
        layer_in,
        factor_one,
        normed,
        queries,
        all_keys,
        all_values,
        log_total,
        mixed_heads,
        hidden_state,
        factor_two,
        normed_two,
        gate_act,
        upward,
        inner_act,
    )
    return (result, kept_values)


def layer_backward(weights, kept_values, grad_result, places, begins, angles):
    gain_one, query_w, key_w, value_w, out_w, gain_two, gate_w, up_w, down_w = weights
    (
        layer_in,
        factor_one,
        normed,
        queries,
        all_keys,
        all_values,
        log_total,
        mixed_heads,
        hidden_state,
        factor_two,
        normed_two,
        gate_act,
        upward,
        inner_act,
    ) = kept_values
    span_rows = layer_in.shape[0]
    kv_local = key_w.shape[1] // HD
    group_size = query_w.shape[1] // key_w.shape[1]
    score_scale = 1.0 / math.sqrt(HD)
    grad_branch = grad_result.astype(jnp.bfloat16)
    grad_down = outer_sum(inner_act, grad_branch)
    grad_inner = back_dot(grad_branch, down_w)
    sigmoid_gate = jax.nn.sigmoid(gate_act)
    grad_gate_act = (
        grad_inner * upward * sigmoid_gate * (1.0 + gate_act * (1.0 - sigmoid_gate))
    ).astype(jnp.bfloat16)
    grad_upward = (grad_inner * gate_act * sigmoid_gate).astype(jnp.bfloat16)
    grad_gate = outer_sum(normed_two, grad_gate_act)
    grad_up = outer_sum(normed_two, grad_upward)
    normed_two_part = back_dot(grad_gate_act, gate_w) + back_dot(grad_upward, up_w)
    grad_normed_two = row_share(normed_two_part)
    grad_base = own_rows(grad_result)
    grad_hidden_part, grad_gain_two = norm_back(
        grad_normed_two, hidden_state, factor_two, gain_two.astype(jnp.float32)
    )
    grad_hidden = grad_base + grad_hidden_part
    grad_attn = grad_hidden.astype(jnp.bfloat16)
    grad_attn = all_rows(grad_attn)
    grad_out = outer_sum(mixed_heads, grad_attn)
    grad_mixed = (
        back_dot(grad_attn, out_w).astype(jnp.bfloat16).reshape(span_rows, kv_local, group_size, HD)
    )
    scores = masked_scores(queries, all_keys, places, begins)
    soft_weights = jnp.exp(scores - log_total)
    grad_soft = jnp.einsum(
        "qkgd,skd->kgqs", grad_mixed, all_values, preferred_element_type=jnp.float32
    )
    row_dot = jnp.sum(grad_soft * soft_weights, axis=-1, keepdims=True)
    grad_scores = (soft_weights * (grad_soft - row_dot)).astype(jnp.bfloat16)
    grad_queries = (
        jnp.einsum("kgqs,skd->qkgd", grad_scores, all_keys, preferred_element_type=jnp.float32)
        * score_scale
    )
    grad_keys_part = (
        jnp.einsum("kgqs,qkgd->skd", grad_scores, queries, preferred_element_type=jnp.float32)
        * score_scale
    )
    grad_values_part = jnp.einsum(
        "kgqs,qkgd->skd",
        soft_weights.astype(jnp.bfloat16),
        grad_mixed,
        preferred_element_type=jnp.float32,
    )
    grad_key_rot, grad_value_rows = (
        lax.psum_scatter(
            grad_keys_part.astype(jnp.bfloat16), "dp", scatter_dimension=0, tiled=True
        ).astype(jnp.float32),
        lax.psum_scatter(
            grad_values_part.astype(jnp.bfloat16), "dp", scatter_dimension=0, tiled=True
        ).astype(jnp.float32),
    )
    grad_query_raw = (
        unrotate(grad_queries.reshape(span_rows, kv_local * group_size, HD), angles[:, None, :])
        .reshape(span_rows, -1)
        .astype(jnp.bfloat16)
    )
    grad_key_raw = (
        unrotate(grad_key_rot, angles[:, None, :]).reshape(span_rows, -1).astype(jnp.bfloat16)
    )
    grad_value_raw = grad_value_rows.reshape(span_rows, -1).astype(jnp.bfloat16)
    grad_query = outer_sum(normed, grad_query_raw)
    grad_key = outer_sum(normed, grad_key_raw)
    grad_value = outer_sum(normed, grad_value_raw)
    normed_part = (
        back_dot(grad_query_raw, query_w)
        + back_dot(grad_key_raw, key_w)
        + back_dot(grad_value_raw, value_w)
    )
    grad_normed = row_share(normed_part)
    input_rows = own_rows(layer_in)
    factor_rows = own_rows(factor_one)
    grad_in_part, grad_gain_one = norm_back(
        grad_normed, input_rows, factor_rows, gain_one.astype(jnp.float32)
    )
    grad_parts = (
        grad_gain_one,
        grad_query,
        grad_key,
        grad_value,
        grad_out,
        grad_gain_two,
        grad_gate,
        grad_up,
        grad_down,
    )
    return (grad_hidden + grad_in_part, grad_parts)


def on_device(
    inputs,
    cotangent,
    doc_lengths,
    norm_one,
    query_w,
    key_w,
    value_w,
    out_w,
    norm_two,
    gate_w,
    up_w,
    down_w,
):
    weights = (
        norm_one[0],
        query_w[0],
        key_w[0],
        value_w[0],
        out_w[0],
        norm_two[0],
        gate_w[0],
        up_w[0],
        down_w[0],
    )
    batches = inputs.shape[0]
    span_rows = inputs.shape[1]
    width = inputs.shape[2]
    share_count = span_rows // lax.axis_size("tensor")
    row_start = lax.axis_index("dp") * span_rows
    is_first = lax.axis_index("section") == 0
    choose_section = partial(jnp.where, is_first)
    forward_inputs, forward_outputs, forward_kept = ([], [], [])
    received = jnp.zeros((share_count, width), jnp.bfloat16)
    for moment in range(batches + 1):
        first_batch = min(moment, batches - 1)
        second_batch = max(moment - 1, 0)
        received_rows = all_rows(received)
        layer_in = jnp.where(is_first, inputs[first_batch], received_rows)
        lengths_now = jnp.where(is_first, doc_lengths[first_batch], doc_lengths[second_batch])
        places, begins, angles = doc_layout(lengths_now, row_start, span_rows)
        result, kept_values = layer_forward(
            weights, layer_in.astype(jnp.float32), places, begins, angles
        )
        result_low = result.astype(jnp.bfloat16)
        forward_inputs.append(layer_in)
        forward_outputs.append(result_low)
        forward_kept.append(kept_values)
        if moment < batches:
            received = from_behind(result_low, "section", 1)
    batch_kept = [
        jax.tree.map(choose_section, forward_kept[number], forward_kept[number + 1])
        for number in range(batches)
    ]
    totals = tuple((jnp.zeros(weight.shape, jnp.float32) for weight in weights))
    backward_grads = []
    received_grad = jnp.zeros((share_count, width), jnp.bfloat16)
    for moment in range(batches + 1):
        first_batch = max(moment - 1, 0)
        second_batch = min(moment, batches - 1)
        is_live = jnp.where(is_first, moment >= 1, moment < batches)
        grad_rows = all_rows(received_grad)
        grad_result = jnp.where(is_first, grad_rows, cotangent[second_batch]).astype(jnp.float32)
        lengths_now = jnp.where(is_first, doc_lengths[first_batch], doc_lengths[second_batch])
        places, begins, angles = doc_layout(lengths_now, row_start, span_rows)
        kept_values = jax.tree.map(
            choose_section, batch_kept[first_batch], batch_kept[second_batch]
        )
        grad_input, grad_parts = layer_backward(
            weights, kept_values, grad_result, places, begins, angles
        )
        totals = tuple(
            (
                total_item + jnp.where(is_live, grad_item, 0.0)
                for total_item, grad_item in zip(totals, grad_parts)
            )
        )
        backward_grads.append(grad_input)
        if moment < batches:
            received_grad = from_behind(grad_input.astype(jnp.bfloat16), "section", -1)
    summed = (
        lax.psum(totals[0].astype(jnp.bfloat16), "dp").astype(jnp.float32),
        lax.psum(totals[1].astype(jnp.bfloat16), "dp").astype(jnp.float32),
        lax.psum(totals[2].astype(jnp.bfloat16), "dp").astype(jnp.float32),
        lax.psum(totals[3].astype(jnp.bfloat16), "dp").astype(jnp.float32),
        lax.psum(totals[4].astype(jnp.bfloat16), "dp").astype(jnp.float32),
        lax.psum(totals[5].astype(jnp.bfloat16), "dp").astype(jnp.float32),
        lax.psum(totals[6].astype(jnp.bfloat16), "dp").astype(jnp.float32),
        lax.psum(totals[7].astype(jnp.bfloat16), "dp").astype(jnp.float32),
        lax.psum(totals[8].astype(jnp.bfloat16), "dp").astype(jnp.float32),
    )
    gain_first, gain_second = together((summed[0], summed[5]), "tensor")
    summed = (
        gain_first,
        summed[1],
        summed[2],
        summed[3],
        summed[4],
        gain_second,
        summed[6],
        summed[7],
        summed[8],
    )
    layer_outputs = jnp.stack(
        [
            choose_section(forward_outputs[number], forward_outputs[number + 1])
            for number in range(batches)
        ]
    )[None]
    input_grads = jnp.stack(
        [
            choose_section(backward_grads[number + 1], backward_grads[number])
            for number in range(batches)
        ]
    )[None]
    return (layer_outputs, input_grads) + tuple((grad_item[None] for grad_item in summed))


def solution(mesh):
    in_specs = (
        P(None, "dp", None),
        P(None, "dp", None),
        P(),
        P("section", None),
        P("section", None, "tensor"),
        P("section", None, "tensor"),
        P("section", None, "tensor"),
        P("section", "tensor", None),
        P("section", None),
        P("section", None, "tensor"),
        P("section", None, "tensor"),
        P("section", "tensor", None),
    )
    out_specs = (
        P("section", None, ("dp", "tensor"), None),
        P("section", None, ("dp", "tensor"), None),
        P("section", None),
        P("section", None, "tensor"),
        P("section", None, "tensor"),
        P("section", None, "tensor"),
        P("section", "tensor", None),
        P("section", None),
        P("section", None, "tensor"),
        P("section", None, "tensor"),
        P("section", "tensor", None),
    )
    return jax.shard_map(
        on_device, mesh=mesh, in_specs=in_specs, out_specs=out_specs, check_vma=False
    )
```

profile of v0, /device:TPU:24, one launch (start us, length us, event | category | flops | bytes accessed | tf_op | source)
XLA Modules:
  0.0 1377.0 jit_solution(11252441210969224925)
XLA Ops:
  10.5 3.1 fusion.82
  22.7 39.6 %all-gather = bf16[393216]{0:T(1024)(128)(2,1)} all-gather(bf16[49152]{0:T(1024)(128)(2,1)S(1)} %pad_maximum_fusion), channel_id=2, replica_groups=mesh['section'=2,'tensor'=8,'dp'=8] {'dp'}, dimensions={0}, use_global_device_ids=true | all-gather | bytes 884736 | tf_op jit(solution)/shard_map/all_gather | solution.py:47
  77.3 3.2 fusion.126
  81.8 6.3 all-to-all-start
  90.0 5.7 all-to-all-done
  98.9 12.7 all_to_all.118
  115.2 12.6 all_to_all.119
  130.5 16.3 %all_to_all.120 = bf16[8,32,1536]{2,1,0:T(8,128)(2,1)S(1)} all-to-all(bf16[8,32,1536]{2,1,0:T(8,128)(2,1)S(1)} %broadcast_in_dim.182), channel_id=1, replica_groups=mesh['section'=2,'tensor'=8,'dp'=8] {'tensor'}, dimensions={0} | all-to-all | bytes 1572864 | tf_op jit(solution)/shard_map/all_to_all | solution.py:31
  160.1 38.8 %all-gather.1 = bf16[393216]{0:T(1024)(128)(2,1)} all-gather(bf16[49152]{0:T(1024)(128)(2,1)S(1)} %pad_maximum_fusion.2), channel_id=3, replica_groups=mesh['section'=2,'tensor'=8,'dp'=8] {'dp'}, dimensions={0}, use_global_device_ids=true | all-gather | bytes 884736 | tf_op jit(solution)/shard_map/all_gather | solution.py:47
  213.5 3.2 fusion.123
  218.0 6.7 all-to-all-start.4
  227.2 5.2 all-to-all-done.4
  236.4 6.0 all-to-all-start.5
  245.1 5.1 all-to-all-done.5
  257.2 12.8 all_to_all.121
  274.5 6.5 all-to-all-start.7
  284.3 8.2 all-to-all-done.7
  292.5 6.1 all-to-all-start.11
  298.6 3.1 convert_select_fusion
  316.4 38.9 %all-gather.2 = bf16[393216]{0:T(1024)(128)(2,1)} all-gather(bf16[49152]{0:T(1024)(128)(2,1)S(1)} %pad_maximum_fusion.4), channel_id=4, replica_groups=mesh['section'=2,'tensor'=8,'dp'=8] {'dp'}, dimensions={0}, use_global_device_ids=true | all-gather | bytes 884736 | tf_op jit(solution)/shard_map/all_gather | solution.py:47
  357.6 3.3 broadcast_select_fusion.12
  371.2 3.9 broadcast_select_fusion.33
  376.4 5.9 all-to-all-start.8
  384.2 5.7 all-to-all-done.8
  396.5 6.0 all-to-all-start.12
  423.0 3.7 fusion.57
  430.8 60.5 %reduce-scatter.7.cloned.1.call-done = bf16[256,1,96]{0,2,1:T(8,128)(2,1)} async-done(((bf16[2048,1,96]{0,2,1:T(8,128)(2,1)}), bf16[256,1,96]{0,2,1:T(8,128)(2,1)}) %reduce-scatter.7.cloned.1.call-update) | async-done | bytes 49168 | tf_op jit(solution)/shard_map/reduce_scatter | solution.py:291
  496.6 68.7 %reduce-scatter.9.cloned.1.call-done = bf16[256,1,96]{0,2,1:T(8,128)(2,1)} async-done(((bf16[2048,1,96]{0,2,1:T(8,128)(2,1)}), bf16[256,1,96]{0,2,1:T(8,128)(2,1)}) %reduce-scatter.9.cloned.1.call-update) | async-done | bytes 49168 | tf_op jit(solution)/shard_map/reduce_scatter | solution.py:294
  568.0 5.1 all-to-all-start.13
  574.3 7.5 all-to-all-done.13
  583.7 5.9 all-to-all-start.9
  595.6 3.0 all-to-all-done.9
  600.5 6.1 all-to-all-start.14
  609.1 7.0 all-to-all-done.14
  624.4 6.0 all-to-all-start.15
  632.8 7.5 all-to-all-done.15
  646.6 5.8 all-to-all-start.16
  652.4 3.6 convolution_select_fusion.1
  679.0 3.7 fusion.56
  682.7 2.9 fusion.118
  689.9 56.7 %reduce-scatter.11.cloned.1.call-done = bf16[256,1,96]{0,2,1:T(8,128)(2,1)} async-done(((bf16[2048,1,96]{0,2,1:T(8,128)(2,1)}), bf16[256,1,96]{0,2,1:T(8,128)(2,1)}) %reduce-scatter.11.cloned.1.call-update) | async-done | bytes 49168 | tf_op jit(solution)/shard_map/reduce_scatter | solution.py:291
  751.9 68.4 %reduce-scatter.13.cloned.1.call-done = bf16[256,1,96]{0,2,1:T(8,128)(2,1)} async-done(((bf16[2048,1,96]{0,2,1:T(8,128)(2,1)}), bf16[256,1,96]{0,2,1:T(8,128)(2,1)}) %reduce-scatter.13.cloned.1.call-update) | async-done | bytes 49168 | tf_op jit(solution)/shard_map/reduce_scatter | solution.py:294
  823.2 5.1 all-to-all-start.17
  833.6 3.4 all-to-all-done.17
  847.1 6.2 all-to-all-start.18
  853.4 3.5 fusion.186
  859.1 6.2 all-to-all-done.18
  873.8 5.6 all-to-all-start.19
  879.5 4.7 convolution_add_fusion
  895.4 5.7 all-to-all-start.20
  901.1 4.1 fusion.23
  905.2 3.8 fusion.24
  923.6 3.7 fusion.55
  936.1 55.0 %reduce-scatter.15.cloned.1.call-done = bf16[256,1,96]{0,2,1:T(8,128)(2,1)} async-done(((bf16[2048,1,96]{0,2,1:T(8,128)(2,1)}), bf16[256,1,96]{0,2,1:T(8,128)(2,1)}) %reduce-scatter.15.cloned.1.call-update) | async-done | bytes 49168 | tf_op jit(solution)/shard_map/reduce_scatter | solution.py:291
  994.2 70.6 %reduce-scatter.17.cloned.1.call-done = bf16[256,1,96]{0,2,1:T(8,128)(2,1)} async-done(((bf16[2048,1,96]{0,2,1:T(8,128)(2,1)}), bf16[256,1,96]{0,2,1:T(8,128)(2,1)}) %reduce-scatter.17.cloned.1.call-update) | async-done | bytes 49168 | tf_op jit(solution)/shard_map/reduce_scatter | solution.py:294
  1070.1 5.2 all-to-all-start.10
  1075.4 16.8 %all-to-all-done.10 = bf16[8,32,1536]{2,1,0:T(8,128)(2,1)S(1)} async-done(((bf16[8,32,1536]{2,1,0:T(8,128)(2,1)}), bf16[8,32,1536]{2,1,0:T(8,128)(2,1)S(1)}, u32[]{:S(2)}, u32[]{:S(2)}) %all-to-all-start.10) | async-done | bytes 786464 | tf_op jit(solution)/shard_map/all_to_all | solution.py:25
  1095.7 4.9 all-to-all-start.21
  1101.5 15.7 %all-to-all-done.21 = bf16[8,32,1536]{2,1,0:T(8,128)(2,1)S(1)} async-done(((bf16[8,32,1536]{2,1,0:T(8,128)(2,1)}), bf16[8,32,1536]{2,1,0:T(8,128)(2,1)S(1)}, u32[]{:S(2)}, u32[]{:S(2)}) %all-to-all-start.21) | async-done | bytes 786464 | tf_op jit(solution)/shard_map/all_to_all | solution.py:25
  1118.6 24.0 %all-reduce = (bf16[1536]{0:T(1024)(128)(2,1)S(1)}, bf16[1536]{0:T(1024)(128)(2,1)S(1)}) all-reduce(bf16[1536]{0:T(1024)(128)(2,1)S(1)} %get-tuple-element.182, bf16[1536]{0:T(1024)(128)(2,1)S(1)} %get-tuple-element.183), channel_id=1, replica_groups=mesh['section'=2,'tensor'=8,'dp'=8] {'dp'}, use_global_device_ids=true, to_apply=%region_54.55 | all-reduce | flops 3072 | bytes 12288 | tf_op jit(solution)/shard_map/psum | solution.py:421
  1143.2 4.8 all-to-all-start.22
  1149.9 3.2 all-to-all-done.22
  1154.4 203.5 %all-reduce.4.cloned.1.call-done = (bf16[1,1536,192]{1,2,0:T(8,128)(2,1)}, bf16[1,1536,96]{1,2,0:T(8,128)(2,1)}, bf16[1,1536,96]{1,2,0:T(8,128)(2,1)}, bf16[1,19...) async-done(((bf16[1,1536,192]{1,2,0:T(8,128)(2,1)}, bf16[1,1536,96]{1,2,0:T(8,128)(2,1)}, ...) | async-done | bytes 6488080 | tf_op jit(solution)/shard_map/psum | solution.py:417
  1357.9 3.6 broadcast_in_dim.373
  (673 shorter events, 313.6 us)
Async XLA Ops:
  7.2 107.5 %copy-start = (bf16[1,512,1536]{2,1,0:T(8,128)(2,1)S(1)}, bf16[1,512,1536]{2,1,0:T(8,128)(2,1)}, u32[]{:S(2)}) copy-start(bf16[1,512,1536]{2,1,0:T(8,128)(2,1)} %param.23) | copy-start | bytes 4718596
  7.2 7.0 copy-start.4
  7.2 7.9 copy-start.182
  7.2 7.9 copy-start.41
  7.2 63.4 %copy-start.161 = (f32[48]{0:T(128)}, f32[48]{0:T(128)S(1)}, u32[]{:S(2)}) copy-start(f32[48]{0:T(128)S(1)} %multiply_exponential_fusion) | copy-start | bytes 580
  9.9 60.8 %copy-start.168 = (f32[256]{0:T(256)}, f32[256]{0:T(256)S(1)}, u32[]{:S(2)}) copy-start(f32[256]{0:T(256)S(1)} %subtract_convert_fusion.7) | copy-start | bytes 3076
  81.8 13.9 %all-to-all-start = ((bf16[8,32,1536]{2,1,0:T(8,128)(2,1)}), bf16[8,32,1536]{2,1,0:T(8,128)(2,1)}, u32[]{:S(2)}, u32[]{:S(2)}) async-start(bf16[8,32,1536]{2,1,0:T(8,128)(2,1)} %bitcast.644), calls=%async_computation | async-start | bytes 1572864 | tf_op jit(solution)/shard_map/all_to_all | solution.py:25
  97.0 14.6 %copy-start.1 = (bf16[1,1536,512]{2,1,0:T(8,128)(2,1)S(1)}, bf16[1,1536,512]{2,1,0:T(8,128)(2,1)}, u32[]{:S(2)}) copy-start(bf16[1,1536,512]{2,1,0:T(8,128)(2,1)} %param.21) | copy-start | bytes 4718596
  98.2 29.8 %copy-start.63 = (f32[32,1536]{1,0:T(8,128)}, f32[32,1536]{1,0:T(8,128)S(1)}, u32[]{:S(2)}) copy-start(f32[32,1536]{1,0:T(8,128)S(1)} %get-tuple-element.88) | copy-start | bytes 589828
  114.7 13.2 copy-start.65
  128.0 18.8 %copy-start.5 = (bf16[2,256,1536]{2,1,0:T(8,128)(2,1)S(1)}, bf16[2,256,1536]{2,1,0:T(8,128)(2,1)}, u32[]{:S(2)}) copy-start(bf16[2,256,1536]{2,1,0:T(8,128)(2,1)} %param.12) | copy-start | bytes 4718596
  128.0 2.4 collective-permute-start
  218.0 14.4 %all-to-all-start.4 = ((bf16[8,32,1536]{2,1,0:T(8,128)(2,1)}), bf16[8,32,1536]{2,1,0:T(8,128)(2,1)}, u32[]{:S(2)}, u32[]{:S(2)}) async-start(bf16[8,32,1536]{2,1,0:T(8,128)(2,1)} %bitcast.646), calls=%async_computation.4 | async-start | bytes 1572864 | tf_op jit(solution)/shard_map/all_to_all | solution.py:25
  236.4 13.7 all-to-all-start.5
  256.6 13.4 copy-start.58
  257.1 12.9 copy-start.50
  257.2 12.9 copy-start.132
  271.4 2.2 collective-permute-start.1
  274.5 17.9 %all-to-all-start.7 = ((bf16[8,32,1536]{2,1,0:T(8,128)(2,1)}), bf16[8,32,1536]{2,1,0:T(8,128)(2,1)}, u32[]{:S(2)}, u32[]{:S(2)}) async-start(bf16[8,32,1536]{2,1,0:T(8,128)(2,1)} %broadcast_in_dim.185), calls=%async_computation.7 | async-start | bytes 1572864 | tf_op jit(solution)/shard_map/all_to_all | solution.py:31
  292.5 83.9 %all-to-all-start.11 = ((bf16[8,32,1536]{2,1,0:T(8,128)(2,1)}), bf16[8,32,1536]{2,1,0:T(8,128)(2,1)}, u32[]{:S(2)}, u32[]{:S(2)}) async-start(bf16[8,32,1536]{2,1,0:T(8,128)(2,1)} %bitcast.642), calls=%async_computation.11 | async-start | bytes 1572864 | tf_op jit(solution)/shard_map/all_to_all | solution.py:25
  376.4 13.6 all-to-all-start.8
  382.2 10.1 copy-start.189
  382.2 10.1 copy-start.191
  396.5 13.7 all-to-all-start.12
  402.6 88.8 %reduce-scatter.7.cloned.1.call-start = ((), (), s32[]{:S(2)}) async-start(), calls=%async_computation.29 | async-start | bytes 442368 | tf_op jit(solution)/shard_map/reduce_scatter | solution.py:291
  419.7 145.5 %reduce-scatter.9.cloned.1.call-start = ((), (), s32[]{:S(2)}) async-start(), calls=%async_computation.30 | async-start | bytes 442368 | tf_op jit(solution)/shard_map/reduce_scatter | solution.py:294
  568.0 13.8 %all-to-all-start.13 = ((bf16[8,32,1536]{2,1,0:T(8,128)(2,1)}), bf16[8,32,1536]{2,1,0:T(8,128)(2,1)}, u32[]{:S(2)}, u32[]{:S(2)}) async-start(bf16[8,32,1536]{2,1,0:T(8,128)(2,1)} %bitcast.649), calls=%async_computation.15 | async-start | bytes 1572864 | tf_op jit(solution)/shard_map/all_to_all | solution.py:25
  583.7 15.0 %all-to-all-start.9 = ((bf16[8,32,1536]{2,1,0:T(8,128)(2,1)}), bf16[8,32,1536]{2,1,0:T(8,128)(2,1)}, u32[]{:S(2)}, u32[]{:S(2)}) async-start(bf16[8,32,1536]{2,1,0:T(8,128)(2,1)} %broadcast_in_dim.187), calls=%async_computation.9 | async-start | bytes 1572864 | tf_op jit(solution)/shard_map/all_to_all | solution.py:31
  594.4 4.3 collective-permute-start.2
  600.5 15.6 %all-to-all-start.14 = ((bf16[8,32,1536]{2,1,0:T(8,128)(2,1)}), bf16[8,32,1536]{2,1,0:T(8,128)(2,1)}, u32[]{:S(2)}, u32[]{:S(2)}) async-start(bf16[8,32,1536]{2,1,0:T(8,128)(2,1)} %broadcast_in_dim.350), calls=%async_computation.16 | async-start | bytes 1572864 | tf_op jit(solution)/shard_map/all_to_all | solution.py:31
  624.4 15.9 %all-to-all-start.15 = ((bf16[8,32,1536]{2,1,0:T(8,128)(2,1)}), bf16[8,32,1536]{2,1,0:T(8,128)(2,1)}, u32[]{:S(2)}, u32[]{:S(2)}) async-start(bf16[8,32,1536]{2,1,0:T(8,128)(2,1)} %bitcast.643), calls=%async_computation.17 | async-start | bytes 1572864 | tf_op jit(solution)/shard_map/all_to_all | solution.py:25
  646.6 20.0 %all-to-all-start.16 = ((bf16[8,32,1536]{2,1,0:T(8,128)(2,1)}), bf16[8,32,1536]{2,1,0:T(8,128)(2,1)}, u32[]{:S(2)}, u32[]{:S(2)}) async-start(bf16[8,32,1536]{2,1,0:T(8,128)(2,1)} %broadcast_in_dim.352), calls=%async_computation.18 | async-start | bytes 1572864 | tf_op jit(solution)/shard_map/all_to_all | solution.py:31
  652.4 94.2 %reduce-scatter.11.cloned.1.call-start = ((), (), s32[]{:S(2)}) async-start(), calls=%async_computation.31 | async-start | bytes 442368 | tf_op jit(solution)/shard_map/reduce_scatter | solution.py:291
  676.3 144.0 %reduce-scatter.13.cloned.1.call-start = ((), (), s32[]{:S(2)}) async-start(), calls=%async_computation.32 | async-start | bytes 442368 | tf_op jit(solution)/shard_map/reduce_scatter | solution.py:294
  823.2 13.8 %all-to-all-start.17 = ((bf16[8,32,1536]{2,1,0:T(8,128)(2,1)}), bf16[8,32,1536]{2,1,0:T(8,128)(2,1)}, u32[]{:S(2)}, u32[]{:S(2)}) async-start(bf16[8,32,1536]{2,1,0:T(8,128)(2,1)} %bitcast.647), calls=%async_computation.21 | async-start | bytes 1572864 | tf_op jit(solution)/shard_map/all_to_all | solution.py:25
  837.0 6.8 copy-start.11
  837.0 6.9 copy-start.13
  837.0 6.9 copy-start.95
  842.6 3.6 collective-permute-start.3
  847.1 18.2 %all-to-all-start.18 = ((bf16[8,32,1536]{2,1,0:T(8,128)(2,1)}), bf16[8,32,1536]{2,1,0:T(8,128)(2,1)}, u32[]{:S(2)}, u32[]{:S(2)}) async-start(bf16[8,32,1536]{2,1,0:T(8,128)(2,1)} %broadcast_in_dim.353), calls=%async_computation.22 | async-start | bytes 1572864 | tf_op jit(solution)/shard_map/all_to_all | solution.py:31
  873.8 16.9 %all-to-all-start.19 = ((bf16[8,32,1536]{2,1,0:T(8,128)(2,1)}), bf16[8,32,1536]{2,1,0:T(8,128)(2,1)}, u32[]{:S(2)}, u32[]{:S(2)}) async-start(bf16[8,32,1536]{2,1,0:T(8,128)(2,1)} %bitcast.133), calls=%async_computation.23 | async-start | bytes 1572864 | tf_op jit(solution)/shard_map/all_to_all | solution.py:25
  892.7 8.4 copy-start.67
  895.4 16.2 %all-to-all-start.20 = ((bf16[8,32,1536]{2,1,0:T(8,128)(2,1)}), bf16[8,32,1536]{2,1,0:T(8,128)(2,1)}, u32[]{:S(2)}, u32[]{:S(2)}) async-start(bf16[8,32,1536]{2,1,0:T(8,128)(2,1)} %broadcast_in_dim.354), calls=%async_computation.24 | async-start | bytes 1572864 | tf_op jit(solution)/shard_map/all_to_all | solution.py:31
  901.1 90.0 %reduce-scatter.15.cloned.1.call-start = ((), (), s32[]{:S(2)}) async-start(), calls=%async_computation.33 | async-start | bytes 442368 | tf_op jit(solution)/shard_map/reduce_scatter | solution.py:291
  920.8 144.0 %reduce-scatter.17.cloned.1.call-start = ((), (), s32[]{:S(2)}) async-start(), calls=%async_computation.34 | async-start | bytes 442368 | tf_op jit(solution)/shard_map/reduce_scatter | solution.py:294
  929.9 427.9 %all-reduce.4.cloned.1.call-start = ((), (), s32[]{:S(2)}) async-start(), calls=%async_computation.35 | async-start | bytes 12976128 | tf_op jit(solution)/shard_map/psum | solution.py:417
  933.8 58.2 %copy-start.164 = (f32[48]{0:T(128)S(1)}, f32[48]{0:T(128)}, u32[]{:S(2)}) copy-start(f32[48]{0:T(128)} %copy-done.161) | copy-start | bytes 580
  933.8 58.1 %copy-start.170 = (f32[256]{0:T(256)S(1)}, f32[256]{0:T(256)}, u32[]{:S(2)}) copy-start(f32[256]{0:T(256)} %copy-done.168) | copy-start | bytes 3076
  936.1 57.0 %copy-start.33 = (bf16[1,256,1536]{2,1,0:T(8,128)(2,1)S(1)}, bf16[1,256,1536]{2,1,0:T(8,128)(2,1)}, u32[]{:S(2)}) copy-start(bf16[1,256,1536]{2,1,0:T(8,128)(2,1)} %get-tuple-element.40) | copy-start | bytes 2359300
  1068.7 6.7 copy-start.193
  1070.1 23.0 %copy-start.27 = (bf16[1,1536,192]{1,2,0:T(8,128)(2,1)S(1)}, bf16[1,1536,192]{1,2,0:T(8,128)(2,1)}, u32[]{:S(2)}) copy-start(bf16[1,1536,192]{1,2,0:T(8,128)(2,1)} %param.16) | copy-start | bytes 1769476
  1070.1 22.2 %all-to-all-start.10 = ((bf16[8,32,1536]{2,1,0:T(8,128)(2,1)}), bf16[8,32,1536]{2,1,0:T(8,128)(2,1)S(1)}, u32[]{:S(2)}, u32[]{:S(2)}) async-start(bf16[8,32,1536]{2,1,0:T(8,128)(2,1)} %bitcast.648), calls=%async_computation.10 | async-start | bytes 1572864 | tf_op jit(solution)/shard_map/all_to_all | solution.py:25
  1075.4 18.0 %copy-start.145 = (bf16[256,48]{0,1:T(8,128)(2,1)S(1)}, bf16[256,48]{0,1:T(8,128)(2,1)}, u32[]{:S(2)}) copy-start(bf16[256,48]{0,1:T(8,128)(2,1)} %copy-done.144) | copy-start | bytes 73732
  1075.4 18.0 %copy-start.147 = (bf16[256,48]{0,1:T(8,128)(2,1)S(1)}, bf16[256,48]{0,1:T(8,128)(2,1)}, u32[]{:S(2)}) copy-start(bf16[256,48]{0,1:T(8,128)(2,1)} %copy-done.146) | copy-start | bytes 73732
  1095.7 21.5 %all-to-all-start.21 = ((bf16[8,32,1536]{2,1,0:T(8,128)(2,1)}), bf16[8,32,1536]{2,1,0:T(8,128)(2,1)S(1)}, u32[]{:S(2)}, u32[]{:S(2)}) async-start(bf16[8,32,1536]{2,1,0:T(8,128)(2,1)} %bitcast.161), calls=%async_computation.27 | async-start | bytes 1572864 | tf_op jit(solution)/shard_map/all_to_all | solution.py:25
  1100.7 17.8 %copy-start.156 = (f32[1536]{0:T(1024)S(1)}, f32[1536]{0:T(1024)}, u32[]{:S(2)}) copy-start(f32[1536]{0:T(1024)} %get-tuple-element.17) | copy-start | bytes 18436
  1100.7 17.8 %copy-start.157 = (f32[1536]{0:T(1024)S(1)}, f32[1536]{0:T(1024)}, u32[]{:S(2)}) copy-start(f32[1536]{0:T(1024)} %get-tuple-element.19) | copy-start | bytes 18436
  1100.7 17.8 %copy-start.158 = (f32[1536]{0:T(1024)S(1)}, f32[1536]{0:T(1024)}, u32[]{:S(2)}) copy-start(f32[1536]{0:T(1024)} %get-tuple-element.15) | copy-start | bytes 18436
  1100.7 17.8 %copy-start.159 = (f32[1536]{0:T(1024)S(1)}, f32[1536]{0:T(1024)}, u32[]{:S(2)}) copy-start(f32[1536]{0:T(1024)} %get-tuple-element.11) | copy-start | bytes 18436
  1100.7 17.8 %copy-start.160 = (f32[1536]{0:T(1024)S(1)}, f32[1536]{0:T(1024)}, u32[]{:S(2)}) copy-start(f32[1536]{0:T(1024)} %get-tuple-element.21) | copy-start | bytes 18436
  1100.7 47.3 %copy-start.85 = (f32[32,1536]{1,0:T(8,128)S(1)}, f32[32,1536]{1,0:T(8,128)}, u32[]{:S(2)}) copy-start(f32[32,1536]{1,0:T(8,128)} %copy-done.84) | copy-start | bytes 589828
  1100.7 47.3 %copy-start.110 = (f32[32,1536]{1,0:T(8,128)S(1)}, f32[32,1536]{1,0:T(8,128)}, u32[]{:S(2)}) copy-start(f32[32,1536]{1,0:T(8,128)} %get-tuple-element.46) | copy-start | bytes 589828
  1100.8 48.3 %copy-start.109 = (f32[1,32,1536]{2,1,0:T(8,128)S(1)}, f32[1,32,1536]{2,1,0:T(8,128)}, u32[]{:S(2)}) copy-start(f32[1,32,1536]{2,1,0:T(8,128)} %get-tuple-element.43) | copy-start | bytes 589828
  1143.2 9.9 all-to-all-start.22
  (169 other events, 368.7 us)
Sparse Core Ops, SparseCore 0:
  419.9 71.4 reduce-scatter.6
  495.4 69.7 reduce-scatter.8
  676.5 70.1 reduce-scatter.10
  750.6 69.7 reduce-scatter.12
  920.9 70.1 reduce-scatter.14
  995.1 69.6 reduce-scatter.16
  1069.0 288.8 all-reduce.3
where the time goes:
time: 1390 us; the launch traced here: 1380 us
  waiting for transfers between devices  690 us (50%)
  blocking collectives  196 us (14%)
  matrix products  153 us (11%)
  starting transfers between devices  116 us (8%)
  other arithmetic  107 us (8%)
  local copies, waits for them, and re-layouts  99.1 us (7%)
  between operations  16.6 us (1%)
    reduce_scatter x3, waiting for transfers between devices, layer_backward(): lax.psum_scatter(grad_values_part.astype(jnp.bfloat16), 'dp', scatter_dim...  208 us
    psum x1, waiting for transfers between devices, on_device(): lax.psum(totals[1].astype(jnp.bfloat16), 'dp').astype(jnp.float32)  203 us
    reduce_scatter x3, waiting for transfers between devices, layer_backward(): lax.psum_scatter(grad_keys_part.astype(jnp.bfloat16), 'dp', scatter_dimen...  172 us
    all_gather x3, blocking collectives, one_gather(): lines, at, finished = (lax.all_gather(line, axis), 0, [])  117 us
    all_to_all x10, waiting for transfers between devices, summed_on_arrival(): blocks = lax.all_to_all(in_blocks(x, dim, peers), axis, 0, 0, tiled=True)  67.7 us
    all_to_all x10, starting transfers between devices, summed_on_arrival(): blocks = lax.all_to_all(in_blocks(x, dim, peers), axis, 0, 0, tiled=True)  57 us
    all_to_all x9, starting transfers between devices, copy_for_each(): lax.all_to_all(jnp.broadcast_to(x[None], (peers, *x.shape)), axis, 0, 0,...  53.2 us
    dot_general x21, matrix products, outer_sum(): lax.dot_general(left_side, right_side, (((0,), (0,)), ((), ())), preferre...  47 us
  transfers between devices with their start and end apart: 30, of which 25 were waited for; matrix products, arithmetic and copies ran while one was open for 12% of the time, Pallas kernels for 0%

commit v1 on v0

v1 whole, which is shorter than its diff:
```python
import math

import jax
import jax.numpy as jnp
from jax import lax
from jax.experimental import pallas as pl
from jax.experimental.pallas import tpu as pltpu
from jax.sharding import PartitionSpec as P

MESH = pl.DeviceIdType.MESH
F32 = jnp.float32
BF16 = jnp.bfloat16

HD = 96
HALF = HD // 2
D = 1536
FF = 512
ROWS = 256
OWN = 32
SCALE = 1.0 / math.sqrt(HD)
EPS = 1e-05
ROPE = 100000.0
MASKED = -1e30


def dot(a, b):
    return lax.dot_general(a, b, (((1,), (0,)), ((), ())), preferred_element_type=F32)


def dot_nt(a, b):
    return lax.dot_general(a, b, (((1,), (1,)), ((), ())), preferred_element_type=F32)


def dot_tn(a, b):
    return lax.dot_general(a, b, (((0,), (0,)), ((), ())), preferred_element_type=F32)


def lanes_of(v):
    return lax.broadcasted_iota(jnp.int32, v.shape, 1)


def swapped(v):
    return jnp.where(lanes_of(v) < HALF, pltpu.roll(v, 128 - HALF, 1), pltpu.roll(v, HALF, 1))


def factor_of(v):
    return lax.rsqrt(jnp.mean(v * v, axis=-1, keepdims=True) + EPS)


def kernel(
    x_hbm, ct_hbm, wqkv_hbm, wo_hbm, wg_hbm, wu_hbm, wd_hbm, gains_hbm, cos_ref, sin_ref, beg_ref,
    y_out, dx_out, ga_out, gb_out, gn_out,
    wqkv, wo, wgu, wd, gains, x_v, df,
    n1, n2, q2, q2t, kv, o_f, o_b, stat_m, stat_l, gate_s, up_s, u_s, x_own, h_own,
    rsrc, land, da, do2, do2t, dgu, dq, dqkv, dkv_t, dkv_src, dkv_land, acc, s_m,
    ga, gb, za, zb, xa, xb, fa, fb, yb, dxb, dgain, dg_peer, dg_t, dg_d,
    w_l, w_s, w_r, ag_s, ag_r, rs_s, rs_r, kv_s, kv_r, dkv_s, dkv_r, out_l, out_s, out_r,
    gs, gr, zs, zr, xs, xr, cs, cr, es, er, gl, ns, nr,
):
    sec = lax.axis_index("section")
    t = lax.axis_index("tensor")
    d = lax.axis_index("dp")
    other = 1 - sec
    z, xh = d // 2, d % 2

    barrier = pltpu.get_barrier_semaphore()

    def greet(axis, me, k, _):
        pl.semaphore_signal(barrier, inc=1, device_id={axis: (me + k) % 8}, device_id_type=MESH)
        return _

    pl.semaphore_signal(barrier, inc=1, device_id={"section": other}, device_id_type=MESH)
    lax.fori_loop(1, 8, lambda k, c: greet("tensor", t, k, c), 0)
    lax.fori_loop(1, 8, lambda k, c: greet("dp", d, k, c), 0)

    x_copy = pltpu.make_async_copy(x_hbm.at[sec], x_v, w_l.at[6])
    ct_copy = pltpu.make_async_copy(ct_hbm.at[sec], df, w_l.at[7])
    own_parts = [
        (wqkv_hbm, wqkv),
        (wo_hbm, wo),
        (wg_hbm, wgu.at[:, :, 0:FF]),
        (wu_hbm, wgu.at[:, :, FF : 2 * FF]),
        (wd_hbm, wd),
        (gains_hbm, gains),
    ]
    own_copies = [pltpu.make_async_copy(a, b.at[sec], w_l.at[i]) for i, (a, b) in enumerate(own_parts)]
    x_copy.start()
    own_copies[5].start()
    for i in range(5):
        own_copies[i].start()
    ct_copy.start()
    pl.semaphore_wait(barrier, 15)
    sent_parts = [
        pltpu.make_async_remote_copy(
            src_ref=a, dst_ref=b.at[sec], send_sem=w_s.at[i], recv_sem=w_r.at[i],
            device_id={"section": other}, device_id_type=MESH,
        )
        for i, (a, b) in enumerate(own_parts)
    ]
    for i in (5, 0, 1, 2, 3, 4):
        sent_parts[i].start()

    def weight_ready(layer, *which):
        @pl.when(layer == sec)
        def _():
            for i in which:
                own_copies[i].wait()

        @pl.when(layer != sec)
        def _():
            for i in which:
                a, b = own_parts[i]
                pltpu.make_async_remote_copy(
                    src_ref=a, dst_ref=b.at[other], send_sem=w_s.at[i], recv_sem=w_r.at[i],
                    device_id={"section": other}, device_id_type=MESH,
                ).wait_recv()

    def rows_of(i):
        return pl.ds(pl.multiple_of(i * OWN, OWN), OWN)

    my_rows = rows_of(t)

    def ag_start(buf, i):
        def body(k, c):
            p = (t + k) % 8
            pltpu.make_async_remote_copy(
                src_ref=buf.at[my_rows], dst_ref=buf.at[my_rows], send_sem=ag_s.at[i, p], recv_sem=ag_r.at[i, t],
                device_id={"tensor": p}, device_id_type=MESH,
            ).start()
            return c

        lax.fori_loop(1, 8, body, 0)

    def ag_wait(buf, i):
        def body(k, c):
            p = (t + k) % 8
            copy = pltpu.make_async_remote_copy(
                src_ref=buf.at[my_rows], dst_ref=buf.at[rows_of(p)], send_sem=ag_s.at[i, p], recv_sem=ag_r.at[i, p],
                device_id={"tensor": p}, device_id_type=MESH,
            )
            copy.wait_recv()
            copy.wait_send()
            return c

        lax.fori_loop(1, 8, body, 0)

    def rs_start(i):
        def body(k, c):
            p = (t + k) % 8
            pltpu.make_async_remote_copy(
                src_ref=rsrc.at[i, rows_of(p)], dst_ref=land.at[i, t], send_sem=rs_s.at[i, p], recv_sem=rs_r.at[i, t],
                device_id={"tensor": p}, device_id_type=MESH,
            ).start()
            return c

        lax.fori_loop(1, 8, body, 0)

    def rs_sum(i):
        acc_rows = rsrc[i, my_rows, :].astype(F32)

        def body(k, total):
            p = (t + k) % 8
            copy = pltpu.make_async_remote_copy(
                src_ref=rsrc.at[i, rows_of(p)], dst_ref=land.at[i, p], send_sem=rs_s.at[i, p], recv_sem=rs_r.at[i, p],
                device_id={"tensor": p}, device_id_type=MESH,
            )
            copy.wait_recv()
            copy.wait_send()
            return total + land[i, p].astype(F32)

        return lax.fori_loop(1, 8, body, acc_rows)

    def allowed_of(j):
        rows = lax.broadcasted_iota(jnp.int32, (ROWS, ROWS), 0) + d * ROWS
        cols = lax.broadcasted_iota(jnp.int32, (ROWS, ROWS), 1) + j * ROWS
        return (cols <= rows) & (cols >= beg_ref[...][:, 0:1])

    weight_ready(0, 5)
    x_copy.wait()

    def first_norm(i, c):
        rows = pl.ds(pl.multiple_of(i * OWN, OWN), OWN)
        v = x_v[rows, :].astype(F32)
        n1[0, rows, :] = (v * factor_of(v) * gains[0, 0:1, :]).astype(BF16)
        return c

    lax.fori_loop(0, ROWS // OWN, first_norm, 0)
    x_own[0] = x_v[my_rows, :].astype(F32)

    def forward_layer(layer, c):
        @pl.when(layer == 1)
        def _():
            weight_ready(1, 5)
            v = x_own[1]
            n1[1, my_rows, :] = (v * factor_of(v) * gains[1, 0:1, :]).astype(BF16)
            ag_start(n1.at[1], 0)
            ag_wait(n1.at[1], 0)

        weight_ready(layer, 0)
        raw = dot(n1[layer], wqkv[layer])
        c0, c1, c2 = raw[:, 0:128], raw[:, 128:256], raw[:, 256:384]
        lane = lanes_of(c0)
        q1 = jnp.where(lane < 32, pltpu.roll(c0, 32, 1), pltpu.roll(c1, 32, 1))
        k0 = jnp.where(lane < 64, pltpu.roll(c1, 64, 1), pltpu.roll(c2, 64, 1))
        v0 = pltpu.roll(c2, 96, 1)
        cosine, sine = cos_ref[...], sin_ref[...]
        for h, part in ((0, c0), (1, q1)):
            turned = part * cosine + swapped(part) * sine
            q2[layer, pl.ds(h * ROWS, ROWS), :] = turned[:, 0:HD].astype(BF16)
            q2t[layer, :, pl.ds(h * ROWS, ROWS)] = jnp.transpose(turned)[0:HD, :].astype(BF16)
        turned = k0 * cosine + swapped(k0) * sine
        kv[layer, d, pl.ds(0, HD), :] = jnp.transpose(turned)[0:HD, :].astype(BF16)
        kv[layer, d, pl.ds(HD, HD), :] = jnp.transpose(v0)[0:HD, :].astype(BF16)

        def kv_copy(owner, to):
            return pltpu.make_async_remote_copy(
                src_ref=kv.at[layer, owner], dst_ref=kv.at[layer, owner], send_sem=kv_s.at[to], recv_sem=kv_r.at[owner, layer],
                device_id={"dp": to}, device_id_type=MESH,
            )

        def kv_send(k, c):
            kv_copy(d, k).start()
            return c

        lax.fori_loop(d + 1, 8, kv_send, 0)
        s_m[...] = jnp.full(s_m.shape, MASKED, F32)
        stat_l[layer] = jnp.zeros((2 * ROWS, 1), F32)
        acc[...] = jnp.zeros(acc.shape, F32)

        def attend(i, c):
            j = d - i

            @pl.when(i > 0)
            def _():
                kv_copy(j, d).wait_recv()

            allowed = allowed_of(j)
            for h in range(2):
                rows = pl.ds(h * ROWS, ROWS)
                s = dot(q2[layer, rows, :], kv[layer, j, pl.ds(0, HD), :]) * SCALE
                s = jnp.where(allowed, s, MASKED)
                old = s_m[rows, :]
                new = jnp.maximum(old, jnp.max(s, axis=-1, keepdims=True))
                p = jnp.exp(s - new)
                shrink = jnp.exp(old - new)
                s_m[rows, :] = new
                stat_l[layer, rows, :] = stat_l[layer, rows, :] * shrink + jnp.sum(p, axis=-1, keepdims=True)
                acc[rows, :] = acc[rows, :] * shrink + dot_nt(p.astype(BF16), kv[layer, j, pl.ds(HD, HD), :])
            return c

        lax.fori_loop(0, d + 1, attend, 0)
        total = stat_l[layer]
        mixed = acc[...] / total
        o_f[layer] = mixed
        o_b[layer] = mixed.astype(BF16)
        stat_m[layer] = s_m[...] + jnp.log(total)

        def kv_sent(k, c):
            kv_copy(d, k).wait_send()
            return c

        weight_ready(layer, 1)

        def out_part(n, c):
            cols = pl.ds(pl.multiple_of(n * 512, 512), 512)
            part = dot(o_b[layer, pl.ds(0, ROWS), :], wo[layer, pl.ds(0, HD), cols])
            part += dot(o_b[layer, pl.ds(ROWS, ROWS), :], wo[layer, pl.ds(HD, HD), cols])
            rsrc[0, :, cols] = part.astype(BF16)
            return c

        lax.fori_loop(0, 3, out_part, 0)
        rs_start(0)
        lax.fori_loop(d + 1, 8, kv_sent, 0)
        v = x_own[layer] + rs_sum(0)
        h_own[layer] = v
        n2[layer, my_rows, :] = (v * factor_of(v) * gains[layer, 8:9, :]).astype(BF16)
        ag_start(n2.at[layer], 1)
        ag_wait(n2.at[layer], 1)
        weight_ready(layer, 2, 3)

        def units(n, c):
            cols = pl.ds(pl.multiple_of(n * 256, 256), 256)
            upper = pl.ds(pl.multiple_of(n * 256 + FF, 256), 256)
            g = dot(n2[layer], wgu[layer, :, cols])
            up = dot(n2[layer], wgu[layer, :, upper])
            gate_s[layer, :, cols] = g
            up_s[layer, :, cols] = up
            u_s[layer, :, cols] = (g * jax.nn.sigmoid(g) * up).astype(BF16)
            return c

        lax.fori_loop(0, 2, units, 0)
        weight_ready(layer, 4)

        def down_part(n, c):
            cols = pl.ds(pl.multiple_of(n * 512, 512), 512)
            rsrc[1, :, cols] = dot(u_s[layer], wd[layer, :, cols]).astype(BF16)
            return c

        lax.fori_loop(0, 3, down_part, 0)
        rs_start(1)
        y = (h_own[layer] + rs_sum(1)).astype(BF16)
        yb[layer] = y

        @pl.when(layer == 0)
        def _():
            x_own[1] = y.astype(F32)

        row_out(layer, yb, y_out, 0)
        return c

    def row_out(layer, buf, out, i):
        @pl.when(layer == sec)
        def _():
            pltpu.make_async_copy(buf.at[layer], out.at[sec], out_l.at[i]).start()

        @pl.when(layer != sec)
        def _():
            pltpu.make_async_remote_copy(
                src_ref=buf.at[layer], dst_ref=out.at[sec], send_sem=out_s.at[i], recv_sem=out_r.at[i],
                device_id={"section": other}, device_id_type=MESH,
            ).start()

    def row_out_wait(buf, out, i):
        pltpu.make_async_copy(buf.at[sec], out.at[sec], out_l.at[i]).wait()
        copy = pltpu.make_async_remote_copy(
            src_ref=buf.at[other], dst_ref=out.at[other], send_sem=out_s.at[i], recv_sem=out_r.at[i],
            device_id={"section": other}, device_id_type=MESH,
        )
        copy.wait_send()
        copy.wait_recv()

    lax.fori_loop(0, 2, forward_layer, 0)

    ct_copy.wait()

    def to_owner(layer, buf, i):
        return pltpu.make_async_remote_copy(
            src_ref=buf.at[sec * (1 - layer)], dst_ref=buf.at[1], send_sem=gs.at[i], recv_sem=gr.at[i],
            device_id={"section": other}, device_id_type=MESH,
        )

    def z_copy(buf, landing, i, to, sender):
        slot = (sender - to + 3) % 4
        return pltpu.make_async_remote_copy(
            src_ref=buf.at[0, to], dst_ref=landing.at[slot], send_sem=zs.at[i, to], recv_sem=zr.at[i, slot],
            device_id={"dp": to * 2 + xh}, device_id_type=MESH,
        )

    def x_copy_of(buf, landing, i):
        half = landing.shape[0]
        return pltpu.make_async_remote_copy(
            src_ref=buf.at[0, z, pl.ds((1 - xh) * half, half)], dst_ref=landing, send_sem=xs.at[i], recv_sem=xr.at[i],
            device_id={"dp": z * 2 + 1 - xh}, device_id_type=MESH,
        )

    def x_back(done, i, which):
        half = done.shape[0] // 2
        part = done.at[pl.ds(which * half, half)]
        return pltpu.make_async_remote_copy(
            src_ref=part, dst_ref=part, send_sem=cs.at[i], recv_sem=cr.at[i],
            device_id={"dp": z * 2 + 1 - xh}, device_id_type=MESH,
        )

    def z_back(done, out, i, to, sender):
        return pltpu.make_async_remote_copy(
            src_ref=done, dst_ref=out.at[sender], send_sem=es.at[i, to], recv_sem=er.at[i, sender],
            device_id={"dp": to * 2 + xh}, device_id_type=MESH,
        )

    def sum_step_1(buf, landing, i):
        to_owner(0, buf, i).wait_recv()
        rows = buf.shape[2] // 4
        for c in (2, 1, 3, 0):
            chunk = (z + c) % 4

            def add(n, carry):
                part = pl.ds(pl.multiple_of(n * rows, rows), rows)
                buf[0, chunk, part, :] = (buf[0, chunk, part, :].astype(F32) + buf[1, chunk, part, :].astype(F32)).astype(BF16)
                return carry

            lax.fori_loop(0, 4, add, 0)
            if c:
                z_copy(buf, landing, i, chunk, z).start()

    def sum_step_2(buf, landing, over, i):
        for c in range(1, 4):
            z_copy(buf, landing, i, z, (z + c) % 4).wait_recv()
        rows = buf.shape[2] // 4

        def add(n, carry):
            part = pl.ds(pl.multiple_of(n * rows, rows), rows)
            total = buf[0, z, part, :].astype(F32)
            for s in range(3):
                total += landing[s, part, :].astype(F32)
            buf[0, z, part, :] = total.astype(BF16)
            return carry

        lax.fori_loop(0, 4, add, 0)
        x_copy_of(buf, over, i).start()

    def sum_step_3(buf, over, done, i):
        x_copy_of(buf, over, i).wait_recv()
        half = over.shape[0]
        rows = half // 2

        def add(n, carry):
            part = pl.ds(pl.multiple_of(xh * half + n * rows, 16), rows)
            here = pl.ds(pl.multiple_of(n * rows, 16), rows)
            done[part, :] = (buf[0, z, part, :].astype(F32) + over[here, :].astype(F32)).astype(BF16)
            return carry

        lax.fori_loop(0, 2, add, 0)
        x_back(done, i, xh).start()

    def sum_step_4(done, out, i):
        x_back(done, i, 1 - xh).wait_recv()
        for c in (2, 1, 3):
            z_back(done, out, i, (z + c) % 4, z).start()
        pltpu.make_async_copy(done, out.at[z], gl.at[i]).start()

    def sum_step_5(buf, landing, over, done, out, i):
        x_copy_of(buf, over, i).wait_send()
        x_back(done, i, xh).wait_send()
        pltpu.make_async_copy(done, out.at[z], gl.at[i]).wait()
        for c in range(1, 4):
            peer = (z + c) % 4
            z_copy(buf, landing, i, peer, z).wait_send()
            z_back(done, out, i, peer, z).wait_send()
            z_back(done, out, i, z, peer).wait_recv()

    def backward_layer(step, c):
        layer = 1 - step
        mine = sec * (1 - layer)

        @pl.when(layer == 0)
        def _():
            ag_start(df, 2)

            @pl.when(sec == 1)
            def _():
                sum_step_1(ga, za, 0)

            ag_wait(df, 2)

        dy = df[my_rows, :].astype(F32)
        dxb[layer] = dy

        def unit_grads(n, c):
            cols = pl.ds(pl.multiple_of(n * 256, 256), 256)
            upper = pl.ds(pl.multiple_of(n * 256 + FF, 256), 256)
            du = dot_nt(df[...], wd[layer, cols, :])
            g, up = gate_s[layer, :, cols], up_s[layer, :, cols]
            sig = jax.nn.sigmoid(g)
            dgu[:, cols] = (du * up * sig * (1.0 + g * (1.0 - sig))).astype(BF16)
            dgu[:, upper] = (du * g * sig).astype(BF16)
            return c

        lax.fori_loop(0, 2, unit_grads, 0)

        def normed_part(n, c):
            cols = pl.ds(pl.multiple_of(n * 256, 256), 256)
            rsrc[0, :, cols] = dot_nt(dgu[...], wgu[layer, cols, :]).astype(BF16)
            return c

        lax.fori_loop(0, 6, normed_part, 0)
        rs_start(0)

        @pl.when((step == 1) & (sec == 0))
        def _():
            to_owner(1, ga, 0).wait_send()
            to_owner(1, gb, 1).wait_send()

        def unit_weights(n, c):
            cols = pl.ds(pl.multiple_of(n * 384, 384), 384)
            got = dot_tn(n2[layer, :, cols], dgu[...]).astype(BF16)
            ga[mine, n, pl.ds(0, 384), :] = got[:, 0:FF]
            ga[mine, n, pl.ds(384, 384), :] = got[:, FF : 2 * FF]
            cols = pl.ds(pl.multiple_of(n * 128, 128), 128)
            got = dot_tn(u_s[layer, :, cols], df[...]).astype(BF16)
            for i in range(3):
                ga[mine, n, pl.ds(768 + 128 * i, 128), :] = got[:, 512 * i : 512 * i + 512]
            return c

        lax.fori_loop(0, 4, unit_weights, 0)

        @pl.when(layer != sec)
        def _():
            to_owner(layer, ga, 0).start()

        @pl.when((step == 1) & (sec == 1))
        def _():
            sum_step_1(gb, zb, 1)

        dn = rs_sum(0)
        h = h_own[layer]
        r = factor_of(h)
        tt = dn * gains[layer, 8:9, :]
        dh = dxb[layer] + r * tt - h * (r * r * r * jnp.mean(h * tt, axis=-1, keepdims=True))
        dgain[layer, 1:2, :] = jnp.sum(dn * h * r, axis=0, keepdims=True)
        dxb[layer] = dh
        da[my_rows, :] = dh.astype(BF16)
        ag_start(da, 3)

        @pl.when((step == 1) & (sec == 1))
        def _():
            sum_step_2(ga, za, xa, 0)

        @pl.when((step == 1) & (sec == 0))
        def _():
            sum_step_1(ga, za, 0)

        ag_wait(da, 3)
        for h in range(2):
            rows = pl.ds(h * ROWS, ROWS)
            got = dot_nt(da[...], wo[layer, pl.ds(h * HD, HD), :])
            do2[rows, :] = got.astype(BF16)
            padded = jnp.concatenate([got, jnp.zeros((ROWS, 128 - HD), F32)], axis=1)
            do2t[:, rows] = jnp.transpose(padded)[0:HD, :].astype(BF16)
        dot_rows = jnp.sum(do2[...].astype(F32) * o_f[layer], axis=-1, keepdims=True)
        s_m[...] = dot_rows
        acc[...] = jnp.zeros(acc.shape, F32)

        def dkv_copy(to, sender):
            return pltpu.make_async_remote_copy(
                src_ref=dkv_src.at[to], dst_ref=dkv_land.at[layer, sender], send_sem=dkv_s.at[to], recv_sem=dkv_r.at[layer, sender],
                device_id={"dp": to}, device_id_type=MESH,
            )

        def attend_back(j, c):
            allowed = allowed_of(j)
            dkt = jnp.zeros((HD, ROWS), F32)
            dvt = jnp.zeros((HD, ROWS), F32)
            for h in range(2):
                rows = pl.ds(h * ROWS, ROWS)
                kt = kv[layer, j, pl.ds(0, HD), :]
                s = dot(q2[layer, rows, :], kt) * SCALE
                p = jnp.exp(jnp.where(allowed, s, MASKED) - stat_m[layer, rows, :])
                dp = dot(do2[rows, :], kv[layer, j, pl.ds(HD, HD), :])
                ds = (p * (dp - s_m[rows, :])).astype(BF16)
                acc[rows, :] += dot_nt(ds, kt)
                dkt += dot(q2t[layer, :, rows], ds)
                dvt += dot(do2t[:, rows], p.astype(BF16))
            dkv_src[j, pl.ds(0, HD), :] = (dkt * SCALE).astype(BF16)
            dkv_src[j, pl.ds(HD, HD), :] = dvt.astype(BF16)

            @pl.when(j < d)
            def _():
                dkv_copy(j, d).start()

            return c

        lax.fori_loop(0, d + 1, attend_back, 0)

        def dkv_sent(k, c):
            dkv_copy(k, d).wait_send()
            return c

        def out_weights(n, c):
            cols = pl.ds(pl.multiple_of(n * 384, 384), 384)
            for h in range(2):
                got = dot_tn(o_b[layer, pl.ds(h * ROWS, ROWS), :], da[:, cols])
                gb[mine, n, pl.ds(h * HD, HD), :] = got.astype(BF16)
            return c

        lax.fori_loop(0, 4, out_weights, 0)
        lax.fori_loop(0, d, dkv_sent, 0)

        @pl.when((step == 1) & (sec == 1))
        def _():
            sum_step_2(gb, zb, xb, 1)
            sum_step_3(ga, xa, fa, 0)

        @pl.when((step == 1) & (sec == 0))
        def _():
            sum_step_2(ga, za, xa, 0)

        def dkv_sum(k, total):
            dkv_copy(d, k).wait_recv()
            return total + dkv_land[layer, k].astype(F32)

        dkv_total = lax.fori_loop(d + 1, 8, dkv_sum, dkv_src[d].astype(F32))
        dkv_t[...] = jnp.zeros(dkv_t.shape, F32)
        dkv_t[0, pl.ds(0, HD), :] = dkv_total[0:HD]
        dkv_t[1, pl.ds(0, HD), :] = dkv_total[HD : 2 * HD]
        dk_rot = jnp.transpose(dkv_t[0])
        dv = jnp.transpose(dkv_t[1])
        cosine, sine = cos_ref[...], sin_ref[...]
        dq[...] = jnp.zeros(dq.shape, F32)
        dq[:, 0:HD] = acc[...] * SCALE
        dq0, dq1 = dq[pl.ds(0, ROWS), :], dq[pl.ds(ROWS, ROWS), :]
        dq0 = dq0 * cosine - swapped(dq0) * sine
        dq1 = dq1 * cosine - swapped(dq1) * sine
        dk = dk_rot * cosine - swapped(dk_rot) * sine
        lane = lanes_of(dk)
        dqkv[:, 0:128] = jnp.where(lane < HD, dq0, pltpu.roll(dq1, 96, 1)).astype(BF16)
        dqkv[:, 128:256] = jnp.where(lane < 64, pltpu.roll(dq1, 96, 1), pltpu.roll(dk, 64, 1)).astype(BF16)
        dqkv[:, 256:384] = jnp.where(lane < 32, pltpu.roll(dk, 64, 1), pltpu.roll(dv, 32, 1)).astype(BF16)

        def input_part(n, c):
            cols = pl.ds(pl.multiple_of(n * 256, 256), 256)
            rsrc[1, :, cols] = dot_nt(dqkv[...], wqkv[layer, cols, :]).astype(BF16)
            return c

        lax.fori_loop(0, 6, input_part, 0)
        rs_start(1)

        def qkv_weights(n, c):
            cols = pl.ds(pl.multiple_of(n * 384, 384), 384)
            gb[mine, n, pl.ds(2 * HD, 384), :] = dot_tn(n1[layer, :, cols], dqkv[...]).astype(BF16)
            return c

        lax.fori_loop(0, 4, qkv_weights, 0)

        @pl.when(layer != sec)
        def _():
            to_owner(layer, gb, 1).start()

        @pl.when((step == 1) & (sec == 1))
        def _():
            sum_step_3(gb, xb, fb, 1)
            sum_step_4(fa, ga_out, 0)

        @pl.when((step == 1) & (sec == 0))
        def _():
            sum_step_3(ga, xa, fa, 0)

        dn = rs_sum(1)
        v = x_own[layer]
        r = factor_of(v)
        tt = dn * gains[layer, 0:1, :]
        dx = dxb[layer] + r * tt - v * (r * r * r * jnp.mean(v * tt, axis=-1, keepdims=True))
        dgain[layer, 0:1, :] = jnp.sum(dn * v * r, axis=0, keepdims=True)
        dxb[layer] = dx
        df[my_rows, :] = dx.astype(BF16)
        row_out(layer, dxb, dx_out, 1)
        return c

    dgain[...] = jnp.zeros(dgain.shape, F32)
    lax.fori_loop(0, 2, backward_layer, 0)

    mate = pltpu.make_async_remote_copy(
        src_ref=dgain.at[other], dst_ref=dg_peer, send_sem=ns.at[0, 0], recv_sem=nr.at[0, 0],
        device_id={"section": other}, device_id_type=MESH,
    )
    mate.start()

    @pl.when(sec == 0)
    def _():
        sum_step_4(fa, ga_out, 0)
        sum_step_1(gb, zb, 1)

    @pl.when(sec == 1)
    def _():
        sum_step_4(fb, gb_out, 1)

    def gain_copy(axis, i, buf, me, to, sender):
        return pltpu.make_async_remote_copy(
            src_ref=buf.at[me], dst_ref=buf.at[sender], send_sem=ns.at[i, to], recv_sem=nr.at[i, sender],
            device_id={axis: to}, device_id_type=MESH,
        )

    def gain_round(axis, i, buf, me):
        def send(k, c):
            gain_copy(axis, i, buf, me, (me + k) % 8, me).start()
            return c

        def take(k, total):
            p = (me + k) % 8
            gain_copy(axis, i, buf, me, p, p).wait_recv()
            return total + buf[p]

        def sent(k, c):
            gain_copy(axis, i, buf, me, (me + k) % 8, me).wait_send()
            return c

        lax.fori_loop(1, 8, send, 0)
        total = lax.fori_loop(1, 8, take, buf[me])
        lax.fori_loop(1, 8, sent, 0)
        return total

    mate.wait_recv()
    mate.wait_send()
    dg_t[t] = dgain[sec] + dg_peer[...]
    dg_d[d] = gain_round("tensor", 1, dg_t, t)

    @pl.when(sec == 0)
    def _():
        sum_step_2(gb, zb, xb, 1)

    gn_out[...] = gain_round("dp", 2, dg_d, d)

    @pl.when(sec == 0)
    def _():
        sum_step_3(gb, xb, fb, 1)
        sum_step_4(fb, gb_out, 1)

    @pl.when(sec == 1)
    def _():
        to_owner(0, ga, 0).wait_send()
        to_owner(0, gb, 1).wait_send()

    sum_step_5(ga, za, xa, fa, ga_out, 0)
    sum_step_5(gb, zb, xb, fb, gb_out, 1)
    row_out_wait(yb, y_out, 0)
    row_out_wait(dxb, dx_out, 1)
    for i in range(6):
        sent_parts[i].wait_send()


def step_call(*args):
    hbm = pl.BlockSpec(memory_space=pl.ANY)
    vmem = pl.BlockSpec(memory_space=pltpu.VMEM)
    dma = pltpu.SemaphoreType.DMA
    scratch = [
        pltpu.VMEM((2, D, 384), BF16), pltpu.VMEM((2, 192, D), BF16), pltpu.VMEM((2, D, 2 * FF), BF16),
        pltpu.VMEM((2, FF, D), BF16), pltpu.VMEM((2, 16, D), F32), pltpu.VMEM((ROWS, D), BF16), pltpu.VMEM((ROWS, D), BF16),
        pltpu.VMEM((2, ROWS, D), BF16), pltpu.VMEM((2, ROWS, D), BF16), pltpu.VMEM((2, 2 * ROWS, HD), BF16),
        pltpu.VMEM((2, HD, 2 * ROWS), BF16), pltpu.VMEM((2, 8, 2 * HD, ROWS), BF16), pltpu.VMEM((2, 2 * ROWS, HD), F32),
        pltpu.VMEM((2, 2 * ROWS, HD), BF16), pltpu.VMEM((2, 2 * ROWS, 1), F32), pltpu.VMEM((2, 2 * ROWS, 1), F32),
        pltpu.VMEM((2, ROWS, FF), F32), pltpu.VMEM((2, ROWS, FF), F32), pltpu.VMEM((2, ROWS, FF), BF16),
        pltpu.VMEM((2, OWN, D), F32), pltpu.VMEM((2, OWN, D), F32),
        pltpu.VMEM((2, ROWS, D), BF16), pltpu.VMEM((2, 8, OWN, D), BF16), pltpu.VMEM((ROWS, D), BF16),
        pltpu.VMEM((2 * ROWS, HD), BF16), pltpu.VMEM((HD, 2 * ROWS), BF16), pltpu.VMEM((ROWS, 2 * FF), BF16),
        pltpu.VMEM((2 * ROWS, 128), F32), pltpu.VMEM((ROWS, 384), BF16), pltpu.VMEM((2, 128, ROWS), F32),
        pltpu.VMEM((8, 2 * HD, ROWS), BF16), pltpu.VMEM((2, 8, 2 * HD, ROWS), BF16), pltpu.VMEM((2 * ROWS, HD), F32),
        pltpu.VMEM((2 * ROWS, 1), F32),
        pltpu.VMEM((2, 4, 1152, 512), BF16), pltpu.VMEM((2, 4, 576, 384), BF16), pltpu.VMEM((3, 1152, 512), BF16),
        pltpu.VMEM((3, 576, 384), BF16), pltpu.VMEM((576, 512), BF16), pltpu.VMEM((288, 384), BF16),
        pltpu.VMEM((1152, 512), BF16), pltpu.VMEM((576, 384), BF16),
        pltpu.VMEM((2, OWN, D), BF16), pltpu.VMEM((2, OWN, D), F32), pltpu.VMEM((2, 8, D), F32), pltpu.VMEM((8, D), F32),
        pltpu.VMEM((8, 8, D), F32), pltpu.VMEM((8, 8, D), F32),
        dma((8,)), dma((6,)), dma((6,)), dma((4, 8)), dma((4, 8)), dma((2, 8)), dma((2, 8)), dma((8,)), dma((8, 2)),
        dma((8,)), dma((2, 8)), dma((2,)), dma((2,)), dma((2,)),
        dma((2,)), dma((2,)), dma((2, 4)), dma((2, 3)), dma((2,)), dma((2,)), dma((2,)), dma((2,)), dma((2, 4)),
        dma((2, 4)), dma((2,)), dma((3, 8)), dma((3, 8)),
    ]
    return pl.pallas_call(
        kernel,
        out_shape=(
            jax.ShapeDtypeStruct((2, OWN, D), BF16),
            jax.ShapeDtypeStruct((2, OWN, D), F32),
            jax.ShapeDtypeStruct((4, 1152, 512), BF16),
            jax.ShapeDtypeStruct((4, 576, 384), BF16),
            jax.ShapeDtypeStruct((8, D), F32),
        ),
        in_specs=[hbm] * 8 + [vmem] * 3,
        out_specs=(hbm, hbm, hbm, hbm, vmem),
        scratch_shapes=scratch,
        compiler_params=pltpu.CompilerParams(
            collective_id=0, has_side_effects=True, vmem_limit_bytes=64 * 1024 * 1024 - 65536
        ),
        name="train_step",
    )(*args)


def on_device(inputs, cotangent, doc_lengths, norm_one, query_w, key_w, value_w, out_w, norm_two, gate_w, up_w, down_w):
    wqkv = jnp.concatenate([query_w[0], key_w[0], value_w[0]], axis=1)
    gains = jnp.concatenate([jnp.broadcast_to(norm_one, (8, D)), jnp.broadcast_to(norm_two, (8, D))]).astype(F32)
    lengths = lax.dynamic_index_in_dim(doc_lengths, lax.axis_index("section"), 0, keepdims=False)
    starts = jnp.cumsum(lengths) - lengths
    places = lax.axis_index("dp") * ROWS + jnp.arange(ROWS, dtype=jnp.int32)
    begins = jnp.max(jnp.where(starts[None, :] <= places[:, None], starts[None, :], 0), axis=1)
    inverse = jnp.exp(jnp.arange(HALF, dtype=F32) * (-2.0 * math.log(ROPE) / HD))
    angles = (places - begins).astype(F32)[:, None] * inverse[None, :]
    cosine, sine = jnp.cos(angles), jnp.sin(angles)
    rest = jnp.zeros((ROWS, 128 - HD), F32)
    cosine = jnp.concatenate([cosine, cosine, rest], axis=1)
    sine = jnp.concatenate([-sine, sine, rest], axis=1)
    begins = jnp.broadcast_to(begins[:, None], (ROWS, 128))
    y, dx, ga, gb, gn = step_call(
        inputs, cotangent, wqkv, out_w[0], gate_w[0], up_w[0], down_w[0], gains, cosine, sine, begins
    )
    gate = ga[:, 0:384].reshape(D, FF).astype(F32)
    up = ga[:, 384:768].reshape(D, FF).astype(F32)
    down = ga[:, 768:].reshape(4, 3, 128, 512).transpose(0, 2, 1, 3).reshape(FF, D).astype(F32)
    out = gb[:, 0:192].transpose(1, 0, 2).reshape(192, D).astype(F32)
    qkv = gb[:, 192:].reshape(D, 384)
    grads = (
        gn[0:1], qkv[:, 0:192].astype(F32), qkv[:, 192:288].astype(F32), qkv[:, 288:384].astype(F32), out, gn[1:2], gate, up, down,
    )
    return (y[None], dx[None]) + tuple(g if g.shape[0] == 1 else g[None] for g in grads)


def solution(mesh):
    in_specs = (
        P(None, "dp", None),
        P(None, "dp", None),
        P(),
        P("section", None),
        P("section", None, "tensor"),
        P("section", None, "tensor"),
        P("section", None, "tensor"),
        P("section", "tensor", None),
        P("section", None),
        P("section", None, "tensor"),
        P("section", None, "tensor"),
        P("section", "tensor", None),
    )
    out_specs = (
        P("section", None, ("dp", "tensor"), None),
        P("section", None, ("dp", "tensor"), None),
        P("section", None),
        P("section", None, "tensor"),
        P("section", None, "tensor"),
        P("section", None, "tensor"),
        P("section", "tensor", None),
        P("section", None),
        P("section", None, "tensor"),
        P("section", None, "tensor"),
        P("section", "tensor", None),
    )
    return jax.shard_map(on_device, mesh=mesh, in_specs=in_specs, out_specs=out_specs, check_vma=False)
```

time: 1390 us -> 381 us (0.27)
  waiting for transfers between devices: 690 us -> 0 us
  Pallas kernels: 0 us -> 343 us
  blocking collectives: 196 us -> 0 us
  matrix products: 153 us -> 0 us
  starting transfers between devices: 116 us -> 0 us
  other arithmetic: 107 us -> 11.6 us
  local copies, waits for them, and re-layouts: 99.1 us -> 21.5 us
  between operations: 16.6 us -> 0.84 us
    reduce_scatter x6 -> x0, waiting for transfers between devices: 380 us -> none  [the longest x3 208 us: layer_backward(): lax.psum_scatter(grad_values_part.astype(jnp.bfloat16), 'dp', scatter_dim...]
    pallas_call x0 -> x1, Pallas kernels: none -> 343 us  [step_call(): pl.pallas_call(kernel, out_shape=(jax.ShapeDtypeStruct((2, OWN, D), BF16)...]
    psum x1 -> x0, waiting for transfers between devices: 203 us -> none  [on_device(): lax.psum(totals[1].astype(jnp.bfloat16), 'dp').astype(jnp.float32)]
    dot_general x84 -> x0, matrix products: 153 us -> none  [the longest x21 47 us: outer_sum(): lax.dot_general(left_side, right_side, (((0,), (0,)), ((), ())), preferre...]
    all_gather x3 -> x0, blocking collectives: 117 us -> none  [one_gather(): lines, at, finished = (lax.all_gather(line, axis), 0, [])]
    all_to_all x19 -> x0, starting transfers between devices: 110 us -> none  [the longest x10 57 us: summed_on_arrival(): blocks = lax.all_to_all(in_blocks(x, dim, peers), axis, 0, 0, tiled=True)]
    all_to_all x19 -> x0, waiting for transfers between devices: 104 us -> none  [the longest x10 67.7 us: summed_on_arrival(): blocks = lax.all_to_all(in_blocks(x, dim, peers), axis, 0, 0, tiled=True)]
    all_to_all x4 -> x0, blocking collectives: 54.4 us -> none  [the longest x2 28.9 us: copy_for_each(): lax.all_to_all(jnp.broadcast_to(x[None], (peers, *x.shape)), axis, 0, 0,...]
  transfers between devices with their start and end apart: 30 -> 0, of which waited for: 25 -> 0; matrix products, arithmetic and copies ran while one was open for 12% -> 0% of each run, Pallas kernels for 0% -> 0%
where the time goes in v1:
time: 381 us; the launch traced here: 377 us
  Pallas kernels  343 us (90%)
  local copies, waits for them, and re-layouts  21.5 us (6%)
  other arithmetic  11.6 us (3%)
    pallas_call x1, Pallas kernels, step_call(): pl.pallas_call(kernel, out_shape=(jax.ShapeDtypeStruct((2, OWN, D), BF16)...  343 us

profile of v1, /device:TPU:24, one launch (start us, length us, event | category | flops | bytes accessed | tf_op | source)
XLA Modules:
  0.0 376.9 jit_solution(1236168234077394863)
XLA Ops:
  0.6 0.0 copy-start.1
  0.7 0.0 copy-start.3
  0.7 0.8 constant_dynamic-slice_fusion
  1.4 0.2 reduce-window_clone.1
  1.6 0.7 subtract_bitcast_fusion
  2.3 0.1 select_reduce_fusion
  2.4 0.0 copy-start.4
  2.5 0.5 fusion
  3.0 0.1 pad.5.clone
  3.1 0.8 maximum_maximum_fusion.1
  3.9 0.8 broadcast_in_dim.72.beg_ref
  4.7 0.0 copy-done.1
  4.7 0.3 copy.39
  5.0 0.0 copy-done.3
  5.0 0.2 copy.40
  5.2 0.0 copy-done.4
  5.2 0.0 copy-start.6
  5.2 0.0 copy-start.7
  5.2 0.2 copy.41
  5.5 1.5 pad_maximum_fusion.wqkv_hbm
  7.0 0.0 copy-done.6
  7.0 0.0 copy-done.7
  7.1 0.6 maximum_convert_fusion.gains_hbm
  7.7 342.8 %train_step.1 = (bf16[2,32,1536]{2,1,0:T(8,128)(2,1)}, f32[2,32,1536]{2,1,0:T(8,128)}, bf16[4,1152,512]{2,1,0:T(8,128)(2,1)}, bf16[4,576,384]{2,1,0:T(8,128)(2,1)}, f32[8,1536]{1,0:T(8,128)}) custom-call(bf16[2,256,1536]{2,1,0:T(8,128)(2,1)} %x_hbm.1, bf16[2,256,1536]{2,1,0:T(8,128)(2,1)} %ct_hbm.1, bf16[1536,384]{1,0:T(8,128)(2,1)} %pad_maximum_fusion.wqkv_hbm, ...), custom_call_target="tpu_custom_call" | custom-call | tf_op jit(solution)/shard_map/train_step/pallas_call | solution.py:737
  350.6 3.8 %fusion.1 = (bf16[4,384,512]{2,1,0:T(8,128)(2,1)}, bf16[4,384,512]{2,1,0:T(8,128)(2,1)S(1)}, bf16[4,384,512]{2,1,0:T(8,128)(2,1)S(1)}) fusion(bf16[4,1152,512]{2,1,0:T(8,128)(2,1)} %get-tuple-element.20), kind=kLoop, calls=%fused_computation.19 | loop fusion | bytes 9437184 | tf_op jit(solution)/shard_map/slice | solution.py:775
  354.4 3.6 bitcast_convert_fusion
  358.0 2.7 copy.46
  360.7 2.8 reshape.109
  363.5 0.0 copy-start
  363.5 3.7 copy.47
  367.2 0.0 copy-done
  367.2 0.1 slice.31
  367.3 0.3 fusion.2
  367.6 0.2 copy.49
  367.8 0.2 copy.50
  367.9 1.1 bitcast_convert_fusion.3
  369.1 0.1 slice.40
  369.1 0.3 copy.48
  369.4 1.1 bitcast_convert_fusion.2
  370.5 1.1 convert_bitcast_fusion
  371.7 0.8 copy.45
  372.4 0.0 copy-start.5
  372.5 0.0 copy-start.2
  372.5 1.5 reshape.106
  374.0 1.5 fusion.3
  375.4 0.0 copy-done.5
  375.4 0.7 copy.53
  376.1 0.0 copy-done.2
  376.1 0.7 copy.54
  (8 shorter events, 0.1 us)
Async XLA Ops:
  0.6 4.0 %copy-start.1 = (bf16[1,1536,192]{1,2,0:T(8,128)(2,1)S(1)}, bf16[1,1536,192]{1,2,0:T(8,128)(2,1)}, u32[]{:S(2)}) copy-start(bf16[1,1536,192]{1,2,0:T(8,128)(2,1)} %param.16) | copy-start | bytes 1769476
  0.7 4.3 %copy-start.3 = (bf16[1,1536,96]{1,2,0:T(8,128)(2,1)S(1)}, bf16[1,1536,96]{1,2,0:T(8,128)(2,1)}, u32[]{:S(2)}) copy-start(bf16[1,1536,96]{1,2,0:T(8,128)(2,1)} %param.17) | copy-start | bytes 884740
  2.4 2.7 copy-start.4
  5.2 1.8 copy-start.6
  5.2 1.8 copy-start.7
  363.5 3.7 copy-start
  372.4 3.0 copy-start.5
  372.5 3.7 copy-start.2

commit v2 on v1

--- a/solution.py
+++ b/solution.py
@@ -48,14 +48,14 @@
 
 
 def kernel(
-    x_hbm, ct_hbm, wqkv_hbm, wo_hbm, wg_hbm, wu_hbm, wd_hbm, gains_hbm, cos_ref, sin_ref, beg_ref,
+    x_hbm, ct_hbm, wq_hbm, wk_hbm, wv_hbm, wo_hbm, wg_hbm, wu_hbm, wd_hbm, gains_hbm, cos_ref, sin_ref, beg_ref,
     y_out, dx_out, ga_out, gb_out, gn_out,
-    wqkv, wo, wgu, wd, gains, x_v, df,
+    wqkv, wo, wgu, wd, gains, df,
     n1, n2, q2, q2t, kv, o_f, o_b, stat_m, stat_l, gate_s, up_s, u_s, x_own, h_own,
     rsrc, land, da, do2, do2t, dgu, dq, dqkv, dkv_t, dkv_src, dkv_land, acc, s_m,
-    ga, gb, za, zb, xa, xb, fa, fb, yb, dxb, dgain, dg_peer, dg_t, dg_d,
+    ga, gb, da_in, db_in, za, rb, xa, fa, fb, yb, dxb, dgain, dg_peer, dg_t, dg_d,
     w_l, w_s, w_r, ag_s, ag_r, rs_s, rs_r, kv_s, kv_r, dkv_s, dkv_r, out_l, out_s, out_r,
-    gs, gr, zs, zr, xs, xr, cs, cr, es, er, gl, ns, nr,
+    ds_s, ds_r, z_s, z_r, x_s, x_r, a_s, a_r, a_l, f_s, f_r, b_s, b_r, e_s, e_r, e_l, ns, nr,
 ):
     sec = lax.axis_index("section")
     t = lax.axis_index("tensor")
@@ -73,31 +73,33 @@
     lax.fori_loop(1, 8, lambda k, c: greet("tensor", t, k, c), 0)
     lax.fori_loop(1, 8, lambda k, c: greet("dp", d, k, c), 0)
 
-    x_copy = pltpu.make_async_copy(x_hbm.at[sec], x_v, w_l.at[6])
-    ct_copy = pltpu.make_async_copy(ct_hbm.at[sec], df, w_l.at[7])
+    x_copy = pltpu.make_async_copy(x_hbm.at[sec], df, w_l.at[8])
+    ct_copy = pltpu.make_async_copy(ct_hbm.at[sec], df, w_l.at[9])
     own_parts = [
-        (wqkv_hbm, wqkv),
-        (wo_hbm, wo),
-        (wg_hbm, wgu.at[:, :, 0:FF]),
-        (wu_hbm, wgu.at[:, :, FF : 2 * FF]),
-        (wd_hbm, wd),
-        (gains_hbm, gains),
+        (wq_hbm, lambda i: wqkv.at[i, pl.ds(0, 2 * HD)]),
+        (wk_hbm, lambda i: wqkv.at[i, pl.ds(2 * HD, HD)]),
+        (wv_hbm, lambda i: wqkv.at[i, pl.ds(3 * HD, HD)]),
+        (wo_hbm, lambda i: wo.at[i]),
+        (wg_hbm, lambda i: wgu.at[i, :, 0:FF]),
+        (wu_hbm, lambda i: wgu.at[i, :, FF : 2 * FF]),
+        (wd_hbm, lambda i: wd.at[i]),
+        (gains_hbm, lambda i: gains.at[i]),
     ]
-    own_copies = [pltpu.make_async_copy(a, b.at[sec], w_l.at[i]) for i, (a, b) in enumerate(own_parts)]
+    n_parts = len(own_parts)
+    own_copies = [pltpu.make_async_copy(a, b(sec), w_l.at[i]) for i, (a, b) in enumerate(own_parts)]
     x_copy.start()
-    own_copies[5].start()
-    for i in range(5):
+    own_copies[7].start()
+    for i in range(7):
         own_copies[i].start()
-    ct_copy.start()
     pl.semaphore_wait(barrier, 15)
     sent_parts = [
         pltpu.make_async_remote_copy(
-            src_ref=a, dst_ref=b.at[sec], send_sem=w_s.at[i], recv_sem=w_r.at[i],
+            src_ref=a, dst_ref=b(sec), send_sem=w_s.at[i], recv_sem=w_r.at[i],
             device_id={"section": other}, device_id_type=MESH,
         )
         for i, (a, b) in enumerate(own_parts)
     ]
-    for i in (5, 0, 1, 2, 3, 4):
+    for i in (7, 0, 1, 2, 3, 4, 5, 6):
         sent_parts[i].start()
 
     def weight_ready(layer, *which):
@@ -111,7 +113,7 @@
             for i in which:
                 a, b = own_parts[i]
                 pltpu.make_async_remote_copy(
-                    src_ref=a, dst_ref=b.at[other], send_sem=w_s.at[i], recv_sem=w_r.at[i],
+                    src_ref=a, dst_ref=b(other), send_sem=w_s.at[i], recv_sem=w_r.at[i],
                     device_id={"section": other}, device_id_type=MESH,
                 ).wait_recv()
 
@@ -175,29 +177,30 @@
         cols = lax.broadcasted_iota(jnp.int32, (ROWS, ROWS), 1) + j * ROWS
         return (cols <= rows) & (cols >= beg_ref[...][:, 0:1])
 
-    weight_ready(0, 5)
+    weight_ready(0, 7)
     x_copy.wait()
 
     def first_norm(i, c):
         rows = pl.ds(pl.multiple_of(i * OWN, OWN), OWN)
-        v = x_v[rows, :].astype(F32)
+        v = df[rows, :].astype(F32)
         n1[0, rows, :] = (v * factor_of(v) * gains[0, 0:1, :]).astype(BF16)
         return c
 
     lax.fori_loop(0, ROWS // OWN, first_norm, 0)
-    x_own[0] = x_v[my_rows, :].astype(F32)
+    x_own[0] = df[my_rows, :].astype(F32)
+    ct_copy.start()
 
     def forward_layer(layer, c):
         @pl.when(layer == 1)
         def _():
-            weight_ready(1, 5)
+            weight_ready(1, 7)
             v = x_own[1]
             n1[1, my_rows, :] = (v * factor_of(v) * gains[1, 0:1, :]).astype(BF16)
             ag_start(n1.at[1], 0)
             ag_wait(n1.at[1], 0)
 
-        weight_ready(layer, 0)
-        raw = dot(n1[layer], wqkv[layer])
+        weight_ready(layer, 0, 1, 2)
+        raw = dot_nt(n1[layer], wqkv[layer])
         c0, c1, c2 = raw[:, 0:128], raw[:, 128:256], raw[:, 256:384]
         lane = lanes_of(c0)
         q1 = jnp.where(lane < 32, pltpu.roll(c0, 32, 1), pltpu.roll(c1, 32, 1))
@@ -259,7 +262,7 @@
             kv_copy(d, k).wait_send()
             return c
 
-        weight_ready(layer, 1)
+        weight_ready(layer, 3)
 
         def out_part(n, c):
             cols = pl.ds(pl.multiple_of(n * 512, 512), 512)
@@ -276,7 +279,7 @@
         n2[layer, my_rows, :] = (v * factor_of(v) * gains[layer, 8:9, :]).astype(BF16)
         ag_start(n2.at[layer], 1)
         ag_wait(n2.at[layer], 1)
-        weight_ready(layer, 2, 3)
+        weight_ready(layer, 4, 5)
 
         def units(n, c):
             cols = pl.ds(pl.multiple_of(n * 256, 256), 256)
@@ -289,7 +292,7 @@
             return c
 
         lax.fori_loop(0, 2, units, 0)
-        weight_ready(layer, 4)
+        weight_ready(layer, 6)
 
         def down_part(n, c):
             cols = pl.ds(pl.multiple_of(n * 512, 512), 512)
@@ -333,113 +336,222 @@
 
     ct_copy.wait()
 
-    def to_owner(layer, buf, i):
+    before, after = (z + 3) % 4, (z + 1) % 4
+    far = (z + 2) % 4
+    upper, lower = pl.ds(0, 288), pl.ds(288, 288)
+
+    def dp_at(zz, xx):
+        return zz * 2 + xx
+
+    def swap_cores(layer, i):
+        buf, landing = ((ga, da_in), (gb, db_in))[i]
         return pltpu.make_async_remote_copy(
-            src_ref=buf.at[sec * (1 - layer)], dst_ref=buf.at[1], send_sem=gs.at[i], recv_sem=gr.at[i],
+            src_ref=buf.at[layer, other], dst_ref=landing.at[layer], send_sem=ds_s.at[i, layer], recv_sem=ds_r.at[i, layer],
             device_id={"section": other}, device_id_type=MESH,
         )
 
-    def z_copy(buf, landing, i, to, sender):
-        slot = (sender - to + 3) % 4
+    def add_rows(target, index, rows, sources, count):
+        first, size = rows
+
+        def add(n, carry):
+            here = pl.ds(pl.multiple_of(first + n * count, 16), count)
+            total = target[(*index, here)].astype(F32)
+            for ref, place, start in sources:
+                total += ref[(*place, pl.ds(pl.multiple_of(start + n * count, 16), count))].astype(F32)
+            target[(*index, here)] = total.astype(BF16)
+            return carry
+
+        lax.fori_loop(0, size // count, add, 0)
+
+    def z_piece(layer, piece, chunk, rows, to):
         return pltpu.make_async_remote_copy(
-            src_ref=buf.at[0, to], dst_ref=landing.at[slot], send_sem=zs.at[i, to], recv_sem=zr.at[i, slot],
-            device_id={"dp": to * 2 + xh}, device_id_type=MESH,
-        )
-
-    def x_copy_of(buf, landing, i):
-        half = landing.shape[0]
+            src_ref=ga.at[layer, sec, chunk, rows], dst_ref=za.at[layer, piece], send_sem=z_s.at[layer, piece],
+            recv_sem=z_r.at[layer, piece], device_id={"dp": dp_at(to, xh)}, device_id_type=MESH,
+        )
+
+    def ffn_1(layer):
+        swap_cores(layer, 0).wait_recv()
+        for chunk, sends in (
+            (far, ((0, upper, after), (1, lower, before))),
+            (after, ((2, lower, after),)),
+            (before, ((3, upper, before),)),
+            (z, ()),
+        ):
+            add_rows(ga, (layer, sec, chunk), (0, 576), [(da_in, (layer, chunk), 0)], 96)
+            for piece, rows, to in sends:
+                z_piece(layer, piece, chunk, rows, to).start()
+
+    def ffn_2(layer):
+        z_piece(layer, 0, far, upper, after).wait_recv()
+        add_rows(ga, (layer, sec, after), (0, 288), [(za, (layer, 0), 0)], 96)
+        z_piece(layer, 4, after, upper, after).start()
+        z_piece(layer, 1, far, lower, before).wait_recv()
+        add_rows(ga, (layer, sec, before), (288, 288), [(za, (layer, 1), 0)], 96)
+        z_piece(layer, 5, before, lower, before).start()
+
+    def x_over(layer):
         return pltpu.make_async_remote_copy(
-            src_ref=buf.at[0, z, pl.ds((1 - xh) * half, half)], dst_ref=landing, send_sem=xs.at[i], recv_sem=xr.at[i],
-            device_id={"dp": z * 2 + 1 - xh}, device_id_type=MESH,
-        )
-
-    def x_back(done, i, which):
-        half = done.shape[0] // 2
-        part = done.at[pl.ds(which * half, half)]
+            src_ref=ga.at[layer, sec, z, pl.ds((1 - xh) * 288, 288)], dst_ref=xa.at[layer], send_sem=x_s.at[0, layer],
+            recv_sem=x_r.at[0, layer], device_id={"dp": dp_at(z, 1 - xh)}, device_id_type=MESH,
+        )
+
+    def x_back(layer, which):
+        part = fa.at[layer, pl.ds(which * 288, 288)]
         return pltpu.make_async_remote_copy(
-            src_ref=part, dst_ref=part, send_sem=cs.at[i], recv_sem=cr.at[i],
-            device_id={"dp": z * 2 + 1 - xh}, device_id_type=MESH,
-        )
-
-    def z_back(done, out, i, to, sender):
+            src_ref=part, dst_ref=part, send_sem=x_s.at[1, layer], recv_sem=x_r.at[1, layer],
+            device_id={"dp": dp_at(z, 1 - xh)}, device_id_type=MESH,
+        )
+
+    def ffn_3(layer):
+        for piece in (2, 3, 4, 5):
+            z_piece(layer, piece, z, upper, after).wait_recv()
+        add_rows(ga, (layer, sec, z), (0, 288), [(za, (layer, 3), 0), (za, (layer, 4), 0)], 96)
+        add_rows(ga, (layer, sec, z), (288, 288), [(za, (layer, 2), 0), (za, (layer, 5), 0)], 96)
+        x_over(layer).start()
+
+    def ffn_4(layer):
+        x_over(layer).wait_recv()
+
+        def add(n, carry):
+            here = pl.ds(pl.multiple_of(n * 96, 16), 96)
+            there = pl.ds(pl.multiple_of(xh * 288 + n * 96, 16), 96)
+            fa[layer, there, :] = (ga[layer, sec, z, there, :].astype(F32) + xa[layer, here, :].astype(F32)).astype(BF16)
+            return carry
+
+        lax.fori_loop(0, 3, add, 0)
+        x_back(layer, xh).start()
+
+    def spread(layer, half, chunk, to, i):
         return pltpu.make_async_remote_copy(
-            src_ref=done, dst_ref=out.at[sender], send_sem=es.at[i, to], recv_sem=er.at[i, sender],
-            device_id={"dp": to * 2 + xh}, device_id_type=MESH,
-        )
-
-    def sum_step_1(buf, landing, i):
-        to_owner(0, buf, i).wait_recv()
-        rows = buf.shape[2] // 4
-        for c in (2, 1, 3, 0):
-            chunk = (z + c) % 4
-
-            def add(n, carry):
-                part = pl.ds(pl.multiple_of(n * rows, rows), rows)
-                buf[0, chunk, part, :] = (buf[0, chunk, part, :].astype(F32) + buf[1, chunk, part, :].astype(F32)).astype(BF16)
-                return carry
-
-            lax.fori_loop(0, 4, add, 0)
-            if c:
-                z_copy(buf, landing, i, chunk, z).start()
-
-    def sum_step_2(buf, landing, over, i):
-        for c in range(1, 4):
-            z_copy(buf, landing, i, z, (z + c) % 4).wait_recv()
-        rows = buf.shape[2] // 4
-
-        def add(n, carry):
-            part = pl.ds(pl.multiple_of(n * rows, rows), rows)
-            total = buf[0, z, part, :].astype(F32)
-            for s in range(3):
-                total += landing[s, part, :].astype(F32)
-            buf[0, z, part, :] = total.astype(BF16)
-            return carry
-
-        lax.fori_loop(0, 4, add, 0)
-        x_copy_of(buf, over, i).start()
-
-    def sum_step_3(buf, over, done, i):
-        x_copy_of(buf, over, i).wait_recv()
-        half = over.shape[0]
-        rows = half // 2
-
-        def add(n, carry):
-            part = pl.ds(pl.multiple_of(xh * half + n * rows, 16), rows)
-            here = pl.ds(pl.multiple_of(n * rows, 16), rows)
-            done[part, :] = (buf[0, z, part, :].astype(F32) + over[here, :].astype(F32)).astype(BF16)
-            return carry
-
-        lax.fori_loop(0, 2, add, 0)
-        x_back(done, i, xh).start()
-
-    def sum_step_4(done, out, i):
-        x_back(done, i, 1 - xh).wait_recv()
-        for c in (2, 1, 3):
-            z_back(done, out, i, (z + c) % 4, z).start()
-        pltpu.make_async_copy(done, out.at[z], gl.at[i]).start()
-
-    def sum_step_5(buf, landing, over, done, out, i):
-        x_copy_of(buf, over, i).wait_send()
-        x_back(done, i, xh).wait_send()
-        pltpu.make_async_copy(done, out.at[z], gl.at[i]).wait()
-        for c in range(1, 4):
-            peer = (z + c) % 4
-            z_copy(buf, landing, i, peer, z).wait_send()
-            z_back(done, out, i, peer, z).wait_send()
-            z_back(done, out, i, z, peer).wait_recv()
+            src_ref=fa.at[layer], dst_ref=ga_out.at[half, chunk], send_sem=a_s.at[layer, i], recv_sem=a_r.at[half, chunk],
+            device_id={"section": layer, "dp": dp_at(to, xh)}, device_id_type=MESH,
+        )
+
+    def keep(layer):
+        return pltpu.make_async_copy(fa.at[layer], ga_out.at[sec, z], a_l)
+
+    def ffn_5(layer):
+        x_back(layer, 1 - xh).wait_recv()
+        spread(layer, sec, z, after, 0).start()
+        spread(layer, sec, z, before, 1).start()
+
+        @pl.when(layer == sec)
+        def _():
+            keep(layer).start()
+
+        @pl.when(layer != sec)
+        def _():
+            spread(layer, sec, z, z, 2).start()
+
+    def pass_on(half, i, chunk, rows, to):
+        part = ga_out.at[half, chunk, rows]
+        return pltpu.make_async_remote_copy(
+            src_ref=part, dst_ref=part, send_sem=f_s.at[half, i], recv_sem=f_r.at[half, i],
+            device_id={"dp": dp_at(to, xh)}, device_id_type=MESH,
+        )
+
+    def ffn_6():
+        for half in range(2):
+            spread(sec, half, before, z, 0).wait_recv()
+            pass_on(half, 0, before, upper, after).start()
+            spread(sec, half, after, z, 0).wait_recv()
+            pass_on(half, 1, after, lower, before).start()
+
+    def ffn_7():
+        keep(sec).wait()
+        spread(sec, other, z, z, 2).wait_recv()
+        for half in range(2):
+            pass_on(half, 0, far, upper, z).wait_recv()
+            pass_on(half, 1, far, lower, z).wait_recv()
+            pass_on(half, 0, before, upper, after).wait_send()
+            pass_on(half, 1, after, lower, before).wait_send()
+        spread(other, sec, z, z, 2).wait_send()
+        for layer in range(2):
+            swap_cores(layer, 0).wait_send()
+            for piece in range(6):
+                z_piece(layer, piece, z, upper, after).wait_send()
+            x_over(layer).wait_send()
+            x_back(layer, xh).wait_send()
+            spread(layer, sec, z, after, 0).wait_send()
+            spread(layer, sec, z, before, 1).wait_send()
+
+    def b_piece(layer, to, sender):
+        return pltpu.make_async_remote_copy(
+            src_ref=gb.at[layer, sec, to // 2, pl.ds((to % 2) * 144, 144)], dst_ref=rb.at[layer, sender],
+            send_sem=b_s.at[layer, to], recv_sem=b_r.at[layer, sender], device_id={"dp": to}, device_id_type=MESH,
+        )
+
+    def b_spread(layer, half, to, sender):
+        return pltpu.make_async_remote_copy(
+            src_ref=fb.at[layer], dst_ref=gb_out.at[half, sender // 2, pl.ds((sender % 2) * 144, 144)],
+            send_sem=e_s.at[layer, to], recv_sem=e_r.at[half, sender], device_id={"section": layer, "dp": to},
+            device_id_type=MESH,
+        )
+
+    def b_keep(layer):
+        return pltpu.make_async_copy(fb.at[layer], gb_out.at[sec, z, pl.ds(xh * 144, 144)], e_l)
+
+    def attn_1(layer):
+        swap_cores(layer, 1).wait_recv()
+        for chunk in (far, after, before, z):
+            add_rows(gb, (layer, sec, chunk), (0, 288), [(db_in, (layer, chunk), 0)], 144)
+
+        def send(k, c):
+            b_piece(layer, (d + k) % 8, d).start()
+            return c
+
+        lax.fori_loop(1, 8, send, 0)
+
+    def attn_2(layer):
+        def take(k, total):
+            p = (d + k) % 8
+            b_piece(layer, d, p).wait_recv()
+            return total + rb[layer, p].astype(F32)
+
+        mine = gb[layer, sec, z, pl.ds(pl.multiple_of(xh * 144, 16), 144), :].astype(F32)
+        fb[layer] = lax.fori_loop(1, 8, take, mine).astype(BF16)
+
+        def send(k, c):
+            b_spread(layer, sec, (d + k) % 8, d).start()
+            return c
+
+        lax.fori_loop(1, 8, send, 0)
+
+        @pl.when(layer == sec)
+        def _():
+            b_keep(layer).start()
+
+        @pl.when(layer != sec)
+        def _():
+            b_spread(layer, sec, d, d).start()
+
+    def attn_3():
+        b_keep(sec).wait()
+        b_spread(sec, other, d, d).wait_recv()
+        b_spread(other, sec, d, d).wait_send()
+
+        def finish(k, c):
+            p = (d + k) % 8
+            b_spread(sec, 0, d, p).wait_recv()
+            b_spread(sec, 1, d, p).wait_recv()
+            for layer in range(2):
+                b_piece(layer, p, d).wait_send()
+                b_spread(layer, sec, p, d).wait_send()
+            return c
+
+        lax.fori_loop(1, 8, finish, 0)
+        for layer in range(2):
+            swap_cores(layer, 1).wait_send()
 
     def backward_layer(step, c):
         layer = 1 - step
-        mine = sec * (1 - layer)
 
         @pl.when(layer == 0)
         def _():
             ag_start(df, 2)
 
-            @pl.when(sec == 1)
-            def _():
-                sum_step_1(ga, za, 0)
-
+            attn_1(1)
+            ffn_4(1)
             ag_wait(df, 2)
 
         dy = df[my_rows, :].astype(F32)
@@ -465,31 +577,26 @@
         lax.fori_loop(0, 6, normed_part, 0)
         rs_start(0)
 
-        @pl.when((step == 1) & (sec == 0))
-        def _():
-            to_owner(1, ga, 0).wait_send()
-            to_owner(1, gb, 1).wait_send()
-
         def unit_weights(n, c):
             cols = pl.ds(pl.multiple_of(n * 384, 384), 384)
             got = dot_tn(n2[layer, :, cols], dgu[...]).astype(BF16)
-            ga[mine, n, pl.ds(0, 384), :] = got[:, 0:FF]
-            ga[mine, n, pl.ds(384, 384), :] = got[:, FF : 2 * FF]
+            for h in range(2):
+                ga[layer, h, n, pl.ds(0, 192), :] = got[192 * h : 192 * h + 192, 0:FF]
+                ga[layer, h, n, pl.ds(192, 192), :] = got[192 * h : 192 * h + 192, FF : 2 * FF]
             cols = pl.ds(pl.multiple_of(n * 128, 128), 128)
             got = dot_tn(u_s[layer, :, cols], df[...]).astype(BF16)
-            for i in range(3):
-                ga[mine, n, pl.ds(768 + 128 * i, 128), :] = got[:, 512 * i : 512 * i + 512]
+            for h in range(2):
+                for i in range(3):
+                    ga[layer, h, n, pl.ds(384 + 64 * i, 64), :] = got[64 * h : 64 * h + 64, 512 * i : 512 * i + 512]
             return c
 
         lax.fori_loop(0, 4, unit_weights, 0)
-
-        @pl.when(layer != sec)
-        def _():
-            to_owner(layer, ga, 0).start()
-
-        @pl.when((step == 1) & (sec == 1))
-        def _():
-            sum_step_1(gb, zb, 1)
+        swap_cores(layer, 0).start()
+
+        @pl.when(step == 1)
+        def _():
+            ffn_5(1)
+            attn_2(1)
 
         dn = rs_sum(0)
         h = h_own[layer]
@@ -500,14 +607,11 @@
         dxb[layer] = dh
         da[my_rows, :] = dh.astype(BF16)
         ag_start(da, 3)
+        ffn_1(layer)
 
         @pl.when((step == 1) & (sec == 1))
         def _():
-            sum_step_2(ga, za, xa, 0)
-
-        @pl.when((step == 1) & (sec == 0))
-        def _():
-            sum_step_1(ga, za, 0)
+            ffn_6()
 
         ag_wait(da, 3)
         for h in range(2):
@@ -559,20 +663,13 @@
             cols = pl.ds(pl.multiple_of(n * 384, 384), 384)
             for h in range(2):
                 got = dot_tn(o_b[layer, pl.ds(h * ROWS, ROWS), :], da[:, cols])
-                gb[mine, n, pl.ds(h * HD, HD), :] = got.astype(BF16)
+                gb[layer, 0, n, pl.ds(h * HD, HD), :] = got.astype(BF16)
             return c
 
         lax.fori_loop(0, 4, out_weights, 0)
         lax.fori_loop(0, d, dkv_sent, 0)
 
-        @pl.when((step == 1) & (sec == 1))
-        def _():
-            sum_step_2(gb, zb, xb, 1)
-            sum_step_3(ga, xa, fa, 0)
-
-        @pl.when((step == 1) & (sec == 0))
-        def _():
-            sum_step_2(ga, za, xa, 0)
+        ffn_2(layer)
 
         def dkv_sum(k, total):
             dkv_copy(d, k).wait_recv()
@@ -598,7 +695,7 @@
 
         def input_part(n, c):
             cols = pl.ds(pl.multiple_of(n * 256, 256), 256)
-            rsrc[1, :, cols] = dot_nt(dqkv[...], wqkv[layer, cols, :]).astype(BF16)
+            rsrc[1, :, cols] = dot(dqkv[...], wqkv[layer, :, cols]).astype(BF16)
             return c
 
         lax.fori_loop(0, 6, input_part, 0)
@@ -606,24 +703,14 @@
 
         def qkv_weights(n, c):
             cols = pl.ds(pl.multiple_of(n * 384, 384), 384)
-            gb[mine, n, pl.ds(2 * HD, 384), :] = dot_tn(n1[layer, :, cols], dqkv[...]).astype(BF16)
+            got = dot_tn(dqkv[...], n1[layer, :, cols]).astype(BF16)
+            gb[layer, 0, n, pl.ds(2 * HD, HD), :] = got[0:HD]
+            gb[layer, 1, n] = got[HD : 4 * HD]
             return c
 
         lax.fori_loop(0, 4, qkv_weights, 0)
-
-        @pl.when(layer != sec)
-        def _():
-            to_owner(layer, gb, 1).start()
-
-        @pl.when((step == 1) & (sec == 1))
-        def _():
-            sum_step_3(gb, xb, fb, 1)
-            sum_step_4(fa, ga_out, 0)
-
-        @pl.when((step == 1) & (sec == 0))
-        def _():
-            sum_step_3(ga, xa, fa, 0)
-
+        swap_cores(layer, 1).start()
+        ffn_3(layer)
         dn = rs_sum(1)
         v = x_own[layer]
         r = factor_of(v)
@@ -643,15 +730,8 @@
         device_id={"section": other}, device_id_type=MESH,
     )
     mate.start()
-
-    @pl.when(sec == 0)
-    def _():
-        sum_step_4(fa, ga_out, 0)
-        sum_step_1(gb, zb, 1)
-
-    @pl.when(sec == 1)
-    def _():
-        sum_step_4(fb, gb_out, 1)
+    ffn_4(0)
+    attn_1(0)
 
     def gain_copy(axis, i, buf, me, to, sender):
         return pltpu.make_async_remote_copy(
@@ -681,29 +761,20 @@
     mate.wait_recv()
     mate.wait_send()
     dg_t[t] = dgain[sec] + dg_peer[...]
+    ffn_5(0)
     dg_d[d] = gain_round("tensor", 1, dg_t, t)
+    attn_2(0)
 
     @pl.when(sec == 0)
     def _():
-        sum_step_2(gb, zb, xb, 1)
+        ffn_6()
 
     gn_out[...] = gain_round("dp", 2, dg_d, d)
-
-    @pl.when(sec == 0)
-    def _():
-        sum_step_3(gb, xb, fb, 1)
-        sum_step_4(fb, gb_out, 1)
-
-    @pl.when(sec == 1)
-    def _():
-        to_owner(0, ga, 0).wait_send()
-        to_owner(0, gb, 1).wait_send()
-
-    sum_step_5(ga, za, xa, fa, ga_out, 0)
-    sum_step_5(gb, zb, xb, fb, gb_out, 1)
+    attn_3()
+    ffn_7()
     row_out_wait(yb, y_out, 0)
     row_out_wait(dxb, dx_out, 1)
-    for i in range(6):
+    for i in range(n_parts):
         sent_parts[i].wait_send()
 
 
@@ -712,8 +783,8 @@
     vmem = pl.BlockSpec(memory_space=pltpu.VMEM)
     dma = pltpu.SemaphoreType.DMA
     scratch = [
-        pltpu.VMEM((2, D, 384), BF16), pltpu.VMEM((2, 192, D), BF16), pltpu.VMEM((2, D, 2 * FF), BF16),
-        pltpu.VMEM((2, FF, D), BF16), pltpu.VMEM((2, 16, D), F32), pltpu.VMEM((ROWS, D), BF16), pltpu.VMEM((ROWS, D), BF16),
+        pltpu.VMEM((2, 384, D), BF16), pltpu.VMEM((2, 192, D), BF16), pltpu.VMEM((2, D, 2 * FF), BF16),
+        pltpu.VMEM((2, FF, D), BF16), pltpu.VMEM((2, 16, D), F32), pltpu.VMEM((ROWS, D), BF16),
         pltpu.VMEM((2, ROWS, D), BF16), pltpu.VMEM((2, ROWS, D), BF16), pltpu.VMEM((2, 2 * ROWS, HD), BF16),
         pltpu.VMEM((2, HD, 2 * ROWS), BF16), pltpu.VMEM((2, 8, 2 * HD, ROWS), BF16), pltpu.VMEM((2, 2 * ROWS, HD), F32),
         pltpu.VMEM((2, 2 * ROWS, HD), BF16), pltpu.VMEM((2, 2 * ROWS, 1), F32), pltpu.VMEM((2, 2 * ROWS, 1), F32),
@@ -724,26 +795,26 @@
         pltpu.VMEM((2 * ROWS, 128), F32), pltpu.VMEM((ROWS, 384), BF16), pltpu.VMEM((2, 128, ROWS), F32),
         pltpu.VMEM((8, 2 * HD, ROWS), BF16), pltpu.VMEM((2, 8, 2 * HD, ROWS), BF16), pltpu.VMEM((2 * ROWS, HD), F32),
         pltpu.VMEM((2 * ROWS, 1), F32),
-        pltpu.VMEM((2, 4, 1152, 512), BF16), pltpu.VMEM((2, 4, 576, 384), BF16), pltpu.VMEM((3, 1152, 512), BF16),
-        pltpu.VMEM((3, 576, 384), BF16), pltpu.VMEM((576, 512), BF16), pltpu.VMEM((288, 384), BF16),
-        pltpu.VMEM((1152, 512), BF16), pltpu.VMEM((576, 384), BF16),
+        pltpu.VMEM((2, 2, 4, 576, 512), BF16), pltpu.VMEM((2, 2, 4, 288, 384), BF16), pltpu.VMEM((2, 4, 576, 512), BF16),
+        pltpu.VMEM((2, 4, 288, 384), BF16), pltpu.VMEM((2, 6, 288, 512), BF16), pltpu.VMEM((2, 8, 144, 384), BF16),
+        pltpu.VMEM((2, 288, 512), BF16), pltpu.VMEM((2, 576, 512), BF16), pltpu.VMEM((2, 144, 384), BF16),
         pltpu.VMEM((2, OWN, D), BF16), pltpu.VMEM((2, OWN, D), F32), pltpu.VMEM((2, 8, D), F32), pltpu.VMEM((8, D), F32),
         pltpu.VMEM((8, 8, D), F32), pltpu.VMEM((8, 8, D), F32),
-        dma((8,)), dma((6,)), dma((6,)), dma((4, 8)), dma((4, 8)), dma((2, 8)), dma((2, 8)), dma((8,)), dma((8, 2)),
+        dma((10,)), dma((8,)), dma((8,)), dma((4, 8)), dma((4, 8)), dma((2, 8)), dma((2, 8)), dma((8,)), dma((8, 2)),
         dma((8,)), dma((2, 8)), dma((2,)), dma((2,)), dma((2,)),
-        dma((2,)), dma((2,)), dma((2, 4)), dma((2, 3)), dma((2,)), dma((2,)), dma((2,)), dma((2,)), dma((2, 4)),
-        dma((2, 4)), dma((2,)), dma((3, 8)), dma((3, 8)),
+        dma((2, 2)), dma((2, 2)), dma((2, 6)), dma((2, 6)), dma((2, 2)), dma((2, 2)), dma((2, 3)), dma((2, 4)), dma,
+        dma((2, 2)), dma((2, 2)), dma((2, 8)), dma((2, 8)), dma((2, 8)), dma((2, 8)), dma, dma((3, 8)), dma((3, 8)),
     ]
     return pl.pallas_call(
         kernel,
         out_shape=(
             jax.ShapeDtypeStruct((2, OWN, D), BF16),
             jax.ShapeDtypeStruct((2, OWN, D), F32),
-            jax.ShapeDtypeStruct((4, 1152, 512), BF16),
-            jax.ShapeDtypeStruct((4, 576, 384), BF16),
+            jax.ShapeDtypeStruct((2, 4, 576, 512), BF16),
+            jax.ShapeDtypeStruct((2, 4, 288, 384), BF16),
             jax.ShapeDtypeStruct((8, D), F32),
         ),
-        in_specs=[hbm] * 8 + [vmem] * 3,
+        in_specs=[hbm] * 10 + [vmem] * 3,
         out_specs=(hbm, hbm, hbm, hbm, vmem),
         scratch_shapes=scratch,
         compiler_params=pltpu.CompilerParams(
@@ -753,8 +824,36 @@
     )(*args)
 
 
+def widen(ga_ref, gb_ref, gate_ref, up_ref, down_ref, out_ref, query_ref, key_ref, value_ref):
+    for h in range(2):
+        rows = pl.ds(192 * h, 192)
+        gate_ref[rows, :] = ga_ref[h, 0, 0:192, :].astype(F32)
+        up_ref[rows, :] = ga_ref[h, 0, 192:384, :].astype(F32)
+        for i in range(3):
+            down_ref[pl.ds(64 * h, 64), pl.ds(512 * i, 512)] = ga_ref[h, 0, 384 + 64 * i : 448 + 64 * i, :].astype(F32)
+    out_ref[...] = gb_ref[0, 0, 0:192, :].astype(F32)
+    query_ref[0:HD, :] = gb_ref[0, 0, 192:288, :].astype(F32)
+    query_ref[HD : 2 * HD, :] = gb_ref[1, 0, 0:HD, :].astype(F32)
+    key_ref[...] = gb_ref[1, 0, HD : 2 * HD, :].astype(F32)
+    value_ref[...] = gb_ref[1, 0, 2 * HD : 3 * HD, :].astype(F32)
+
+
+def widened(ga, gb):
+    shapes = [(D, FF), (D, FF), (FF, D), (192, D), (192, D), (HD, D), (HD, D)]
+    by_row = [pl.BlockSpec((384, FF), lambda c: (c, 0)), pl.BlockSpec((384, FF), lambda c: (c, 0)), pl.BlockSpec((128, D), lambda c: (c, 0))]
+    by_column = [pl.BlockSpec((rows, 384), lambda c: (0, c)) for rows in (192, 192, HD, HD)]
+    return pl.pallas_call(
+        widen,
+        grid=(4,),
+        out_shape=tuple(jax.ShapeDtypeStruct(shape, F32) for shape in shapes),
+        in_specs=[pl.BlockSpec((2, 1, 576, 512), lambda c: (0, c, 0, 0)), pl.BlockSpec((2, 1, 288, 384), lambda c: (0, c, 0, 0))],
+        out_specs=tuple(by_row + by_column),
+        compiler_params=pltpu.CompilerParams(vmem_limit_bytes=40 * 1024 * 1024),
+        name="widen",
+    )(ga, gb)
+
+
 def on_device(inputs, cotangent, doc_lengths, norm_one, query_w, key_w, value_w, out_w, norm_two, gate_w, up_w, down_w):
-    wqkv = jnp.concatenate([query_w[0], key_w[0], value_w[0]], axis=1)
     gains = jnp.concatenate([jnp.broadcast_to(norm_one, (8, D)), jnp.broadcast_to(norm_two, (8, D))]).astype(F32)
     lengths = lax.dynamic_index_in_dim(doc_lengths, lax.axis_index("section"), 0, keepdims=False)
     starts = jnp.cumsum(lengths) - lengths
@@ -768,17 +867,12 @@
     sine = jnp.concatenate([-sine, sine, rest], axis=1)
     begins = jnp.broadcast_to(begins[:, None], (ROWS, 128))
     y, dx, ga, gb, gn = step_call(
-        inputs, cotangent, wqkv, out_w[0], gate_w[0], up_w[0], down_w[0], gains, cosine, sine, begins
+        inputs, cotangent, query_w[0].T, key_w[0].T, value_w[0].T, out_w[0], gate_w[0], up_w[0], down_w[0], gains, cosine, sine, begins
     )
-    gate = ga[:, 0:384].reshape(D, FF).astype(F32)
-    up = ga[:, 384:768].reshape(D, FF).astype(F32)
-    down = ga[:, 768:].reshape(4, 3, 128, 512).transpose(0, 2, 1, 3).reshape(FF, D).astype(F32)
-    out = gb[:, 0:192].transpose(1, 0, 2).reshape(192, D).astype(F32)
-    qkv = gb[:, 192:].reshape(D, 384)
-    grads = (
-        gn[0:1], qkv[:, 0:192].astype(F32), qkv[:, 192:288].astype(F32), qkv[:, 288:384].astype(F32), out, gn[1:2], gate, up, down,
+    gate, up, down, out, query, key, value = widened(ga, gb)
+    return (
+        y[None], dx[None], gn[0:1], query.T[None], key.T[None], value.T[None], out[None], gn[1:2], gate[None], up[None], down[None],
     )
-    return (y[None], dx[None]) + tuple(g if g.shape[0] == 1 else g[None] for g in grads)
 
 
 def solution(mesh):

time: 381 us -> 337 us (0.88)
  Pallas kernels: 343 us -> 320 us
  local copies, waits for them, and re-layouts: 21.5 us -> 8.26 us
  other arithmetic: 11.6 us -> 4.47 us
    pallas_call x1, Pallas kernels: 343 us -> 315 us  [step_call(): pl.pallas_call(kernel, out_shape=(jax.ShapeDtypeStruct((2, OWN, D), BF16)...]
    convert_element_type x4 -> x0, local copies, waits for them, and re-layouts: 7.75 us -> none  [the longest x2 5.5 us: on_device(): ga[:, 768:].reshape(4, 3, 128, 512).transpose(0, 2, 1, 3).reshape(FF, D)]
    pallas_call x0 -> x1, Pallas kernels: none -> 5.07 us  [widened(): pl.pallas_call(widen, grid=(4,), out_shape=tuple((jax.ShapeDtypeStruct(sh...]
    convert_element_type x2 -> x0, other arithmetic: 4.73 us -> none  [the longest x1 3.59 us: on_device(): up = ga[:, 384:768].reshape(D, FF).astype(F32)]
    slice x4 -> x0, local copies, waits for them, and re-layouts: 4.26 us -> none  [the longest x1 3.81 us: on_device(): ga[:, 768:].reshape(4, 3, 128, 512).transpose(0, 2, 1, 3).reshape(FF, D)]
where the time goes in v2:
time: 337 us; the launch traced here: 334 us
  Pallas kernels  320 us (95%)
  local copies, waits for them, and re-layouts  8.26 us (2%)
  other arithmetic  4.47 us (1%)
    pallas_call x1, Pallas kernels, step_call(): pl.pallas_call(kernel, out_shape=(jax.ShapeDtypeStruct((2, OWN, D), BF16)...  315 us

profile of v2, /device:TPU:24, one launch (start us, length us, event | category | flops | bytes accessed | tf_op | source)
XLA Modules:
  0.0 333.6 jit_solution(10839646727357415118)
XLA Ops:
  0.6 0.7 constant_dynamic-slice_fusion
  1.3 0.2 reduce-window_clone.1
  1.5 0.7 subtract_bitcast_fusion
  2.2 0.1 pad.5.clone
  2.3 0.1 select_reduce_fusion
  2.4 0.7 reduce
  3.2 0.7 reduce.1
  3.9 0.6 maximum_convert_fusion.gains_hbm
  4.6 0.8 broadcast_in_dim.71.beg_ref
  5.3 0.5 fusion
  5.8 0.8 maximum_maximum_fusion.1
  6.7 315.1 %train_step.1 = (bf16[2,32,1536]{2,1,0:T(8,128)(2,1)}, f32[2,32,1536]{2,1,0:T(8,128)}, bf16[2,4,576,512]{3,2,1,0:T(8,128)(2,1)}, bf16[2,4,288,384]{3,2,1,0:T(8,128)(2,1)}, f32[8,1536]{1,0:T(8,128)}) custom-call(bf16[2,256,1536]{2,1,0:T(8,128)(2,1)} %x_hbm.1, bf16[2,256,1536]{2,1,0:T(8,128)(2,1)} %ct_hbm.1, bf16[192,1536]{1,0:T(8,128)(2,1)} %bitcast.33, ...), custom_call_target="tpu_custom_call" | custom-call | tf_op jit(solution)/shard_map/train_step/pallas_call | solution.py:808
  321.8 1.5 fusion.1
  323.3 0.0 copy-start
  323.3 2.3 copy-done
  325.6 0.0 copy-start.1
  325.6 1.5 copy-done.1
  327.1 0.0 copy-start.3
  327.1 0.0 copy-start.2
  327.1 5.1 %widen.1 = (f32[1536,512]{1,0:T(8,128)}, f32[1536,512]{1,0:T(8,128)}, f32[512,1536]{1,0:T(8,128)}, f32[192,1536]{1,0:T(8,128)}, f32[192,1536]{1,0:T(8,128)}, /*index=5*/f32[96,1536]{1,0:T(8,128)}, f32[96,1536]{1,0:T(8,128)}) custom-call(bf16[2,4,576,512]{3,2,1,0:T(8,128)(2,1)S(1)} %copy-done, bf16[2,4,288,384]{3,2,1,0:T(8,128)(2,1)S(1)} %copy-done.1), custom_call_target="tpu_custom_call" | custom-call | tf_op jit(solution)/shard_map/widen/pallas_call | solution.py:845
  332.1 0.0 copy-done.3
  332.1 0.7 copy.25
  332.8 0.0 copy-done.2
  332.8 0.7 copy.26
  (6 shorter events, 0.0 us)
Async XLA Ops:
  323.3 2.3 copy-start
  325.6 1.5 copy-start.1
  327.1 5.1 %copy-start.3 = (bf16[2,32,1536]{2,1,0:T(8,128)(2,1)S(1)}, bf16[2,32,1536]{2,1,0:T(8,128)(2,1)}, u32[]{:S(2)}) copy-start(bf16[2,32,1536]{2,1,0:T(8,128)(2,1)} %get-tuple-element.23) | copy-start | bytes 589828
  327.1 5.8 %copy-start.2 = (f32[2,32,1536]{2,1,0:T(8,128)S(1)}, f32[2,32,1536]{2,1,0:T(8,128)}, u32[]{:S(2)}) copy-start(f32[2,32,1536]{2,1,0:T(8,128)} %get-tuple-element.24) | copy-start | bytes 1179652

commit v3 on v2

--- a/solution.py
+++ b/solution.py
@@ -17,6 +17,8 @@
 FF = 512
 ROWS = 256
 OWN = 32
+HROWS = 128
+HOWN = 16
 SCALE = 1.0 / math.sqrt(HD)
 EPS = 1e-05
 ROPE = 100000.0
@@ -73,8 +75,20 @@
     lax.fori_loop(1, 8, lambda k, c: greet("tensor", t, k, c), 0)
     lax.fori_loop(1, 8, lambda k, c: greet("dp", d, k, c), 0)
 
-    x_copy = pltpu.make_async_copy(x_hbm.at[sec], df, w_l.at[8])
-    ct_copy = pltpu.make_async_copy(ct_hbm.at[sec], df, w_l.at[9])
+    def load_rows(source, sem):
+        def body(i, c):
+            h, p = i // 8, i % 8
+            pltpu.make_async_copy(
+                source.at[sec, pl.ds(pl.multiple_of(p * OWN + h * HOWN, HOWN), HOWN)],
+                df.at[pl.ds(pl.multiple_of(h * HROWS + p * HOWN, HOWN), HOWN)], sem,
+            ).start()
+            return c
+
+        lax.fori_loop(0, 16, body, 0)
+
+    def rows_loaded(source, sem):
+        pltpu.make_async_copy(source.at[sec], df, sem).wait()
+
     own_parts = [
         (wq_hbm, lambda i: wqkv.at[i, pl.ds(0, 2 * HD)]),
         (wk_hbm, lambda i: wqkv.at[i, pl.ds(2 * HD, HD)]),
@@ -87,7 +101,7 @@
     ]
     n_parts = len(own_parts)
     own_copies = [pltpu.make_async_copy(a, b(sec), w_l.at[i]) for i, (a, b) in enumerate(own_parts)]
-    x_copy.start()
+    load_rows(x_hbm, w_l.at[8])
     own_copies[7].start()
     for i in range(7):
         own_copies[i].start()
@@ -117,68 +131,79 @@
                     device_id={"section": other}, device_id_type=MESH,
                 ).wait_recv()
 
-    def rows_of(i):
-        return pl.ds(pl.multiple_of(i * OWN, OWN), OWN)
-
-    my_rows = rows_of(t)
-
-    def ag_start(buf, i):
-        def body(k, c):
-            p = (t + k) % 8
-            pltpu.make_async_remote_copy(
-                src_ref=buf.at[my_rows], dst_ref=buf.at[my_rows], send_sem=ag_s.at[i, p], recv_sem=ag_r.at[i, t],
-                device_id={"tensor": p}, device_id_type=MESH,
-            ).start()
-            return c
-
-        lax.fori_loop(1, 8, body, 0)
-
-    def ag_wait(buf, i):
-        def body(k, c):
-            p = (t + k) % 8
-            copy = pltpu.make_async_remote_copy(
-                src_ref=buf.at[my_rows], dst_ref=buf.at[rows_of(p)], send_sem=ag_s.at[i, p], recv_sem=ag_r.at[i, p],
-                device_id={"tensor": p}, device_id_type=MESH,
-            )
-            copy.wait_recv()
-            copy.wait_send()
-            return c
-
-        lax.fori_loop(1, 8, body, 0)
-
-    def rs_start(i):
-        def body(k, c):
-            p = (t + k) % 8
-            pltpu.make_async_remote_copy(
-                src_ref=rsrc.at[i, rows_of(p)], dst_ref=land.at[i, t], send_sem=rs_s.at[i, p], recv_sem=rs_r.at[i, t],
-                device_id={"tensor": p}, device_id_type=MESH,
-            ).start()
-            return c
-
-        lax.fori_loop(1, 8, body, 0)
-
-    def rs_sum(i):
-        acc_rows = rsrc[i, my_rows, :].astype(F32)
-
+    def half_rows(half):
+        return pl.ds(pl.multiple_of(half * HROWS, HROWS), HROWS)
+
+    def pair_rows(half):
+        return pl.ds(pl.multiple_of(half * ROWS, ROWS), ROWS)
+
+    def rows_of(half, owner):
+        return pl.ds(pl.multiple_of(half * HROWS + owner * HOWN, HOWN), HOWN)
+
+    def kept(half):
+        return pl.ds(pl.multiple_of(half * HOWN, HOWN), HOWN)
+
+    def over_peers(body):
+        def step(k, c):
+            body((t + k) % 8)
+            return c
+
+        lax.fori_loop(1, 8, step, 0)
+
+    def ag_copy(buf, i, half, to, owner):
+        rows = rows_of(half, owner)
+        return pltpu.make_async_remote_copy(
+            src_ref=buf.at[rows], dst_ref=buf.at[rows], send_sem=ag_s.at[i, half, to], recv_sem=ag_r.at[i, half, owner],
+            device_id={"tensor": to}, device_id_type=MESH,
+        )
+
+    def ag_start(buf, i, half):
+        over_peers(lambda p: ag_copy(buf, i, half, p, t).start())
+
+    def ag_wait(buf, i, half):
+        over_peers(lambda p: ag_copy(buf, i, half, t, p).wait_recv())
+
+    def ag_sent(buf, i, half):
+        over_peers(lambda p: ag_copy(buf, i, half, p, t).wait_send())
+
+    def rs_copy(i, half, to, sender):
+        return pltpu.make_async_remote_copy(
+            src_ref=rsrc.at[i, rows_of(half, to)], dst_ref=land.at[i, half, sender], send_sem=rs_s.at[i, half, to],
+            recv_sem=rs_r.at[i, half, sender], device_id={"tensor": to}, device_id_type=MESH,
+        )
+
+    def rs_start(i, half):
+        over_peers(lambda p: rs_copy(i, half, p, t).start())
+
+    def rs_sum(i, half):
         def body(k, total):
             p = (t + k) % 8
-            copy = pltpu.make_async_remote_copy(
-                src_ref=rsrc.at[i, rows_of(p)], dst_ref=land.at[i, p], send_sem=rs_s.at[i, p], recv_sem=rs_r.at[i, p],
-                device_id={"tensor": p}, device_id_type=MESH,
-            )
-            copy.wait_recv()
-            copy.wait_send()
-            return total + land[i, p].astype(F32)
-
-        return lax.fori_loop(1, 8, body, acc_rows)
-
-    def allowed_of(j):
-        rows = lax.broadcasted_iota(jnp.int32, (ROWS, ROWS), 0) + d * ROWS
-        cols = lax.broadcasted_iota(jnp.int32, (ROWS, ROWS), 1) + j * ROWS
-        return (cols <= rows) & (cols >= beg_ref[...][:, 0:1])
+            rs_copy(i, half, t, p).wait_recv()
+            return total + land[i, half, p].astype(F32)
+
+        return lax.fori_loop(1, 8, body, rsrc[i, rows_of(half, t), :].astype(F32))
+
+    def rs_sent(i, half):
+        over_peers(lambda p: rs_copy(i, half, p, t).wait_send())
+
+    def both(body):
+        def step(half, c):
+            body(half)
+            return c
+
+        lax.fori_loop(0, 2, step, 0)
+
+    def place_of(i):
+        return OWN * ((i // HOWN) % 8) + HOWN * (i // HROWS) + i % HOWN
+
+    def allowed_of(j, half):
+        rows = place_of(lax.broadcasted_iota(jnp.int32, (HROWS, 1), 0) + half * HROWS) + d * ROWS
+        cols = place_of(lax.broadcasted_iota(jnp.int32, (1, ROWS), 1)) + j * ROWS
+        allowed = (cols <= rows) & (cols >= beg_ref[half_rows(half), 0:1])
+        return jnp.concatenate([jnp.where(allowed, 0.0, MASKED)] * 2, axis=0)
 
     weight_ready(0, 7)
-    x_copy.wait()
+    rows_loaded(x_hbm, w_l.at[8])
 
     def first_norm(i, c):
         rows = pl.ds(pl.multiple_of(i * OWN, OWN), OWN)
@@ -187,61 +212,72 @@
         return c
 
     lax.fori_loop(0, ROWS // OWN, first_norm, 0)
-    x_own[0] = df[my_rows, :].astype(F32)
-    ct_copy.start()
+    for half in range(2):
+        x_own[0, kept(half), :] = df[rows_of(half, t), :].astype(F32)
+    load_rows(ct_hbm, w_l.at[9])
 
     def forward_layer(layer, c):
-        @pl.when(layer == 1)
-        def _():
-            weight_ready(1, 7)
-            v = x_own[1]
-            n1[1, my_rows, :] = (v * factor_of(v) * gains[1, 0:1, :]).astype(BF16)
-            ag_start(n1.at[1], 0)
-            ag_wait(n1.at[1], 0)
-
         weight_ready(layer, 0, 1, 2)
-        raw = dot_nt(n1[layer], wqkv[layer])
-        c0, c1, c2 = raw[:, 0:128], raw[:, 128:256], raw[:, 256:384]
-        lane = lanes_of(c0)
-        q1 = jnp.where(lane < 32, pltpu.roll(c0, 32, 1), pltpu.roll(c1, 32, 1))
-        k0 = jnp.where(lane < 64, pltpu.roll(c1, 64, 1), pltpu.roll(c2, 64, 1))
-        v0 = pltpu.roll(c2, 96, 1)
-        cosine, sine = cos_ref[...], sin_ref[...]
-        for h, part in ((0, c0), (1, q1)):
-            turned = part * cosine + swapped(part) * sine
-            q2[layer, pl.ds(h * ROWS, ROWS), :] = turned[:, 0:HD].astype(BF16)
-            q2t[layer, :, pl.ds(h * ROWS, ROWS)] = jnp.transpose(turned)[0:HD, :].astype(BF16)
-        turned = k0 * cosine + swapped(k0) * sine
-        kv[layer, d, pl.ds(0, HD), :] = jnp.transpose(turned)[0:HD, :].astype(BF16)
-        kv[layer, d, pl.ds(HD, HD), :] = jnp.transpose(v0)[0:HD, :].astype(BF16)
-
-        def kv_copy(owner, to):
+
+        def kv_copy(owner, to, half):
+            part = kv.at[layer, owner, :, half_rows(half)]
             return pltpu.make_async_remote_copy(
-                src_ref=kv.at[layer, owner], dst_ref=kv.at[layer, owner], send_sem=kv_s.at[to], recv_sem=kv_r.at[owner, layer],
+                src_ref=part, dst_ref=part, send_sem=kv_s.at[to, half], recv_sem=kv_r.at[owner, layer, half],
                 device_id={"dp": to}, device_id_type=MESH,
             )
 
-        def kv_send(k, c):
-            kv_copy(d, k).start()
-            return c
-
-        lax.fori_loop(d + 1, 8, kv_send, 0)
-        s_m[...] = jnp.full(s_m.shape, MASKED, F32)
-        stat_l[layer] = jnp.zeros((2 * ROWS, 1), F32)
-        acc[...] = jnp.zeros(acc.shape, F32)
-
-        def attend(i, c):
-            j = d - i
-
-            @pl.when(i > 0)
+        def project(half):
+            rows = half_rows(half)
+
+            @pl.when(layer == 1)
             def _():
-                kv_copy(j, d).wait_recv()
-
-            allowed = allowed_of(j)
-            for h in range(2):
-                rows = pl.ds(h * ROWS, ROWS)
-                s = dot(q2[layer, rows, :], kv[layer, j, pl.ds(0, HD), :]) * SCALE
-                s = jnp.where(allowed, s, MASKED)
+                ag_wait(n1.at[1], 0, half)
+
+            raw = dot_nt(n1[layer, rows, :], wqkv[layer])
+            c0, c1, c2 = raw[:, 0:128], raw[:, 128:256], raw[:, 256:384]
+            lane = lanes_of(c0)
+            q1 = jnp.where(lane < 32, pltpu.roll(c0, 32, 1), pltpu.roll(c1, 32, 1))
+            k0 = jnp.where(lane < 64, pltpu.roll(c1, 64, 1), pltpu.roll(c2, 64, 1))
+            v0 = pltpu.roll(c2, 96, 1)
+            cosine, sine = cos_ref[rows, :], sin_ref[rows, :]
+            turned = k0 * cosine + swapped(k0) * sine
+            kv[layer, d, pl.ds(0, HD), rows] = jnp.transpose(turned)[0:HD, :].astype(BF16)
+            kv[layer, d, pl.ds(HD, HD), rows] = jnp.transpose(v0)[0:HD, :].astype(BF16)
+
+            def kv_send(k, c):
+                kv_copy(d, k, half).start()
+                return c
+
+            lax.fori_loop(d + 1, 8, kv_send, 0)
+            for h, part in ((0, c0), (1, q1)):
+                turned = part * cosine + swapped(part) * sine
+                place = pl.ds(pl.multiple_of(half * ROWS + h * HROWS, HROWS), HROWS)
+                q2[layer, place, :] = turned[:, 0:HD].astype(BF16)
+                q2t[layer, :, place] = jnp.transpose(turned)[0:HD, :].astype(BF16)
+
+        both(project)
+
+        @pl.when(layer == 1)
+        def _():
+            both(lambda half: ag_sent(n1.at[1], 0, half))
+
+        weight_ready(layer, 3)
+
+        def attend_half(half):
+            rows = pair_rows(half)
+            s_m[rows, :] = jnp.full((ROWS, 1), MASKED, F32)
+            stat_l[layer, rows, :] = jnp.zeros((ROWS, 1), F32)
+            acc[rows, :] = jnp.zeros((ROWS, HD), F32)
+
+            def attend(i, c):
+                j = d - i
+
+                @pl.when((i > 0) & (half == 0))
+                def _():
+                    kv_copy(j, d, 0).wait_recv()
+                    kv_copy(j, d, 1).wait_recv()
+
+                s = dot(q2[layer, rows, :], kv[layer, j, pl.ds(0, HD), :]) * SCALE + allowed_of(j, half)
                 old = s_m[rows, :]
                 new = jnp.maximum(old, jnp.max(s, axis=-1, keepdims=True))
                 p = jnp.exp(s - new)
@@ -249,65 +285,92 @@
                 s_m[rows, :] = new
                 stat_l[layer, rows, :] = stat_l[layer, rows, :] * shrink + jnp.sum(p, axis=-1, keepdims=True)
                 acc[rows, :] = acc[rows, :] * shrink + dot_nt(p.astype(BF16), kv[layer, j, pl.ds(HD, HD), :])
-            return c
-
-        lax.fori_loop(0, d + 1, attend, 0)
-        total = stat_l[layer]
-        mixed = acc[...] / total
-        o_f[layer] = mixed
-        o_b[layer] = mixed.astype(BF16)
-        stat_m[layer] = s_m[...] + jnp.log(total)
+                return c
+
+            lax.fori_loop(0, d + 1, attend, 0)
+            total = stat_l[layer, rows, :]
+            mixed = acc[rows, :] / total
+            o_f[layer, rows, :] = mixed
+            o_b[layer, rows, :] = mixed.astype(BF16)
+            stat_m[layer, rows, :] = s_m[rows, :] + jnp.log(total)
+            first = pl.ds(pl.multiple_of(half * ROWS, HROWS), HROWS)
+            second = pl.ds(pl.multiple_of(half * ROWS + HROWS, HROWS), HROWS)
+
+            def out_part(n, c):
+                cols = pl.ds(pl.multiple_of(n * 512, 512), 512)
+                part = dot(o_b[layer, first, :], wo[layer, pl.ds(0, HD), cols])
+                part += dot(o_b[layer, second, :], wo[layer, pl.ds(HD, HD), cols])
+                rsrc[0, half_rows(half), cols] = part.astype(BF16)
+                return c
+
+            lax.fori_loop(0, 3, out_part, 0)
+            rs_start(0, half)
+
+        both(attend_half)
 
         def kv_sent(k, c):
-            kv_copy(d, k).wait_send()
-            return c
-
-        weight_ready(layer, 3)
-
-        def out_part(n, c):
-            cols = pl.ds(pl.multiple_of(n * 512, 512), 512)
-            part = dot(o_b[layer, pl.ds(0, ROWS), :], wo[layer, pl.ds(0, HD), cols])
-            part += dot(o_b[layer, pl.ds(ROWS, ROWS), :], wo[layer, pl.ds(HD, HD), cols])
-            rsrc[0, :, cols] = part.astype(BF16)
-            return c
-
-        lax.fori_loop(0, 3, out_part, 0)
-        rs_start(0)
+            kv_copy(d, k, 0).wait_send()
+            kv_copy(d, k, 1).wait_send()
+            return c
+
         lax.fori_loop(d + 1, 8, kv_sent, 0)
-        v = x_own[layer] + rs_sum(0)
-        h_own[layer] = v
-        n2[layer, my_rows, :] = (v * factor_of(v) * gains[layer, 8:9, :]).astype(BF16)
-        ag_start(n2.at[layer], 1)
-        ag_wait(n2.at[layer], 1)
+
+        def middle(half):
+            v = x_own[layer, kept(half), :] + rs_sum(0, half)
+            h_own[layer, kept(half), :] = v
+            n2[layer, rows_of(half, t), :] = (v * factor_of(v) * gains[layer, 8:9, :]).astype(BF16)
+            ag_start(n2.at[layer], 1, half)
+            rs_sent(0, half)
+
+        both(middle)
         weight_ready(layer, 4, 5)
-
-        def units(n, c):
-            cols = pl.ds(pl.multiple_of(n * 256, 256), 256)
-            upper = pl.ds(pl.multiple_of(n * 256 + FF, 256), 256)
-            g = dot(n2[layer], wgu[layer, :, cols])
-            up = dot(n2[layer], wgu[layer, :, upper])
-            gate_s[layer, :, cols] = g
-            up_s[layer, :, cols] = up
-            u_s[layer, :, cols] = (g * jax.nn.sigmoid(g) * up).astype(BF16)
-            return c
-
-        lax.fori_loop(0, 2, units, 0)
         weight_ready(layer, 6)
 
-        def down_part(n, c):
-            cols = pl.ds(pl.multiple_of(n * 512, 512), 512)
-            rsrc[1, :, cols] = dot(u_s[layer], wd[layer, :, cols]).astype(BF16)
-            return c
-
-        lax.fori_loop(0, 3, down_part, 0)
-        rs_start(1)
-        y = (h_own[layer] + rs_sum(1)).astype(BF16)
-        yb[layer] = y
+        def feed(half):
+            rows = half_rows(half)
+            ag_wait(n2.at[layer], 1, half)
+
+            def units(n, c):
+                cols = pl.ds(pl.multiple_of(n * 256, 256), 256)
+                above = pl.ds(pl.multiple_of(n * 256 + FF, 256), 256)
+                g = dot(n2[layer, rows, :], wgu[layer, :, cols])
+                up = dot(n2[layer, rows, :], wgu[layer, :, above])
+                gate_s[layer, rows, cols] = g
+                up_s[layer, rows, cols] = up
+                u_s[layer, rows, cols] = (g * jax.nn.sigmoid(g) * up).astype(BF16)
+                return c
+
+            lax.fori_loop(0, 2, units, 0)
+
+            def down_part(n, c):
+                cols = pl.ds(pl.multiple_of(n * 512, 512), 512)
+                rsrc[1, rows, cols] = dot(u_s[layer, rows, :], wd[layer, :, cols]).astype(BF16)
+                return c
+
+            lax.fori_loop(0, 3, down_part, 0)
+            rs_start(1, half)
+            ag_sent(n2.at[layer], 1, half)
+
+        both(feed)
 
         @pl.when(layer == 0)
         def _():
-            x_own[1] = y.astype(F32)
-
+            weight_ready(1, 7)
+
+        def result(half):
+            y = (h_own[layer, kept(half), :] + rs_sum(1, half)).astype(BF16)
+            yb[layer, kept(half), :] = y
+
+            @pl.when(layer == 0)
+            def _():
+                v = y.astype(F32)
+                x_own[1, kept(half), :] = v
+                n1[1, rows_of(half, t), :] = (v * factor_of(v) * gains[1, 0:1, :]).astype(BF16)
+                ag_start(n1.at[1], 0, half)
+
+            rs_sent(1, half)
+
+        both(result)
         row_out(layer, yb, y_out, 0)
         return c
 
@@ -334,7 +397,7 @@
 
     lax.fori_loop(0, 2, forward_layer, 0)
 
-    ct_copy.wait()
+    rows_loaded(ct_hbm, w_l.at[9])
 
     before, after = (z + 3) % 4, (z + 1) % 4
     far = (z + 2) % 4
@@ -546,36 +609,45 @@
     def backward_layer(step, c):
         layer = 1 - step
 
-        @pl.when(layer == 0)
-        def _():
-            ag_start(df, 2)
-
+        @pl.when(step == 1)
+        def _():
             attn_1(1)
             ffn_4(1)
-            ag_wait(df, 2)
-
-        dy = df[my_rows, :].astype(F32)
-        dxb[layer] = dy
-
-        def unit_grads(n, c):
-            cols = pl.ds(pl.multiple_of(n * 256, 256), 256)
-            upper = pl.ds(pl.multiple_of(n * 256 + FF, 256), 256)
-            du = dot_nt(df[...], wd[layer, cols, :])
-            g, up = gate_s[layer, :, cols], up_s[layer, :, cols]
-            sig = jax.nn.sigmoid(g)
-            dgu[:, cols] = (du * up * sig * (1.0 + g * (1.0 - sig))).astype(BF16)
-            dgu[:, upper] = (du * g * sig).astype(BF16)
-            return c
-
-        lax.fori_loop(0, 2, unit_grads, 0)
-
-        def normed_part(n, c):
-            cols = pl.ds(pl.multiple_of(n * 256, 256), 256)
-            rsrc[0, :, cols] = dot_nt(dgu[...], wgu[layer, cols, :]).astype(BF16)
-            return c
-
-        lax.fori_loop(0, 6, normed_part, 0)
-        rs_start(0)
+
+        def feed_back(half):
+            rows = half_rows(half)
+
+            @pl.when(step == 1)
+            def _():
+                ag_wait(df, 2, half)
+
+            dxb[layer, kept(half), :] = df[rows_of(half, t), :].astype(F32)
+
+            def unit_grads(n, c):
+                cols = pl.ds(pl.multiple_of(n * 256, 256), 256)
+                above = pl.ds(pl.multiple_of(n * 256 + FF, 256), 256)
+                du = dot_nt(df[rows, :], wd[layer, cols, :])
+                g, up = gate_s[layer, rows, cols], up_s[layer, rows, cols]
+                sig = jax.nn.sigmoid(g)
+                dgu[rows, cols] = (du * up * sig * (1.0 + g * (1.0 - sig))).astype(BF16)
+                dgu[rows, above] = (du * g * sig).astype(BF16)
+                return c
+
+            lax.fori_loop(0, 2, unit_grads, 0)
+
+            def normed_part(n, c):
+                cols = pl.ds(pl.multiple_of(n * 256, 256), 256)
+                rsrc[0, rows, cols] = dot_nt(dgu[rows, :], wgu[layer, cols, :]).astype(BF16)
+                return c
+
+            lax.fori_loop(0, 6, normed_part, 0)
+            rs_start(0, half)
+
+        both(feed_back)
+
+        @pl.when(step == 1)
+        def _():
+            both(lambda half: ag_sent(df, 2, half))
 
         def unit_weights(n, c):
             cols = pl.ds(pl.multiple_of(n * 384, 384), 384)
@@ -598,28 +670,36 @@
             ffn_5(1)
             attn_2(1)
 
-        dn = rs_sum(0)
-        h = h_own[layer]
-        r = factor_of(h)
-        tt = dn * gains[layer, 8:9, :]
-        dh = dxb[layer] + r * tt - h * (r * r * r * jnp.mean(h * tt, axis=-1, keepdims=True))
-        dgain[layer, 1:2, :] = jnp.sum(dn * h * r, axis=0, keepdims=True)
-        dxb[layer] = dh
-        da[my_rows, :] = dh.astype(BF16)
-        ag_start(da, 3)
+        def hidden_grads(half):
+            dn = rs_sum(0, half)
+            h = h_own[layer, kept(half), :]
+            r = factor_of(h)
+            tt = dn * gains[layer, 8:9, :]
+            dh = dxb[layer, kept(half), :] + r * tt - h * (r * r * r * jnp.mean(h * tt, axis=-1, keepdims=True))
+            dgain[layer, 1:2, :] += jnp.sum(dn * h * r, axis=0, keepdims=True)
+            dxb[layer, kept(half), :] = dh
+            da[rows_of(half, t), :] = dh.astype(BF16)
+            ag_start(da, 3, half)
+            rs_sent(0, half)
+
+        both(hidden_grads)
         ffn_1(layer)
 
         @pl.when((step == 1) & (sec == 1))
         def _():
             ffn_6()
 
-        ag_wait(da, 3)
-        for h in range(2):
-            rows = pl.ds(h * ROWS, ROWS)
-            got = dot_nt(da[...], wo[layer, pl.ds(h * HD, HD), :])
-            do2[rows, :] = got.astype(BF16)
-            padded = jnp.concatenate([got, jnp.zeros((ROWS, 128 - HD), F32)], axis=1)
-            do2t[:, rows] = jnp.transpose(padded)[0:HD, :].astype(BF16)
+        def mixed_grads(half):
+            ag_wait(da, 3, half)
+            for h in range(2):
+                place = pl.ds(pl.multiple_of(half * ROWS + h * HROWS, HROWS), HROWS)
+                got = dot_nt(da[half_rows(half), :], wo[layer, pl.ds(h * HD, HD), :])
+                do2[place, :] = got.astype(BF16)
+                padded = jnp.concatenate([got, jnp.zeros((HROWS, 128 - HD), F32)], axis=1)
+                do2t[:, place] = jnp.transpose(padded)[0:HD, :].astype(BF16)
+
+        both(mixed_grads)
+        both(lambda half: ag_sent(da, 3, half))
         dot_rows = jnp.sum(do2[...].astype(F32) * o_f[layer], axis=-1, keepdims=True)
         s_m[...] = dot_rows
         acc[...] = jnp.zeros(acc.shape, F32)
@@ -631,14 +711,13 @@
             )
 
         def attend_back(j, c):
-            allowed = allowed_of(j)
             dkt = jnp.zeros((HD, ROWS), F32)
             dvt = jnp.zeros((HD, ROWS), F32)
-            for h in range(2):
-                rows = pl.ds(h * ROWS, ROWS)
+            for half in range(2):
+                rows = pair_rows(half)
                 kt = kv[layer, j, pl.ds(0, HD), :]
-                s = dot(q2[layer, rows, :], kt) * SCALE
-                p = jnp.exp(jnp.where(allowed, s, MASKED) - stat_m[layer, rows, :])
+                s = dot(q2[layer, rows, :], kt) * SCALE + allowed_of(j, half)
+                p = jnp.exp(s - stat_m[layer, rows, :])
                 dp = dot(do2[rows, :], kv[layer, j, pl.ds(HD, HD), :])
                 ds = (p * (dp - s_m[rows, :])).astype(BF16)
                 acc[rows, :] += dot_nt(ds, kt)
@@ -662,7 +741,8 @@
         def out_weights(n, c):
             cols = pl.ds(pl.multiple_of(n * 384, 384), 384)
             for h in range(2):
-                got = dot_tn(o_b[layer, pl.ds(h * ROWS, ROWS), :], da[:, cols])
+                mixed = [o_b[layer, pl.ds(half * ROWS + h * HROWS, HROWS), :] for half in range(2)]
+                got = dot_tn(jnp.concatenate(mixed, axis=0), da[:, cols])
                 gb[layer, 0, n, pl.ds(h * HD, HD), :] = got.astype(BF16)
             return c
 
@@ -684,7 +764,9 @@
         cosine, sine = cos_ref[...], sin_ref[...]
         dq[...] = jnp.zeros(dq.shape, F32)
         dq[:, 0:HD] = acc[...] * SCALE
-        dq0, dq1 = dq[pl.ds(0, ROWS), :], dq[pl.ds(ROWS, ROWS), :]
+        dq0, dq1 = (
+            jnp.concatenate([dq[pl.ds(half * ROWS + h * HROWS, HROWS), :] for half in range(2)], axis=0) for h in range(2)
+        )
         dq0 = dq0 * cosine - swapped(dq0) * sine
         dq1 = dq1 * cosine - swapped(dq1) * sine
         dk = dk_rot * cosine - swapped(dk_rot) * sine
@@ -693,13 +775,18 @@
         dqkv[:, 128:256] = jnp.where(lane < 64, pltpu.roll(dq1, 96, 1), pltpu.roll(dk, 64, 1)).astype(BF16)
         dqkv[:, 256:384] = jnp.where(lane < 32, pltpu.roll(dk, 64, 1), pltpu.roll(dv, 32, 1)).astype(BF16)
 
-        def input_part(n, c):
-            cols = pl.ds(pl.multiple_of(n * 256, 256), 256)
-            rsrc[1, :, cols] = dot(dqkv[...], wqkv[layer, :, cols]).astype(BF16)
-            return c
-
-        lax.fori_loop(0, 6, input_part, 0)
-        rs_start(1)
+        def project_back(half):
+            rows = half_rows(half)
+
+            def input_part(n, c):
+                cols = pl.ds(pl.multiple_of(n * 512, 512), 512)
+                rsrc[1, rows, cols] = dot(dqkv[rows, :], wqkv[layer, :, cols]).astype(BF16)
+                return c
+
+            lax.fori_loop(0, 3, input_part, 0)
+            rs_start(1, half)
+
+        both(project_back)
 
         def qkv_weights(n, c):
             cols = pl.ds(pl.multiple_of(n * 384, 384), 384)
@@ -711,14 +798,23 @@
         lax.fori_loop(0, 4, qkv_weights, 0)
         swap_cores(layer, 1).start()
         ffn_3(layer)
-        dn = rs_sum(1)
-        v = x_own[layer]
-        r = factor_of(v)
-        tt = dn * gains[layer, 0:1, :]
-        dx = dxb[layer] + r * tt - v * (r * r * r * jnp.mean(v * tt, axis=-1, keepdims=True))
-        dgain[layer, 0:1, :] = jnp.sum(dn * v * r, axis=0, keepdims=True)
-        dxb[layer] = dx
-        df[my_rows, :] = dx.astype(BF16)
+        def input_grads(half):
+            dn = rs_sum(1, half)
+            v = x_own[layer, kept(half), :]
+            r = factor_of(v)
+            tt = dn * gains[layer, 0:1, :]
+            dx = dxb[layer, kept(half), :] + r * tt - v * (r * r * r * jnp.mean(v * tt, axis=-1, keepdims=True))
+            dgain[layer, 0:1, :] += jnp.sum(dn * v * r, axis=0, keepdims=True)
+            dxb[layer, kept(half), :] = dx
+
+            @pl.when(step == 0)
+            def _():
+                df[rows_of(half, t), :] = dx.astype(BF16)
+                ag_start(df, 2, half)
+
+            rs_sent(1, half)
+
+        both(input_grads)
         row_out(layer, dxb, dx_out, 1)
         return c
 
@@ -739,11 +835,14 @@
             device_id={axis: to}, device_id_type=MESH,
         )
 
-    def gain_round(axis, i, buf, me):
+    def gain_send(axis, i, buf, me):
         def send(k, c):
             gain_copy(axis, i, buf, me, (me + k) % 8, me).start()
             return c
 
+        lax.fori_loop(1, 8, send, 0)
+
+    def gain_sum(axis, i, buf, me):
         def take(k, total):
             p = (me + k) % 8
             gain_copy(axis, i, buf, me, p, p).wait_recv()
@@ -753,7 +852,6 @@
             gain_copy(axis, i, buf, me, (me + k) % 8, me).wait_send()
             return c
 
-        lax.fori_loop(1, 8, send, 0)
         total = lax.fori_loop(1, 8, take, buf[me])
         lax.fori_loop(1, 8, sent, 0)
         return total
@@ -761,15 +859,17 @@
     mate.wait_recv()
     mate.wait_send()
     dg_t[t] = dgain[sec] + dg_peer[...]
+    gain_send("tensor", 1, dg_t, t)
     ffn_5(0)
-    dg_d[d] = gain_round("tensor", 1, dg_t, t)
+    dg_d[d] = gain_sum("tensor", 1, dg_t, t)
+    gain_send("dp", 2, dg_d, d)
     attn_2(0)
 
     @pl.when(sec == 0)
     def _():
         ffn_6()
 
-    gn_out[...] = gain_round("dp", 2, dg_d, d)
+    gn_out[...] = gain_sum("dp", 2, dg_d, d)
     attn_3()
     ffn_7()
     row_out_wait(yb, y_out, 0)
@@ -790,7 +890,7 @@
         pltpu.VMEM((2, 2 * ROWS, HD), BF16), pltpu.VMEM((2, 2 * ROWS, 1), F32), pltpu.VMEM((2, 2 * ROWS, 1), F32),
         pltpu.VMEM((2, ROWS, FF), F32), pltpu.VMEM((2, ROWS, FF), F32), pltpu.VMEM((2, ROWS, FF), BF16),
         pltpu.VMEM((2, OWN, D), F32), pltpu.VMEM((2, OWN, D), F32),
-        pltpu.VMEM((2, ROWS, D), BF16), pltpu.VMEM((2, 8, OWN, D), BF16), pltpu.VMEM((ROWS, D), BF16),
+        pltpu.VMEM((2, ROWS, D), BF16), pltpu.VMEM((2, 2, 8, HOWN, D), BF16), pltpu.VMEM((ROWS, D), BF16),
         pltpu.VMEM((2 * ROWS, HD), BF16), pltpu.VMEM((HD, 2 * ROWS), BF16), pltpu.VMEM((ROWS, 2 * FF), BF16),
         pltpu.VMEM((2 * ROWS, 128), F32), pltpu.VMEM((ROWS, 384), BF16), pltpu.VMEM((2, 128, ROWS), F32),
         pltpu.VMEM((8, 2 * HD, ROWS), BF16), pltpu.VMEM((2, 8, 2 * HD, ROWS), BF16), pltpu.VMEM((2 * ROWS, HD), F32),
@@ -800,7 +900,7 @@
         pltpu.VMEM((2, 288, 512), BF16), pltpu.VMEM((2, 576, 512), BF16), pltpu.VMEM((2, 144, 384), BF16),
         pltpu.VMEM((2, OWN, D), BF16), pltpu.VMEM((2, OWN, D), F32), pltpu.VMEM((2, 8, D), F32), pltpu.VMEM((8, D), F32),
         pltpu.VMEM((8, 8, D), F32), pltpu.VMEM((8, 8, D), F32),
-        dma((10,)), dma((8,)), dma((8,)), dma((4, 8)), dma((4, 8)), dma((2, 8)), dma((2, 8)), dma((8,)), dma((8, 2)),
+        dma((10,)), dma((8,)), dma((8,)), dma((4, 2, 8)), dma((4, 2, 8)), dma((2, 2, 8)), dma((2, 2, 8)), dma((8, 2)), dma((8, 2, 2)),
         dma((8,)), dma((2, 8)), dma((2,)), dma((2,)), dma((2,)),
         dma((2, 2)), dma((2, 2)), dma((2, 6)), dma((2, 6)), dma((2, 2)), dma((2, 2)), dma((2, 3)), dma((2, 4)), dma,
         dma((2, 2)), dma((2, 2)), dma((2, 8)), dma((2, 8)), dma((2, 8)), dma((2, 8)), dma, dma((3, 8)), dma((3, 8)),
@@ -857,7 +957,8 @@
     gains = jnp.concatenate([jnp.broadcast_to(norm_one, (8, D)), jnp.broadcast_to(norm_two, (8, D))]).astype(F32)
     lengths = lax.dynamic_index_in_dim(doc_lengths, lax.axis_index("section"), 0, keepdims=False)
     starts = jnp.cumsum(lengths) - lengths
-    places = lax.axis_index("dp") * ROWS + jnp.arange(ROWS, dtype=jnp.int32)
+    i = jnp.arange(ROWS, dtype=jnp.int32)
+    places = lax.axis_index("dp") * ROWS + OWN * ((i // HOWN) % 8) + HOWN * (i // HROWS) + i % HOWN
     begins = jnp.max(jnp.where(starts[None, :] <= places[:, None], starts[None, :], 0), axis=1)
     inverse = jnp.exp(jnp.arange(HALF, dtype=F32) * (-2.0 * math.log(ROPE) / HD))
     angles = (places - begins).astype(F32)[:, None] * inverse[None, :]

time: 337 us -> 318 us (0.944)
  Pallas kernels: 320 us -> 300 us
    pallas_call x1, Pallas kernels: 315 us -> 295 us  [step_call(): pl.pallas_call(kernel, out_shape=(jax.ShapeDtypeStruct((2, OWN, D), BF16)...]
where the time goes in v3:
time: 318 us; the launch traced here: 313 us
  Pallas kernels  300 us (94%)
  local copies, waits for them, and re-layouts  8.26 us (3%)
  other arithmetic  4.48 us (1%)
    pallas_call x1, Pallas kernels, step_call(): pl.pallas_call(kernel, out_shape=(jax.ShapeDtypeStruct((2, OWN, D), BF16)...  295 us

profile of v3, /device:TPU:24, one launch (start us, length us, event | category | flops | bytes accessed | tf_op | source)
XLA Modules:
  0.0 313.1 jit_solution(4279416516941249388)
XLA Ops:
  0.6 0.7 constant_dynamic-slice_fusion
  1.3 0.2 reduce-window_clone.1
  1.5 0.7 subtract_bitcast_fusion
  2.2 0.1 pad.5.clone
  2.3 0.1 select_reduce_fusion
  2.4 0.7 reduce
  3.2 0.7 reduce.1
  3.9 0.6 maximum_convert_fusion.gains_hbm
  4.6 0.8 broadcast_in_dim.71.beg_ref
  5.3 0.5 fusion
  5.9 0.8 maximum_maximum_fusion.1
  6.7 294.6 %train_step.1 = (bf16[2,32,1536]{2,1,0:T(8,128)(2,1)}, f32[2,32,1536]{2,1,0:T(8,128)}, bf16[2,4,576,512]{3,2,1,0:T(8,128)(2,1)}, bf16[2,4,288,384]{3,2,1,0:T(8,128)(2,1)}, f32[8,1536]{1,0:T(8,128)}) custom-call(bf16[2,256,1536]{2,1,0:T(8,128)(2,1)} %x_hbm.1, bf16[2,256,1536]{2,1,0:T(8,128)(2,1)} %ct_hbm.1, bf16[192,1536]{1,0:T(8,128)(2,1)} %bitcast.33, ...), custom_call_target="tpu_custom_call" | custom-call | tf_op jit(solution)/shard_map/train_step/pallas_call | solution.py:908
  301.3 1.5 fusion.10
  302.8 0.0 copy-start
  302.8 2.3 copy-done
  305.1 0.0 copy-start.1
  305.1 1.5 copy-done.1
  306.6 0.0 copy-start.3
  306.6 0.0 copy-start.2
  306.6 5.1 %widen.1 = (f32[1536,512]{1,0:T(8,128)}, f32[1536,512]{1,0:T(8,128)}, f32[512,1536]{1,0:T(8,128)}, f32[192,1536]{1,0:T(8,128)}, f32[192,1536]{1,0:T(8,128)}, /*index=5*/f32[96,1536]{1,0:T(8,128)}, f32[96,1536]{1,0:T(8,128)}) custom-call(bf16[2,4,576,512]{3,2,1,0:T(8,128)(2,1)S(1)} %copy-done, bf16[2,4,288,384]{3,2,1,0:T(8,128)(2,1)S(1)} %copy-done.1), custom_call_target="tpu_custom_call" | custom-call | tf_op jit(solution)/shard_map/widen/pallas_call | solution.py:945
  311.7 0.0 copy-done.3
  311.7 0.7 copy.25
  312.3 0.0 copy-done.2
  312.3 0.7 copy.26
  (6 shorter events, 0.0 us)
Async XLA Ops:
  302.8 2.3 copy-start
  305.1 1.5 copy-start.1
  306.6 5.1 %copy-start.3 = (bf16[2,32,1536]{2,1,0:T(8,128)(2,1)S(1)}, bf16[2,32,1536]{2,1,0:T(8,128)(2,1)}, u32[]{:S(2)}) copy-start(bf16[2,32,1536]{2,1,0:T(8,128)(2,1)} %get-tuple-element.23) | copy-start | bytes 589828
  306.6 5.8 %copy-start.2 = (f32[2,32,1536]{2,1,0:T(8,128)S(1)}, f32[2,32,1536]{2,1,0:T(8,128)}, u32[]{:S(2)}) copy-start(f32[2,32,1536]{2,1,0:T(8,128)} %get-tuple-element.24) | copy-start | bytes 1179652

commit v4 on v3

--- a/solution.py
+++ b/solution.py
@@ -55,9 +55,9 @@
     wqkv, wo, wgu, wd, gains, df,
     n1, n2, q2, q2t, kv, o_f, o_b, stat_m, stat_l, gate_s, up_s, u_s, x_own, h_own,
     rsrc, land, da, do2, do2t, dgu, dq, dqkv, dkv_t, dkv_src, dkv_land, acc, s_m,
-    ga, gb, da_in, db_in, za, rb, xa, fa, fb, yb, dxb, dgain, dg_peer, dg_t, dg_d,
+    ga, gb, da_in, db_in, za, zb, xa, xb, fa, fb, yb, dxb, dgain, dg_peer, dg_t, dg_d,
     w_l, w_s, w_r, ag_s, ag_r, rs_s, rs_r, kv_s, kv_r, dkv_s, dkv_r, out_l, out_s, out_r,
-    ds_s, ds_r, z_s, z_r, x_s, x_r, a_s, a_r, a_l, f_s, f_r, b_s, b_r, e_s, e_r, e_l, ns, nr,
+    ds_s, ds_r, z_s, z_r, x_s, x_r, a_s, a_r, a_l, f_s, f_r, ns, nr,
 ):
     sec = lax.axis_index("section")
     t = lax.axis_index("tensor")
@@ -399,22 +399,25 @@
 
     rows_loaded(ct_hbm, w_l.at[9])
 
+    sets = ((ga, da_in, za, xa, fa, ga_out), (gb, db_in, zb, xb, fb, gb_out))
     before, after = (z + 3) % 4, (z + 1) % 4
     far = (z + 2) % 4
-    upper, lower = pl.ds(0, 288), pl.ds(288, 288)
 
     def dp_at(zz, xx):
         return zz * 2 + xx
 
+    def quarter(i, which):
+        size = (288, 144)[i]
+        return pl.ds(pl.multiple_of(which * size, 16), size)
+
     def swap_cores(layer, i):
-        buf, landing = ((ga, da_in), (gb, db_in))[i]
         return pltpu.make_async_remote_copy(
-            src_ref=buf.at[layer, other], dst_ref=landing.at[layer], send_sem=ds_s.at[i, layer], recv_sem=ds_r.at[i, layer],
-            device_id={"section": other}, device_id_type=MESH,
-        )
-
-    def add_rows(target, index, rows, sources, count):
-        first, size = rows
+            src_ref=sets[i][0].at[layer, other], dst_ref=sets[i][1].at[layer], send_sem=ds_s.at[i, layer],
+            recv_sem=ds_r.at[i, layer], device_id={"section": other}, device_id_type=MESH,
+        )
+
+    def add_rows(target, index, first, size, sources):
+        count = 96 if size % 96 == 0 else 48
 
         def add(n, carry):
             here = pl.ds(pl.multiple_of(first + n * count, 16), count)
@@ -426,193 +429,140 @@
 
         lax.fori_loop(0, size // count, add, 0)
 
-    def z_piece(layer, piece, chunk, rows, to):
+    def z_piece(layer, i, piece, chunk, which, to):
         return pltpu.make_async_remote_copy(
-            src_ref=ga.at[layer, sec, chunk, rows], dst_ref=za.at[layer, piece], send_sem=z_s.at[layer, piece],
-            recv_sem=z_r.at[layer, piece], device_id={"dp": dp_at(to, xh)}, device_id_type=MESH,
-        )
-
-    def ffn_1(layer):
-        swap_cores(layer, 0).wait_recv()
+            src_ref=sets[i][0].at[layer, sec, chunk, quarter(i, which)], dst_ref=sets[i][2].at[layer, piece],
+            send_sem=z_s.at[i, layer, piece], recv_sem=z_r.at[i, layer, piece], device_id={"dp": dp_at(to, xh)},
+            device_id_type=MESH,
+        )
+
+    def sum_1(layer, i):
+        g, arrived = sets[i][0:2]
+        swap_cores(layer, i).wait_recv()
         for chunk, sends in (
-            (far, ((0, upper, after), (1, lower, before))),
-            (after, ((2, lower, after),)),
-            (before, ((3, upper, before),)),
+            (far, ((0, 0, after), (1, 1, before))),
+            (after, ((2, 1, after),)),
+            (before, ((3, 0, before),)),
             (z, ()),
         ):
-            add_rows(ga, (layer, sec, chunk), (0, 576), [(da_in, (layer, chunk), 0)], 96)
-            for piece, rows, to in sends:
-                z_piece(layer, piece, chunk, rows, to).start()
-
-    def ffn_2(layer):
-        z_piece(layer, 0, far, upper, after).wait_recv()
-        add_rows(ga, (layer, sec, after), (0, 288), [(za, (layer, 0), 0)], 96)
-        z_piece(layer, 4, after, upper, after).start()
-        z_piece(layer, 1, far, lower, before).wait_recv()
-        add_rows(ga, (layer, sec, before), (288, 288), [(za, (layer, 1), 0)], 96)
-        z_piece(layer, 5, before, lower, before).start()
-
-    def x_over(layer):
+            add_rows(g, (layer, sec, chunk), 0, g.shape[3], [(arrived, (layer, chunk), 0)])
+            for piece, which, to in sends:
+                z_piece(layer, i, piece, chunk, which, to).start()
+
+    def sum_2(layer, i):
+        g, landed = sets[i][0], sets[i][2]
+        size = landed.shape[2]
+        z_piece(layer, i, 0, far, 0, after).wait_recv()
+        add_rows(g, (layer, sec, after), 0, size, [(landed, (layer, 0), 0)])
+        z_piece(layer, i, 4, after, 0, after).start()
+        z_piece(layer, i, 1, far, 1, before).wait_recv()
+        add_rows(g, (layer, sec, before), size, size, [(landed, (layer, 1), 0)])
+        z_piece(layer, i, 5, before, 1, before).start()
+
+    def x_over(layer, i):
         return pltpu.make_async_remote_copy(
-            src_ref=ga.at[layer, sec, z, pl.ds((1 - xh) * 288, 288)], dst_ref=xa.at[layer], send_sem=x_s.at[0, layer],
-            recv_sem=x_r.at[0, layer], device_id={"dp": dp_at(z, 1 - xh)}, device_id_type=MESH,
-        )
-
-    def x_back(layer, which):
-        part = fa.at[layer, pl.ds(which * 288, 288)]
+            src_ref=sets[i][0].at[layer, sec, z, quarter(i, 1 - xh)], dst_ref=sets[i][3].at[layer],
+            send_sem=x_s.at[i, 0, layer], recv_sem=x_r.at[i, 0, layer], device_id={"dp": dp_at(z, 1 - xh)},
+            device_id_type=MESH,
+        )
+
+    def x_back(layer, i, which):
+        part = sets[i][4].at[layer, quarter(i, which)]
         return pltpu.make_async_remote_copy(
-            src_ref=part, dst_ref=part, send_sem=x_s.at[1, layer], recv_sem=x_r.at[1, layer],
+            src_ref=part, dst_ref=part, send_sem=x_s.at[i, 1, layer], recv_sem=x_r.at[i, 1, layer],
             device_id={"dp": dp_at(z, 1 - xh)}, device_id_type=MESH,
         )
 
-    def ffn_3(layer):
+    def sum_3(layer, i):
+        g, landed = sets[i][0], sets[i][2]
+        size = landed.shape[2]
         for piece in (2, 3, 4, 5):
-            z_piece(layer, piece, z, upper, after).wait_recv()
-        add_rows(ga, (layer, sec, z), (0, 288), [(za, (layer, 3), 0), (za, (layer, 4), 0)], 96)
-        add_rows(ga, (layer, sec, z), (288, 288), [(za, (layer, 2), 0), (za, (layer, 5), 0)], 96)
-        x_over(layer).start()
-
-    def ffn_4(layer):
-        x_over(layer).wait_recv()
+            z_piece(layer, i, piece, z, 0, after).wait_recv()
+        add_rows(g, (layer, sec, z), 0, size, [(landed, (layer, 3), 0), (landed, (layer, 4), 0)])
+        add_rows(g, (layer, sec, z), size, size, [(landed, (layer, 2), 0), (landed, (layer, 5), 0)])
+        x_over(layer, i).start()
+
+    def spread(layer, i, half, chunk, which, to, k):
+        rows = quarter(i, which)
+        return pltpu.make_async_remote_copy(
+            src_ref=sets[i][4].at[layer, rows], dst_ref=sets[i][5].at[half, chunk, rows], send_sem=a_s.at[i, layer, which, k],
+            recv_sem=a_r.at[i, half, chunk, which], device_id={"section": layer, "dp": dp_at(to, xh)}, device_id_type=MESH,
+        )
+
+    def keep(layer, i, which):
+        rows = quarter(i, which)
+        return pltpu.make_async_copy(sets[i][4].at[layer, rows], sets[i][5].at[sec, z, rows], a_l.at[i, which])
+
+    def spread_all(layer, i, which):
+        spread(layer, i, sec, z, which, after, 0).start()
+        spread(layer, i, sec, z, which, before, 1).start()
+
+        @pl.when(layer == sec)
+        def _():
+            keep(layer, i, which).start()
+
+        @pl.when(layer != sec)
+        def _():
+            spread(layer, i, sec, z, which, z, 2).start()
+
+    def sum_4(layer, i):
+        g, over, done = sets[i][0], sets[i][3], sets[i][4]
+        size = over.shape[1]
+        x_over(layer, i).wait_recv()
 
         def add(n, carry):
-            here = pl.ds(pl.multiple_of(n * 96, 16), 96)
-            there = pl.ds(pl.multiple_of(xh * 288 + n * 96, 16), 96)
-            fa[layer, there, :] = (ga[layer, sec, z, there, :].astype(F32) + xa[layer, here, :].astype(F32)).astype(BF16)
+            here = pl.ds(pl.multiple_of(n * 48, 16), 48)
+            there = pl.ds(pl.multiple_of(xh * size + n * 48, 16), 48)
+            done[layer, there, :] = (g[layer, sec, z, there, :].astype(F32) + over[layer, here, :].astype(F32)).astype(BF16)
             return carry
 
-        lax.fori_loop(0, 3, add, 0)
-        x_back(layer, xh).start()
-
-    def spread(layer, half, chunk, to, i):
+        lax.fori_loop(0, size // 48, add, 0)
+        x_back(layer, i, xh).start()
+        spread_all(layer, i, xh)
+
+    def sum_5(layer, i):
+        x_back(layer, i, 1 - xh).wait_recv()
+        spread_all(layer, i, 1 - xh)
+
+    def pass_on(i, half, chunk, which, to):
+        part = sets[i][5].at[half, chunk, quarter(i, which)]
         return pltpu.make_async_remote_copy(
-            src_ref=fa.at[layer], dst_ref=ga_out.at[half, chunk], send_sem=a_s.at[layer, i], recv_sem=a_r.at[half, chunk],
-            device_id={"section": layer, "dp": dp_at(to, xh)}, device_id_type=MESH,
-        )
-
-    def keep(layer):
-        return pltpu.make_async_copy(fa.at[layer], ga_out.at[sec, z], a_l)
-
-    def ffn_5(layer):
-        x_back(layer, 1 - xh).wait_recv()
-        spread(layer, sec, z, after, 0).start()
-        spread(layer, sec, z, before, 1).start()
-
-        @pl.when(layer == sec)
-        def _():
-            keep(layer).start()
-
-        @pl.when(layer != sec)
-        def _():
-            spread(layer, sec, z, z, 2).start()
-
-    def pass_on(half, i, chunk, rows, to):
-        part = ga_out.at[half, chunk, rows]
-        return pltpu.make_async_remote_copy(
-            src_ref=part, dst_ref=part, send_sem=f_s.at[half, i], recv_sem=f_r.at[half, i],
+            src_ref=part, dst_ref=part, send_sem=f_s.at[i, half, which], recv_sem=f_r.at[i, half, which],
             device_id={"dp": dp_at(to, xh)}, device_id_type=MESH,
         )
 
-    def ffn_6():
+    def sum_6(i):
         for half in range(2):
-            spread(sec, half, before, z, 0).wait_recv()
-            pass_on(half, 0, before, upper, after).start()
-            spread(sec, half, after, z, 0).wait_recv()
-            pass_on(half, 1, after, lower, before).start()
-
-    def ffn_7():
-        keep(sec).wait()
-        spread(sec, other, z, z, 2).wait_recv()
-        for half in range(2):
-            pass_on(half, 0, far, upper, z).wait_recv()
-            pass_on(half, 1, far, lower, z).wait_recv()
-            pass_on(half, 0, before, upper, after).wait_send()
-            pass_on(half, 1, after, lower, before).wait_send()
-        spread(other, sec, z, z, 2).wait_send()
+            spread(sec, i, half, before, 0, z, 0).wait_recv()
+            pass_on(i, half, before, 0, after).start()
+            spread(sec, i, half, after, 1, z, 0).wait_recv()
+            pass_on(i, half, after, 1, before).start()
+
+    def sum_7(i):
+        for which in range(2):
+            keep(sec, i, which).wait()
+            spread(sec, i, other, z, which, z, 2).wait_recv()
+            spread(other, i, sec, z, which, z, 2).wait_send()
+            for half in range(2):
+                spread(sec, i, half, (after, before)[which], which, z, 0).wait_recv()
+                pass_on(i, half, far, which, z).wait_recv()
+                pass_on(i, half, z, which, after).wait_send()
         for layer in range(2):
-            swap_cores(layer, 0).wait_send()
+            swap_cores(layer, i).wait_send()
             for piece in range(6):
-                z_piece(layer, piece, z, upper, after).wait_send()
-            x_over(layer).wait_send()
-            x_back(layer, xh).wait_send()
-            spread(layer, sec, z, after, 0).wait_send()
-            spread(layer, sec, z, before, 1).wait_send()
-
-    def b_piece(layer, to, sender):
-        return pltpu.make_async_remote_copy(
-            src_ref=gb.at[layer, sec, to // 2, pl.ds((to % 2) * 144, 144)], dst_ref=rb.at[layer, sender],
-            send_sem=b_s.at[layer, to], recv_sem=b_r.at[layer, sender], device_id={"dp": to}, device_id_type=MESH,
-        )
-
-    def b_spread(layer, half, to, sender):
-        return pltpu.make_async_remote_copy(
-            src_ref=fb.at[layer], dst_ref=gb_out.at[half, sender // 2, pl.ds((sender % 2) * 144, 144)],
-            send_sem=e_s.at[layer, to], recv_sem=e_r.at[half, sender], device_id={"section": layer, "dp": to},
-            device_id_type=MESH,
-        )
-
-    def b_keep(layer):
-        return pltpu.make_async_copy(fb.at[layer], gb_out.at[sec, z, pl.ds(xh * 144, 144)], e_l)
-
-    def attn_1(layer):
-        swap_cores(layer, 1).wait_recv()
-        for chunk in (far, after, before, z):
-            add_rows(gb, (layer, sec, chunk), (0, 288), [(db_in, (layer, chunk), 0)], 144)
-
-        def send(k, c):
-            b_piece(layer, (d + k) % 8, d).start()
-            return c
-
-        lax.fori_loop(1, 8, send, 0)
-
-    def attn_2(layer):
-        def take(k, total):
-            p = (d + k) % 8
-            b_piece(layer, d, p).wait_recv()
-            return total + rb[layer, p].astype(F32)
-
-        mine = gb[layer, sec, z, pl.ds(pl.multiple_of(xh * 144, 16), 144), :].astype(F32)
-        fb[layer] = lax.fori_loop(1, 8, take, mine).astype(BF16)
-
-        def send(k, c):
-            b_spread(layer, sec, (d + k) % 8, d).start()
-            return c
-
-        lax.fori_loop(1, 8, send, 0)
-
-        @pl.when(layer == sec)
-        def _():
-            b_keep(layer).start()
-
-        @pl.when(layer != sec)
-        def _():
-            b_spread(layer, sec, d, d).start()
-
-    def attn_3():
-        b_keep(sec).wait()
-        b_spread(sec, other, d, d).wait_recv()
-        b_spread(other, sec, d, d).wait_send()
-
-        def finish(k, c):
-            p = (d + k) % 8
-            b_spread(sec, 0, d, p).wait_recv()
-            b_spread(sec, 1, d, p).wait_recv()
-            for layer in range(2):
-                b_piece(layer, p, d).wait_send()
-                b_spread(layer, sec, p, d).wait_send()
-            return c
-
-        lax.fori_loop(1, 8, finish, 0)
-        for layer in range(2):
-            swap_cores(layer, 1).wait_send()
+                z_piece(layer, i, piece, z, 0, after).wait_send()
+            x_over(layer, i).wait_send()
+            x_back(layer, i, xh).wait_send()
+            for which in range(2):
+                spread(layer, i, sec, z, which, after, 0).wait_send()
+                spread(layer, i, sec, z, which, before, 1).wait_send()
 
     def backward_layer(step, c):
         layer = 1 - step
 
         @pl.when(step == 1)
         def _():
-            attn_1(1)
-            ffn_4(1)
+            sum_1(1, 1)
 
         def feed_back(half):
             rows = half_rows(half)
@@ -667,8 +617,8 @@
 
         @pl.when(step == 1)
         def _():
-            ffn_5(1)
-            attn_2(1)
+            sum_4(1, 0)
+            sum_2(1, 1)
 
         def hidden_grads(half):
             dn = rs_sum(0, half)
@@ -683,11 +633,12 @@
             rs_sent(0, half)
 
         both(hidden_grads)
-        ffn_1(layer)
-
-        @pl.when((step == 1) & (sec == 1))
-        def _():
-            ffn_6()
+        sum_1(layer, 0)
+
+        @pl.when(step == 1)
+        def _():
+            sum_5(1, 0)
+            sum_3(1, 1)
 
         def mixed_grads(half):
             ag_wait(da, 3, half)
@@ -749,7 +700,11 @@
         lax.fori_loop(0, 4, out_weights, 0)
         lax.fori_loop(0, d, dkv_sent, 0)
 
-        ffn_2(layer)
+        sum_2(layer, 0)
+
+        @pl.when(step == 1)
+        def _():
+            sum_4(1, 1)
 
         def dkv_sum(k, total):
             dkv_copy(d, k).wait_recv()
@@ -797,7 +752,16 @@
 
         lax.fori_loop(0, 4, qkv_weights, 0)
         swap_cores(layer, 1).start()
-        ffn_3(layer)
+        sum_3(layer, 0)
+
+        @pl.when(step == 1)
+        def _():
+            sum_5(1, 1)
+
+            @pl.when(sec == 1)
+            def _():
+                sum_6(0)
+
         def input_grads(half):
             dn = rs_sum(1, half)
             v = x_own[layer, kept(half), :]
@@ -826,8 +790,13 @@
         device_id={"section": other}, device_id_type=MESH,
     )
     mate.start()
-    ffn_4(0)
-    attn_1(0)
+    sum_4(0, 0)
+    sum_1(0, 1)
+
+    @pl.when(sec == 1)
+    def _():
+        sum_6(1)
+
 
     def gain_copy(axis, i, buf, me, to, sender):
         return pltpu.make_async_remote_copy(
@@ -860,18 +829,26 @@
     mate.wait_send()
     dg_t[t] = dgain[sec] + dg_peer[...]
     gain_send("tensor", 1, dg_t, t)
-    ffn_5(0)
+    sum_5(0, 0)
+    sum_2(0, 1)
     dg_d[d] = gain_sum("tensor", 1, dg_t, t)
     gain_send("dp", 2, dg_d, d)
-    attn_2(0)
+    sum_3(0, 1)
 
     @pl.when(sec == 0)
     def _():
-        ffn_6()
+        sum_6(0)
+
+    sum_4(0, 1)
+    sum_5(0, 1)
+
+    @pl.when(sec == 0)
+    def _():
+        sum_6(1)
 
     gn_out[...] = gain_sum("dp", 2, dg_d, d)
-    attn_3()
-    ffn_7()
+    sum_7(0)
+    sum_7(1)
     row_out_wait(yb, y_out, 0)
     row_out_wait(dxb, dx_out, 1)
     for i in range(n_parts):
@@ -896,14 +873,15 @@
         pltpu.VMEM((8, 2 * HD, ROWS), BF16), pltpu.VMEM((2, 8, 2 * HD, ROWS), BF16), pltpu.VMEM((2 * ROWS, HD), F32),
         pltpu.VMEM((2 * ROWS, 1), F32),
         pltpu.VMEM((2, 2, 4, 576, 512), BF16), pltpu.VMEM((2, 2, 4, 288, 384), BF16), pltpu.VMEM((2, 4, 576, 512), BF16),
-        pltpu.VMEM((2, 4, 288, 384), BF16), pltpu.VMEM((2, 6, 288, 512), BF16), pltpu.VMEM((2, 8, 144, 384), BF16),
-        pltpu.VMEM((2, 288, 512), BF16), pltpu.VMEM((2, 576, 512), BF16), pltpu.VMEM((2, 144, 384), BF16),
+        pltpu.VMEM((2, 4, 288, 384), BF16), pltpu.VMEM((2, 6, 288, 512), BF16), pltpu.VMEM((2, 6, 144, 384), BF16),
+        pltpu.VMEM((2, 288, 512), BF16), pltpu.VMEM((2, 144, 384), BF16), pltpu.VMEM((2, 576, 512), BF16),
+        pltpu.VMEM((2, 288, 384), BF16),
         pltpu.VMEM((2, OWN, D), BF16), pltpu.VMEM((2, OWN, D), F32), pltpu.VMEM((2, 8, D), F32), pltpu.VMEM((8, D), F32),
         pltpu.VMEM((8, 8, D), F32), pltpu.VMEM((8, 8, D), F32),
         dma((10,)), dma((8,)), dma((8,)), dma((4, 2, 8)), dma((4, 2, 8)), dma((2, 2, 8)), dma((2, 2, 8)), dma((8, 2)), dma((8, 2, 2)),
         dma((8,)), dma((2, 8)), dma((2,)), dma((2,)), dma((2,)),
-        dma((2, 2)), dma((2, 2)), dma((2, 6)), dma((2, 6)), dma((2, 2)), dma((2, 2)), dma((2, 3)), dma((2, 4)), dma,
-        dma((2, 2)), dma((2, 2)), dma((2, 8)), dma((2, 8)), dma((2, 8)), dma((2, 8)), dma, dma((3, 8)), dma((3, 8)),
+        dma((2, 2)), dma((2, 2)), dma((2, 2, 6)), dma((2, 2, 6)), dma((2, 2, 2)), dma((2, 2, 2)), dma((2, 2, 2, 3)),
+        dma((2, 2, 4, 2)), dma((2, 2)), dma((2, 2, 2)), dma((2, 2, 2)), dma((3, 8)), dma((3, 8)),
     ]
     return pl.pallas_call(
         kernel,

time: 318 us -> 295 us (0.928); the launches traced: 313 us -> 295 us
  Pallas kernels: 300 us -> 281 us
    pallas_call x1, Pallas kernels: 295 us -> 276 us  [step_call(): pl.pallas_call(kernel, out_shape=(jax.ShapeDtypeStruct((2, OWN, D), BF16)...]
where the time goes in v4:
time: 295 us
  Pallas kernels  281 us (95%)
  local copies, waits for them, and re-layouts  8.26 us (3%)
  other arithmetic  4.48 us (2%)
    pallas_call x1, Pallas kernels, step_call(): pl.pallas_call(kernel, out_shape=(jax.ShapeDtypeStruct((2, OWN, D), BF16)...  276 us

profile of v4, /device:TPU:24, one launch (start us, length us, event | category | flops | bytes accessed | tf_op | source)
XLA Modules:
  0.0 294.7 jit_solution(18133982442361252583)
XLA Ops:
  0.6 0.7 constant_dynamic-slice_fusion
  1.3 0.2 reduce-window_clone.1
  1.5 0.7 subtract_bitcast_fusion
  2.2 0.1 pad.5.clone
  2.3 0.1 select_reduce_fusion
  2.4 0.7 reduce
  3.2 0.7 reduce.1
  3.9 0.6 maximum_convert_fusion.gains_hbm
  4.6 0.8 broadcast_in_dim.71.beg_ref
  5.3 0.5 fusion
  5.9 0.8 maximum_maximum_fusion.1
  6.7 276.2 %train_step.1 = (bf16[2,32,1536]{2,1,0:T(8,128)(2,1)}, f32[2,32,1536]{2,1,0:T(8,128)}, bf16[2,4,576,512]{3,2,1,0:T(8,128)(2,1)}, bf16[2,4,288,384]{3,2,1,0:T(8,128)(2,1)}, f32[8,1536]{1,0:T(8,128)}) custom-call(bf16[2,256,1536]{2,1,0:T(8,128)(2,1)} %x_hbm.1, bf16[2,256,1536]{2,1,0:T(8,128)(2,1)} %ct_hbm.1, bf16[192,1536]{1,0:T(8,128)(2,1)} %bitcast.33, ...), custom_call_target="tpu_custom_call" | custom-call | tf_op jit(solution)/shard_map/train_step/pallas_call | solution.py:886
  282.9 1.5 fusion.10
  284.4 0.0 copy-start
  284.4 2.3 copy-done
  286.7 0.0 copy-start.1
  286.7 1.5 copy-done.1
  288.2 0.0 copy-start.3
  288.2 0.0 copy-start.2
  288.2 5.1 %widen.1 = (f32[1536,512]{1,0:T(8,128)}, f32[1536,512]{1,0:T(8,128)}, f32[512,1536]{1,0:T(8,128)}, f32[192,1536]{1,0:T(8,128)}, f32[192,1536]{1,0:T(8,128)}, /*index=5*/f32[96,1536]{1,0:T(8,128)}, f32[96,1536]{1,0:T(8,128)}) custom-call(bf16[2,4,576,512]{3,2,1,0:T(8,128)(2,1)S(1)} %copy-done, bf16[2,4,288,384]{3,2,1,0:T(8,128)(2,1)S(1)} %copy-done.1), custom_call_target="tpu_custom_call" | custom-call | tf_op jit(solution)/shard_map/widen/pallas_call | solution.py:923
  293.3 0.0 copy-done.3
  293.3 0.7 copy.25
  294.0 0.0 copy-done.2
  294.0 0.7 copy.26
  (6 shorter events, 0.0 us)
Async XLA Ops:
  284.4 2.3 copy-start
  286.7 1.5 copy-start.1
  288.2 5.1 %copy-start.3 = (bf16[2,32,1536]{2,1,0:T(8,128)(2,1)S(1)}, bf16[2,32,1536]{2,1,0:T(8,128)(2,1)}, u32[]{:S(2)}) copy-start(bf16[2,32,1536]{2,1,0:T(8,128)(2,1)} %get-tuple-element.23) | copy-start | bytes 589828
  288.2 5.8 %copy-start.2 = (f32[2,32,1536]{2,1,0:T(8,128)S(1)}, f32[2,32,1536]{2,1,0:T(8,128)}, u32[]{:S(2)}) copy-start(f32[2,32,1536]{2,1,0:T(8,128)} %get-tuple-element.24) | copy-start | bytes 1179652

commit v5 on v4

--- a/solution.py
+++ b/solution.py
@@ -563,6 +563,7 @@
         @pl.when(step == 1)
         def _():
             sum_1(1, 1)
+            sum_4(1, 0)
 
         def feed_back(half):
             rows = half_rows(half)
@@ -617,7 +618,7 @@
 
         @pl.when(step == 1)
         def _():
-            sum_4(1, 0)
+            sum_5(1, 0)
             sum_2(1, 1)
 
         def hidden_grads(half):
@@ -637,7 +638,6 @@
 
         @pl.when(step == 1)
         def _():
-            sum_5(1, 0)
             sum_3(1, 1)
 
         def mixed_grads(half):
@@ -926,7 +926,7 @@
         out_shape=tuple(jax.ShapeDtypeStruct(shape, F32) for shape in shapes),
         in_specs=[pl.BlockSpec((2, 1, 576, 512), lambda c: (0, c, 0, 0)), pl.BlockSpec((2, 1, 288, 384), lambda c: (0, c, 0, 0))],
         out_specs=tuple(by_row + by_column),
-        compiler_params=pltpu.CompilerParams(vmem_limit_bytes=40 * 1024 * 1024),
+        compiler_params=pltpu.CompilerParams(vmem_limit_bytes=63 * 1024 * 1024),
         name="widen",
     )(ga, gb)
 

time: 295 us -> 286 us (0.969)
  Pallas kernels: 281 us -> 275 us
  local copies, waits for them, and re-layouts: 8.26 us -> 4.45 us
    pallas_call x1, Pallas kernels: 276 us -> 268 us  [step_call(): pl.pallas_call(kernel, out_shape=(jax.ShapeDtypeStruct((2, OWN, D), BF16)...]
    unnamed x10 -> x6, local copies, waits for them, and re-layouts: 5.24 us -> 1.43 us
where the time goes in v5:
time: 286 us; the launch traced here: 285 us
  Pallas kernels  275 us (96%)
  other arithmetic  4.48 us (2%)
  local copies, waits for them, and re-layouts  4.45 us (2%)
    pallas_call x1, Pallas kernels, step_call(): pl.pallas_call(kernel, out_shape=(jax.ShapeDtypeStruct((2, OWN, D), BF16)...  268 us
    pallas_call x1, Pallas kernels, widened(): pl.pallas_call(widen, grid=(4,), out_shape=tuple((jax.ShapeDtypeStruct(sh...  7.84 us

profile of v5, /device:TPU:24, one launch (start us, length us, event | category | flops | bytes accessed | tf_op | source)
XLA Modules:
  0.0 285.0 jit_solution(12927973595034032754)
XLA Ops:
  0.6 0.7 constant_dynamic-slice_fusion
  1.3 0.2 reduce-window_clone.1
  1.5 0.7 subtract_bitcast_fusion
  2.2 0.1 pad.5.clone
  2.3 0.1 select_reduce_fusion
  2.4 0.7 reduce
  3.2 0.7 reduce.1
  3.9 0.6 maximum_convert_fusion.gains_hbm
  4.6 0.8 broadcast_in_dim.71.beg_ref
  5.3 0.5 fusion
  5.9 0.8 maximum_maximum_fusion.1
  6.7 267.6 %train_step.1 = (bf16[2,32,1536]{2,1,0:T(8,128)(2,1)}, f32[2,32,1536]{2,1,0:T(8,128)}, bf16[2,4,576,512]{3,2,1,0:T(8,128)(2,1)}, bf16[2,4,288,384]{3,2,1,0:T(8,128)(2,1)}, f32[8,1536]{1,0:T(8,128)}) custom-call(bf16[2,256,1536]{2,1,0:T(8,128)(2,1)} %x_hbm.1, bf16[2,256,1536]{2,1,0:T(8,128)(2,1)} %ct_hbm.1, bf16[192,1536]{1,0:T(8,128)(2,1)} %bitcast.33, ...), custom_call_target="tpu_custom_call" | custom-call | tf_op jit(solution)/shard_map/train_step/pallas_call | solution.py:886
  274.3 1.5 fusion.10
  275.7 0.0 copy-start.1
  275.7 0.0 copy-start
  275.7 7.8 %widen.1 = (f32[1536,512]{1,0:T(8,128)}, f32[1536,512]{1,0:T(8,128)}, f32[512,1536]{1,0:T(8,128)}, f32[192,1536]{1,0:T(8,128)}, f32[192,1536]{1,0:T(8,128)}, /*index=5*/f32[96,1536]{1,0:T(8,128)}, f32[96,1536]{1,0:T(8,128)}) custom-call(bf16[2,4,576,512]{3,2,1,0:T(8,128)(2,1)} %get-tuple-element.26.ga_ref, bf16[2,4,288,384]{3,2,1,0:T(8,128)(2,1)} %get-tuple-element.27.gb_ref), custom_call_target="tpu_custom_call" | custom-call | tf_op jit(solution)/shard_map/widen/pallas_call | solution.py:923
  283.6 0.0 copy-done.1
  283.6 0.7 copy.25
  284.3 0.0 copy-done
  284.3 0.7 copy.26
  (6 shorter events, 0.0 us)
Async XLA Ops:
  275.7 7.9 %copy-start.1 = (bf16[2,32,1536]{2,1,0:T(8,128)(2,1)S(1)}, bf16[2,32,1536]{2,1,0:T(8,128)(2,1)}, u32[]{:S(2)}) copy-start(bf16[2,32,1536]{2,1,0:T(8,128)(2,1)} %get-tuple-element.23) | copy-start | bytes 589828
  275.7 8.5 %copy-start = (f32[2,32,1536]{2,1,0:T(8,128)S(1)}, f32[2,32,1536]{2,1,0:T(8,128)}, u32[]{:S(2)}) copy-start(f32[2,32,1536]{2,1,0:T(8,128)} %get-tuple-element.24) | copy-start | bytes 1179652

commit v6 on v5

--- a/solution.py
+++ b/solution.py
@@ -2,6 +2,7 @@
 
 import jax
 import jax.numpy as jnp
+import numpy as np
 from jax import lax
 from jax.experimental import pallas as pl
 from jax.experimental.pallas import tpu as pltpu
@@ -45,14 +46,18 @@
     return jnp.where(lanes_of(v) < HALF, pltpu.roll(v, 128 - HALF, 1), pltpu.roll(v, HALF, 1))
 
 
+def place_of(i):
+    return OWN * ((i // HOWN) % 8) + HOWN * (i // HROWS) + i % HOWN
+
+
 def factor_of(v):
     return lax.rsqrt(jnp.mean(v * v, axis=-1, keepdims=True) + EPS)
 
 
 def kernel(
-    x_hbm, ct_hbm, wq_hbm, wk_hbm, wv_hbm, wo_hbm, wg_hbm, wu_hbm, wd_hbm, gains_hbm, cos_ref, sin_ref, beg_ref,
+    x_hbm, ct_hbm, wq_hbm, wk_hbm, wv_hbm, wo_hbm, wg_hbm, wu_hbm, wd_hbm, one_ref, two_ref, lengths_ref, speed_ref,
     y_out, dx_out, ga_out, gb_out, gn_out,
-    wqkv, wo, wgu, wd, gains, df,
+    wqkv, wo, wgu, wd, gains, gains_own, gains_in, cos_ref, sin_ref, beg_ref, df,
     n1, n2, q2, q2t, kv, o_f, o_b, stat_m, stat_l, gate_s, up_s, u_s, x_own, h_own,
     rsrc, land, da, do2, do2t, dgu, dq, dqkv, dkv_t, dkv_src, dkv_land, acc, s_m,
     ga, gb, da_in, db_in, za, zb, xa, xb, fa, fb, yb, dxb, dgain, dg_peer, dg_t, dg_d,
@@ -97,14 +102,29 @@
         (wg_hbm, lambda i: wgu.at[i, :, 0:FF]),
         (wu_hbm, lambda i: wgu.at[i, :, FF : 2 * FF]),
         (wd_hbm, lambda i: wd.at[i]),
-        (gains_hbm, lambda i: gains.at[i]),
     ]
     n_parts = len(own_parts)
     own_copies = [pltpu.make_async_copy(a, b(sec), w_l.at[i]) for i, (a, b) in enumerate(own_parts)]
     load_rows(x_hbm, w_l.at[8])
-    own_copies[7].start()
-    for i in range(7):
+    for i in range(n_parts):
         own_copies[i].start()
+    gains_own[0:8, :] = jnp.broadcast_to(one_ref[...].astype(F32), (8, D))
+    gains_own[8:16, :] = jnp.broadcast_to(two_ref[...].astype(F32), (8, D))
+    gains[sec] = gains_own[...]
+
+    places = place_of(lax.broadcasted_iota(jnp.int32, (ROWS, 128), 0)) + d * ROWS
+
+    lengths = jnp.where(sec == 0, lengths_ref[0:1, :], lengths_ref[1:2, :])
+    start, begins = jnp.zeros((1, 1), jnp.int32), jnp.zeros((ROWS, 128), jnp.int32)
+    for n in range(lengths.shape[1]):
+        begins = jnp.maximum(begins, jnp.where(start <= places, start, 0))
+        start = start + lengths[:, n : n + 1]
+    beg_ref[...] = begins
+    angles = (places - begins).astype(F32) * speed_ref[0:1, :]
+    lane = lanes_of(angles)
+    cos_ref[...] = jnp.where(lane < HD, jnp.cos(angles), 0.0)
+    sine = jnp.sin(angles)
+    sin_ref[...] = jnp.where(lane < HALF, -sine, jnp.where(lane < HD, sine, 0.0))
     pl.semaphore_wait(barrier, 15)
     sent_parts = [
         pltpu.make_async_remote_copy(
@@ -113,8 +133,20 @@
         )
         for i, (a, b) in enumerate(own_parts)
     ]
-    for i in (7, 0, 1, 2, 3, 4, 5, 6):
+    gains_sent = pltpu.make_async_remote_copy(
+        src_ref=gains_own, dst_ref=gains_in, send_sem=w_s.at[n_parts], recv_sem=w_r.at[n_parts],
+        device_id={"section": other}, device_id_type=MESH,
+    )
+    gains_sent.start()
+    for i in range(n_parts):
         sent_parts[i].start()
+
+    def gains_arrived():
+        pltpu.make_async_remote_copy(
+            src_ref=gains_own, dst_ref=gains_in, send_sem=w_s.at[n_parts], recv_sem=w_r.at[n_parts],
+            device_id={"section": other}, device_id_type=MESH,
+        ).wait_recv()
+        gains[other] = gains_in[...]
 
     def weight_ready(layer, *which):
         @pl.when(layer == sec)
@@ -193,16 +225,13 @@
 
         lax.fori_loop(0, 2, step, 0)
 
-    def place_of(i):
-        return OWN * ((i // HOWN) % 8) + HOWN * (i // HROWS) + i % HOWN
-
     def allowed_of(j, half):
         rows = place_of(lax.broadcasted_iota(jnp.int32, (HROWS, 1), 0) + half * HROWS) + d * ROWS
         cols = place_of(lax.broadcasted_iota(jnp.int32, (1, ROWS), 1)) + j * ROWS
         allowed = (cols <= rows) & (cols >= beg_ref[half_rows(half), 0:1])
         return jnp.concatenate([jnp.where(allowed, 0.0, MASKED)] * 2, axis=0)
 
-    weight_ready(0, 7)
+    pl.when(sec == 1)(gains_arrived)
     rows_loaded(x_hbm, w_l.at[8])
 
     def first_norm(i, c):
@@ -353,9 +382,7 @@
 
         both(feed)
 
-        @pl.when(layer == 0)
-        def _():
-            weight_ready(1, 7)
+        pl.when((layer == 0) & (sec == 0))(gains_arrived)
 
         def result(half):
             y = (h_own[layer, kept(half), :] + rs_sum(1, half)).astype(BF16)
@@ -853,6 +880,7 @@
     row_out_wait(dxb, dx_out, 1)
     for i in range(n_parts):
         sent_parts[i].wait_send()
+    gains_sent.wait_send()
 
 
 def step_call(*args):
@@ -861,7 +889,8 @@
     dma = pltpu.SemaphoreType.DMA
     scratch = [
         pltpu.VMEM((2, 384, D), BF16), pltpu.VMEM((2, 192, D), BF16), pltpu.VMEM((2, D, 2 * FF), BF16),
-        pltpu.VMEM((2, FF, D), BF16), pltpu.VMEM((2, 16, D), F32), pltpu.VMEM((ROWS, D), BF16),
+        pltpu.VMEM((2, FF, D), BF16), pltpu.VMEM((2, 16, D), F32), pltpu.VMEM((16, D), F32), pltpu.VMEM((16, D), F32), pltpu.VMEM((ROWS, 128), F32),
+        pltpu.VMEM((ROWS, 128), F32), pltpu.VMEM((ROWS, 128), jnp.int32), pltpu.VMEM((ROWS, D), BF16),
         pltpu.VMEM((2, ROWS, D), BF16), pltpu.VMEM((2, ROWS, D), BF16), pltpu.VMEM((2, 2 * ROWS, HD), BF16),
         pltpu.VMEM((2, HD, 2 * ROWS), BF16), pltpu.VMEM((2, 8, 2 * HD, ROWS), BF16), pltpu.VMEM((2, 2 * ROWS, HD), F32),
         pltpu.VMEM((2, 2 * ROWS, HD), BF16), pltpu.VMEM((2, 2 * ROWS, 1), F32), pltpu.VMEM((2, 2 * ROWS, 1), F32),
@@ -892,7 +921,7 @@
             jax.ShapeDtypeStruct((2, 4, 288, 384), BF16),
             jax.ShapeDtypeStruct((8, D), F32),
         ),
-        in_specs=[hbm] * 10 + [vmem] * 3,
+        in_specs=[hbm] * 9 + [vmem] * 4,
         out_specs=(hbm, hbm, hbm, hbm, vmem),
         scratch_shapes=scratch,
         compiler_params=pltpu.CompilerParams(
@@ -902,56 +931,78 @@
     )(*args)
 
 
-def widen(ga_ref, gb_ref, gate_ref, up_ref, down_ref, out_ref, query_ref, key_ref, value_ref):
-    for h in range(2):
-        rows = pl.ds(192 * h, 192)
-        gate_ref[rows, :] = ga_ref[h, 0, 0:192, :].astype(F32)
-        up_ref[rows, :] = ga_ref[h, 0, 192:384, :].astype(F32)
-        for i in range(3):
-            down_ref[pl.ds(64 * h, 64), pl.ds(512 * i, 512)] = ga_ref[h, 0, 384 + 64 * i : 448 + 64 * i, :].astype(F32)
-    out_ref[...] = gb_ref[0, 0, 0:192, :].astype(F32)
-    query_ref[0:HD, :] = gb_ref[0, 0, 192:288, :].astype(F32)
-    query_ref[HD : 2 * HD, :] = gb_ref[1, 0, 0:HD, :].astype(F32)
-    key_ref[...] = gb_ref[1, 0, HD : 2 * HD, :].astype(F32)
-    value_ref[...] = gb_ref[1, 0, 2 * HD : 3 * HD, :].astype(F32)
-
-
-def widened(ga, gb):
-    shapes = [(D, FF), (D, FF), (FF, D), (192, D), (192, D), (HD, D), (HD, D)]
-    by_row = [pl.BlockSpec((384, FF), lambda c: (c, 0)), pl.BlockSpec((384, FF), lambda c: (c, 0)), pl.BlockSpec((128, D), lambda c: (c, 0))]
-    by_column = [pl.BlockSpec((rows, 384), lambda c: (0, c)) for rows in (192, 192, HD, HD)]
+def widen(
+    ga_hbm, gb_hbm, gn_ref, y_ref, dx_ref,
+    gate_hbm, up_hbm, down_hbm, out_hbm, query_hbm, key_hbm, value_hbm, one_ref, two_ref, y_out, dx_out,
+    ga, gb, gate, up, down, out, query, key, value, a_in, b_in, sent,
+):
+    parts = [(h, c) for c in range(4) for h in range(2)]
+    a_copies = [pltpu.make_async_copy(ga_hbm.at[h, c], ga.at[h, c], a_in.at[h, c]) for h, c in parts]
+    b_copies = [pltpu.make_async_copy(gb_hbm.at[:, c], gb.at[:, c], b_in.at[c]) for c in range(4)]
+    for copy in b_copies + a_copies:
+        copy.start()
+    one_ref[...] = gn_ref[0:1, :]
+    two_ref[...] = gn_ref[1:2, :]
+    y_out[0] = y_ref[...]
+    dx_out[0] = dx_ref[...]
+    for c in range(4):
+        b_copies[c].wait()
+        cols = pl.ds(384 * c, 384)
+        out[:, cols] = gb[0, c, 0:192, :].astype(F32)
+        query[0:HD, cols] = gb[0, c, 192:288, :].astype(F32)
+        query[HD : 2 * HD, cols] = gb[1, c, 0:HD, :].astype(F32)
+        key[:, cols] = gb[1, c, HD : 2 * HD, :].astype(F32)
+        value[:, cols] = gb[1, c, 2 * HD : 3 * HD, :].astype(F32)
+    leaving = [
+        pltpu.make_async_copy(buf, to, sent.at[i])
+        for i, (buf, to) in enumerate(((out, out_hbm), (query, query_hbm), (key, key_hbm), (value, value_hbm)))
+    ]
+    for copy in leaving:
+        copy.start()
+    for i, (h, c) in enumerate(parts):
+        a_copies[i].wait()
+        rows, few = pl.ds(384 * c + 192 * h, 192), pl.ds(128 * c + 64 * h, 64)
+        gate[rows, :] = ga[h, c, 0:192, :].astype(F32)
+        up[rows, :] = ga[h, c, 192:384, :].astype(F32)
+        for k in range(3):
+            down[few, pl.ds(512 * k, 512)] = ga[h, c, 384 + 64 * k : 448 + 64 * k, :].astype(F32)
+        for k, (buf, to, which) in enumerate(((gate, gate_hbm, rows), (up, up_hbm, rows), (down, down_hbm, few))):
+            copy = pltpu.make_async_copy(buf.at[which], to.at[which], sent.at[4 + 3 * i + k])
+            copy.start()
+            leaving.append(copy)
+    for copy in leaving:
+        copy.wait()
+
+
+def widened(ga, gb, gn, y, dx):
+    grads = [(D, FF), (D, FF), (FF, D), (192, D), (192, D), (HD, D), (HD, D)]
+    shapes = [jax.ShapeDtypeStruct(shape, F32) for shape in grads + [(1, D), (1, D)]]
+    shapes += [jax.ShapeDtypeStruct((1, 2, OWN, D), BF16), jax.ShapeDtypeStruct((1, 2, OWN, D), F32)]
+    hbm = pl.BlockSpec(memory_space=pl.ANY)
+    vmem = pl.BlockSpec(memory_space=pltpu.VMEM)
+    dma = pltpu.SemaphoreType.DMA
     return pl.pallas_call(
         widen,
-        grid=(4,),
-        out_shape=tuple(jax.ShapeDtypeStruct(shape, F32) for shape in shapes),
-        in_specs=[pl.BlockSpec((2, 1, 576, 512), lambda c: (0, c, 0, 0)), pl.BlockSpec((2, 1, 288, 384), lambda c: (0, c, 0, 0))],
-        out_specs=tuple(by_row + by_column),
+        out_shape=tuple(shapes),
+        in_specs=[hbm, hbm, vmem, vmem, vmem],
+        out_specs=tuple([hbm] * 7 + [vmem] * 4),
+        scratch_shapes=[pltpu.VMEM((2, 4, 576, 512), BF16), pltpu.VMEM((2, 4, 288, 384), BF16)]
+        + [pltpu.VMEM(shape, F32) for shape in grads]
+        + [dma((2, 4)), dma((4,)), dma((28,))],
         compiler_params=pltpu.CompilerParams(vmem_limit_bytes=63 * 1024 * 1024),
         name="widen",
-    )(ga, gb)
+    )(ga, gb, gn, y, dx)
 
 
 def on_device(inputs, cotangent, doc_lengths, norm_one, query_w, key_w, value_w, out_w, norm_two, gate_w, up_w, down_w):
-    gains = jnp.concatenate([jnp.broadcast_to(norm_one, (8, D)), jnp.broadcast_to(norm_two, (8, D))]).astype(F32)
-    lengths = lax.dynamic_index_in_dim(doc_lengths, lax.axis_index("section"), 0, keepdims=False)
-    starts = jnp.cumsum(lengths) - lengths
-    i = jnp.arange(ROWS, dtype=jnp.int32)
-    places = lax.axis_index("dp") * ROWS + OWN * ((i // HOWN) % 8) + HOWN * (i // HROWS) + i % HOWN
-    begins = jnp.max(jnp.where(starts[None, :] <= places[:, None], starts[None, :], 0), axis=1)
-    inverse = jnp.exp(jnp.arange(HALF, dtype=F32) * (-2.0 * math.log(ROPE) / HD))
-    angles = (places - begins).astype(F32)[:, None] * inverse[None, :]
-    cosine, sine = jnp.cos(angles), jnp.sin(angles)
-    rest = jnp.zeros((ROWS, 128 - HD), F32)
-    cosine = jnp.concatenate([cosine, cosine, rest], axis=1)
-    sine = jnp.concatenate([-sine, sine, rest], axis=1)
-    begins = jnp.broadcast_to(begins[:, None], (ROWS, 128))
+    lane = np.arange(128) % HALF
+    speed = jnp.asarray(np.exp(lane * (-2.0 * math.log(ROPE) / HD)).astype(np.float32)[None, :])
     y, dx, ga, gb, gn = step_call(
-        inputs, cotangent, query_w[0].T, key_w[0].T, value_w[0].T, out_w[0], gate_w[0], up_w[0], down_w[0], gains, cosine, sine, begins
+        inputs, cotangent, query_w[0].T, key_w[0].T, value_w[0].T, out_w[0], gate_w[0], up_w[0], down_w[0], norm_one, norm_two,
+        doc_lengths, speed,
     )
-    gate, up, down, out, query, key, value = widened(ga, gb)
-    return (
-        y[None], dx[None], gn[0:1], query.T[None], key.T[None], value.T[None], out[None], gn[1:2], gate[None], up[None], down[None],
-    )
+    gate, up, down, out, query, key, value, one, two, y, dx = widened(ga, gb, gn, y, dx)
+    return (y, dx, one, query.T[None], key.T[None], value.T[None], out[None], two, gate[None], up[None], down[None])
 
 
 def solution(mesh):

time: 286 us -> 276 us (0.965)
  other arithmetic: 4.48 us -> 0 us
  local copies, waits for them, and re-layouts: 4.45 us -> 0 us
where the time goes in v6:
time: 276 us; the launch traced here: 275 us
  Pallas kernels  275 us (100%)
    pallas_call x1, Pallas kernels, step_call(): pl.pallas_call(kernel, out_shape=(jax.ShapeDtypeStruct((2, OWN, D), BF16)...  265 us
    pallas_call x1, Pallas kernels, widened(): pl.pallas_call(widen, out_shape=tuple(shapes), in_specs=[hbm, hbm, vmem,...  9.62 us

profile of v6, /device:TPU:24, one launch (start us, length us, event | category | flops | bytes accessed | tf_op | source)
XLA Modules:
  0.0 275.2 jit_solution(17849178322113337258)
XLA Ops:
  0.6 264.9 %train_step.1 = (bf16[2,32,1536]{2,1,0:T(8,128)(2,1)}, f32[2,32,1536]{2,1,0:T(8,128)}, bf16[2,4,576,512]{3,2,1,0:T(8,128)(2,1)}, bf16[2,4,288,384]{3,2,1,0:T(8,128)(2,1)}, f32[8,1536]{1,0:T(8,128)}) custom-call(bf16[2,256,1536]{2,1,0:T(8,128)(2,1)} %x_hbm.1, bf16[2,256,1536]{2,1,0:T(8,128)(2,1)} %ct_hbm.1, bf16[192,1536]{1,0:T(8,128)(2,1)} %bitcast.29, ...), custom_call_target="tpu_custom_call" | custom-call | tf_op jit(solution)/shard_map/train_step/pallas_call | solution.py:915
  265.6 9.6 %widen.1 = (f32[1536,512]{1,0:T(8,128)}, f32[1536,512]{1,0:T(8,128)}, f32[512,1536]{1,0:T(8,128)}, f32[192,1536]{1,0:T(8,128)}, f32[192,1536]{1,0:T(8,128)}, /*i...) custom-call(bf16[2,4,576,512]{3,2,1,0:T(8,128)(2,1)} %get-tuple-elem, ...), custom_call_target="tpu_custom_call" | custom-call | tf_op jit(solution)/shard_map/widen/pallas_call | solution.py:984

commit v7 on v6

--- a/solution.py
+++ b/solution.py
@@ -274,7 +274,7 @@
             kv[layer, d, pl.ds(HD, HD), rows] = jnp.transpose(v0)[0:HD, :].astype(BF16)
 
             def kv_send(k, c):
-                kv_copy(d, k, half).start()
+                kv_copy(d, 8 + d - k, half).start()
                 return c
 
             lax.fori_loop(d + 1, 8, kv_send, 0)
@@ -337,13 +337,6 @@
 
         both(attend_half)
 
-        def kv_sent(k, c):
-            kv_copy(d, k, 0).wait_send()
-            kv_copy(d, k, 1).wait_send()
-            return c
-
-        lax.fori_loop(d + 1, 8, kv_sent, 0)
-
         def middle(half):
             v = x_own[layer, kept(half), :] + rs_sum(0, half)
             h_own[layer, kept(half), :] = v
@@ -398,6 +391,13 @@
             rs_sent(1, half)
 
         both(result)
+
+        def kv_sent(k, c):
+            kv_copy(d, k, 0).wait_send()
+            kv_copy(d, k, 1).wait_send()
+            return c
+
+        lax.fori_loop(d + 1, 8, kv_sent, 0)
         row_out(layer, yb, y_out, 0)
         return c
 
@@ -437,11 +437,14 @@
         size = (288, 144)[i]
         return pl.ds(pl.multiple_of(which * size, 16), size)
 
-    def swap_cores(layer, i):
+    def swap_cores(layer, i, chunk):
         return pltpu.make_async_remote_copy(
-            src_ref=sets[i][0].at[layer, other], dst_ref=sets[i][1].at[layer], send_sem=ds_s.at[i, layer],
-            recv_sem=ds_r.at[i, layer], device_id={"section": other}, device_id_type=MESH,
-        )
+            src_ref=sets[i][0].at[layer, other, chunk], dst_ref=sets[i][1].at[layer, chunk], send_sem=ds_s.at[i, layer, chunk],
+            recv_sem=ds_r.at[i, layer, chunk], device_id={"section": other}, device_id_type=MESH,
+        )
+
+    def chunk_at(n):
+        return (z + jnp.where(n == 0, 2, jnp.where(n == 3, 0, 2 * n - 1))) % 4
 
     def add_rows(target, index, first, size, sources):
         count = 96 if size % 96 == 0 else 48
@@ -465,13 +468,13 @@
 
     def sum_1(layer, i):
         g, arrived = sets[i][0:2]
-        swap_cores(layer, i).wait_recv()
         for chunk, sends in (
             (far, ((0, 0, after), (1, 1, before))),
             (after, ((2, 1, after),)),
             (before, ((3, 0, before),)),
             (z, ()),
         ):
+            swap_cores(layer, i, chunk).wait_recv()
             add_rows(g, (layer, sec, chunk), 0, g.shape[3], [(arrived, (layer, chunk), 0)])
             for piece, which, to in sends:
                 z_piece(layer, i, piece, chunk, which, to).start()
@@ -575,7 +578,8 @@
                 pass_on(i, half, far, which, z).wait_recv()
                 pass_on(i, half, z, which, after).wait_send()
         for layer in range(2):
-            swap_cores(layer, i).wait_send()
+            for chunk in range(4):
+                swap_cores(layer, i, chunk).wait_send()
             for piece in range(6):
                 z_piece(layer, i, piece, z, 0, after).wait_send()
             x_over(layer, i).wait_send()
@@ -587,10 +591,11 @@
     def backward_layer(step, c):
         layer = 1 - step
 
+
         @pl.when(step == 1)
         def _():
-            sum_1(1, 1)
-            sum_4(1, 0)
+            sum_5(1, 0)
+            sum_2(1, 1)
 
         def feed_back(half):
             rows = half_rows(half)
@@ -627,7 +632,8 @@
         def _():
             both(lambda half: ag_sent(df, 2, half))
 
-        def unit_weights(n, c):
+        def unit_weights(k, c):
+            n = chunk_at(k)
             cols = pl.ds(pl.multiple_of(n * 384, 384), 384)
             got = dot_tn(n2[layer, :, cols], dgu[...]).astype(BF16)
             for h in range(2):
@@ -638,15 +644,16 @@
             for h in range(2):
                 for i in range(3):
                     ga[layer, h, n, pl.ds(384 + 64 * i, 64), :] = got[64 * h : 64 * h + 64, 512 * i : 512 * i + 512]
+            swap_cores(layer, 0, n).start()
             return c
 
         lax.fori_loop(0, 4, unit_weights, 0)
-        swap_cores(layer, 0).start()
-
-        @pl.when(step == 1)
-        def _():
-            sum_5(1, 0)
-            sum_2(1, 1)
+        sum_1(layer, 0)
+
+        @pl.when((step == 1) & (sec == 1))
+        def _():
+            sum_6(0)
+
 
         def hidden_grads(half):
             dn = rs_sum(0, half)
@@ -661,11 +668,12 @@
             rs_sent(0, half)
 
         both(hidden_grads)
-        sum_1(layer, 0)
+        sum_2(layer, 0)
 
         @pl.when(step == 1)
         def _():
             sum_3(1, 1)
+
 
         def mixed_grads(half):
             ag_wait(da, 3, half)
@@ -712,10 +720,6 @@
 
         lax.fori_loop(0, d + 1, attend_back, 0)
 
-        def dkv_sent(k, c):
-            dkv_copy(k, d).wait_send()
-            return c
-
         def out_weights(n, c):
             cols = pl.ds(pl.multiple_of(n * 384, 384), 384)
             for h in range(2):
@@ -725,9 +729,8 @@
             return c
 
         lax.fori_loop(0, 4, out_weights, 0)
-        lax.fori_loop(0, d, dkv_sent, 0)
-
-        sum_2(layer, 0)
+
+        sum_3(layer, 0)
 
         @pl.when(step == 1)
         def _():
@@ -770,24 +773,22 @@
 
         both(project_back)
 
-        def qkv_weights(n, c):
+        def qkv_weights(k, c):
+            n = chunk_at(k)
             cols = pl.ds(pl.multiple_of(n * 384, 384), 384)
             got = dot_tn(dqkv[...], n1[layer, :, cols]).astype(BF16)
             gb[layer, 0, n, pl.ds(2 * HD, HD), :] = got[0:HD]
             gb[layer, 1, n] = got[HD : 4 * HD]
+            swap_cores(layer, 1, n).start()
             return c
 
         lax.fori_loop(0, 4, qkv_weights, 0)
-        swap_cores(layer, 1).start()
-        sum_3(layer, 0)
+        sum_1(layer, 1)
+        sum_4(layer, 0)
 
         @pl.when(step == 1)
         def _():
             sum_5(1, 1)
-
-            @pl.when(sec == 1)
-            def _():
-                sum_6(0)
 
         def input_grads(half):
             dn = rs_sum(1, half)
@@ -806,6 +807,12 @@
             rs_sent(1, half)
 
         both(input_grads)
+
+        def dkv_sent(k, c):
+            dkv_copy(k, d).wait_send()
+            return c
+
+        lax.fori_loop(0, d, dkv_sent, 0)
         row_out(layer, dxb, dx_out, 1)
         return c
 
@@ -817,13 +824,12 @@
         device_id={"section": other}, device_id_type=MESH,
     )
     mate.start()
-    sum_4(0, 0)
-    sum_1(0, 1)
+    sum_5(0, 0)
+    sum_2(0, 1)
 
     @pl.when(sec == 1)
     def _():
         sum_6(1)
-
 
     def gain_copy(axis, i, buf, me, to, sender):
         return pltpu.make_async_remote_copy(
@@ -856,16 +862,14 @@
     mate.wait_send()
     dg_t[t] = dgain[sec] + dg_peer[...]
     gain_send("tensor", 1, dg_t, t)
-    sum_5(0, 0)
-    sum_2(0, 1)
-    dg_d[d] = gain_sum("tensor", 1, dg_t, t)
-    gain_send("dp", 2, dg_d, d)
-    sum_3(0, 1)
 
     @pl.when(sec == 0)
     def _():
         sum_6(0)
 
+    sum_3(0, 1)
+    dg_d[d] = gain_sum("tensor", 1, dg_t, t)
+    gain_send("dp", 2, dg_d, d)
     sum_4(0, 1)
     sum_5(0, 1)
 
@@ -909,7 +913,7 @@
         pltpu.VMEM((8, 8, D), F32), pltpu.VMEM((8, 8, D), F32),
         dma((10,)), dma((8,)), dma((8,)), dma((4, 2, 8)), dma((4, 2, 8)), dma((2, 2, 8)), dma((2, 2, 8)), dma((8, 2)), dma((8, 2, 2)),
         dma((8,)), dma((2, 8)), dma((2,)), dma((2,)), dma((2,)),
-        dma((2, 2)), dma((2, 2)), dma((2, 2, 6)), dma((2, 2, 6)), dma((2, 2, 2)), dma((2, 2, 2)), dma((2, 2, 2, 3)),
+        dma((2, 2, 4)), dma((2, 2, 4)), dma((2, 2, 6)), dma((2, 2, 6)), dma((2, 2, 2)), dma((2, 2, 2)), dma((2, 2, 2, 3)),
         dma((2, 2, 4, 2)), dma((2, 2)), dma((2, 2, 2)), dma((2, 2, 2)), dma((3, 8)), dma((3, 8)),
     ]
     return pl.pallas_call(

time: 276 us -> 273 us (0.989)
  Pallas kernels: 275 us -> 271 us
    pallas_call x1, Pallas kernels: 265 us -> 262 us  [step_call(): pl.pallas_call(kernel, out_shape=(jax.ShapeDtypeStruct((2, OWN, D), BF16)...]
where the time goes in v7:
time: 273 us; the launch traced here: 272 us
  Pallas kernels  271 us (99%)
    pallas_call x1, Pallas kernels, step_call(): pl.pallas_call(kernel, out_shape=(jax.ShapeDtypeStruct((2, OWN, D), BF16)...  262 us
    pallas_call x1, Pallas kernels, widened(): pl.pallas_call(widen, out_shape=tuple(shapes), in_specs=[hbm, hbm, vmem,...  9.62 us

profile of v7, /device:TPU:24, one launch (start us, length us, event | category | flops | bytes accessed | tf_op | source)
XLA Modules:
  0.0 271.9 jit_solution(14890756860333023477)
XLA Ops:
  0.6 261.6 %train_step.1 = (bf16[2,32,1536]{2,1,0:T(8,128)(2,1)}, f32[2,32,1536]{2,1,0:T(8,128)}, bf16[2,4,576,512]{3,2,1,0:T(8,128)(2,1)}, bf16[2,4,288,384]{3,2,1,0:T(8,128)(2,1)}, f32[8,1536]{1,0:T(8,128)}) custom-call(bf16[2,256,1536]{2,1,0:T(8,128)(2,1)} %x_hbm.1, bf16[2,256,1536]{2,1,0:T(8,128)(2,1)} %ct_hbm.1, bf16[192,1536]{1,0:T(8,128)(2,1)} %bitcast.29, ...), custom_call_target="tpu_custom_call" | custom-call | tf_op jit(solution)/shard_map/train_step/pallas_call | solution.py:919
  262.2 9.6 %widen.1 = (f32[1536,512]{1,0:T(8,128)}, f32[1536,512]{1,0:T(8,128)}, f32[512,1536]{1,0:T(8,128)}, f32[192,1536]{1,0:T(8,128)}, f32[192,1536]{1,0:T(8,128)}, /*i...) custom-call(bf16[2,4,576,512]{3,2,1,0:T(8,128)(2,1)} %get-tuple-elem, ...), custom_call_target="tpu_custom_call" | custom-call | tf_op jit(solution)/shard_map/widen/pallas_call | solution.py:988

commit v8 on v7

--- a/solution.py
+++ b/solution.py
@@ -594,7 +594,7 @@
 
         @pl.when(step == 1)
         def _():
-            sum_5(1, 0)
+            sum_4(1, 0)
             sum_2(1, 1)
 
         def feed_back(half):
@@ -650,9 +650,9 @@
         lax.fori_loop(0, 4, unit_weights, 0)
         sum_1(layer, 0)
 
-        @pl.when((step == 1) & (sec == 1))
-        def _():
-            sum_6(0)
+        @pl.when(step == 1)
+        def _():
+            sum_5(1, 0)
 
 
         def hidden_grads(half):
@@ -668,7 +668,11 @@
             rs_sent(0, half)
 
         both(hidden_grads)
-        sum_2(layer, 0)
+
+        @pl.when(step == 0)
+        def _():
+            sum_2(1, 0)
+
 
         @pl.when(step == 1)
         def _():
@@ -720,6 +724,11 @@
 
         lax.fori_loop(0, d + 1, attend_back, 0)
 
+
+        @pl.when(step == 1)
+        def _():
+            sum_2(0, 0)
+
         def out_weights(n, c):
             cols = pl.ds(pl.multiple_of(n * 384, 384), 384)
             for h in range(2):
@@ -730,11 +739,20 @@
 
         lax.fori_loop(0, 4, out_weights, 0)
 
-        sum_3(layer, 0)
+
+        @pl.when(step == 0)
+        def _():
+            sum_3(1, 0)
+
 
         @pl.when(step == 1)
         def _():
             sum_4(1, 1)
+
+
+        @pl.when((step == 1) & (sec == 1))
+        def _():
+            sum_6(0)
 
         def dkv_sum(k, total):
             dkv_copy(d, k).wait_recv()
@@ -783,8 +801,16 @@
             return c
 
         lax.fori_loop(0, 4, qkv_weights, 0)
-        sum_1(layer, 1)
-        sum_4(layer, 0)
+
+        @pl.when(step == 1)
+        def _():
+            sum_3(0, 0)
+
+
+        @pl.when(step == 0)
+        def _():
+            sum_1(1, 1)
+
 
         @pl.when(step == 1)
         def _():
@@ -824,13 +850,8 @@
         device_id={"section": other}, device_id_type=MESH,
     )
     mate.start()
-    sum_5(0, 0)
-    sum_2(0, 1)
-
-    @pl.when(sec == 1)
-    def _():
-        sum_6(1)
-
+    sum_1(0, 1)
+    sum_4(0, 0)
     def gain_copy(axis, i, buf, me, to, sender):
         return pltpu.make_async_remote_copy(
             src_ref=buf.at[me], dst_ref=buf.at[sender], send_sem=ns.at[i, to], recv_sem=nr.at[i, sender],
@@ -863,13 +884,20 @@
     dg_t[t] = dgain[sec] + dg_peer[...]
     gain_send("tensor", 1, dg_t, t)
 
+    @pl.when(sec == 1)
+    def _():
+        sum_6(1)
+
+    sum_2(0, 1)
+    sum_5(0, 0)
+    dg_d[d] = gain_sum("tensor", 1, dg_t, t)
+    gain_send("dp", 2, dg_d, d)
+    sum_3(0, 1)
+
     @pl.when(sec == 0)
     def _():
         sum_6(0)
 
-    sum_3(0, 1)
-    dg_d[d] = gain_sum("tensor", 1, dg_t, t)
-    gain_send("dp", 2, dg_d, d)
     sum_4(0, 1)
     sum_5(0, 1)
 

time: 273 us -> 270 us (0.989)
  no operation moved by 1% of the time
where the time goes in v8:
time: 270 us
  Pallas kernels  270 us (100%)
    pallas_call x1, Pallas kernels, step_call(): pl.pallas_call(kernel, out_shape=(jax.ShapeDtypeStruct((2, OWN, D), BF16)...  260 us
    pallas_call x1, Pallas kernels, widened(): pl.pallas_call(widen, out_shape=tuple(shapes), in_specs=[hbm, hbm, vmem,...  9.62 us

profile of v8, /device:TPU:24, one launch (start us, length us, event | category | flops | bytes accessed | tf_op | source)
XLA Modules:
  0.0 270.2 jit_solution(10544513389461311635)
XLA Ops:
  0.6 259.9 %train_step.1 = (bf16[2,32,1536]{2,1,0:T(8,128)(2,1)}, f32[2,32,1536]{2,1,0:T(8,128)}, bf16[2,4,576,512]{3,2,1,0:T(8,128)(2,1)}, bf16[2,4,288,384]{3,2,1,0:T(8,128)(2,1)}, f32[8,1536]{1,0:T(8,128)}) custom-call(bf16[2,256,1536]{2,1,0:T(8,128)(2,1)} %x_hbm.1, bf16[2,256,1536]{2,1,0:T(8,128)(2,1)} %ct_hbm.1, bf16[192,1536]{1,0:T(8,128)(2,1)} %bitcast.29, ...), custom_call_target="tpu_custom_call" | custom-call | tf_op jit(solution)/shard_map/train_step/pallas_call | solution.py:947
  260.5 9.6 %widen.1 = (f32[1536,512]{1,0:T(8,128)}, f32[1536,512]{1,0:T(8,128)}, f32[512,1536]{1,0:T(8,128)}, f32[192,1536]{1,0:T(8,128)}, f32[192,1536]{1,0:T(8,128)}, /*i...) custom-call(bf16[2,4,576,512]{3,2,1,0:T(8,128)(2,1)} %get-tuple-elem, ...), custom_call_target="tpu_custom_call" | custom-call | tf_op jit(solution)/shard_map/widen/pallas_call | solution.py:1016
